TPU v7x, 32 devices: a whole 2x2x4 slice. The times are simulated.
32 devices in a mesh: grp: 2 (over x), tm: 16 (over z, y, core).
Axes of the slice: x: 2, y: 2, z: 4, core: 2. Of those that a mesh axis runs over, the one named last changes fastest.
Arguments:
- queries: bfloat16 [24576, 128], P(('grp', 'tm')), parts along dimension 0, may hold values from -6 to 6
- key_codes: bfloat16 [24576, 128], P(('grp', 'tm')), parts along dimension 0, may hold values from -6 to 6
- value_codes: bfloat16 [24576, 128], P(('grp', 'tm')), parts along dimension 0, may hold values from -6 to 6
- key_scales: float32 [192], P(('grp', 'tm')), parts along dimension 0, may hold values from 0.6 to 1.6
- value_scales: float32 [192], P(('grp', 'tm')), parts along dimension 0, may hold values from 0.3 to 3
- scale_slot: int32 [32, 6], P(('grp', 'tm')), parts along dimension 0, may hold values from 0 to 5, each once within a row
- grad_out: bfloat16 [24576, 128], P(('grp', 'tm')), parts along dimension 0, may hold values from -384 to 384
Outputs:
- query_grad: bfloat16 [24576, 128], P(('grp', 'tm')), parts along dimension 0
- key_grad: bfloat16 [24576, 128], P(('grp', 'tm')), parts along dimension 0
- value_grad: bfloat16 [24576, 128], P(('grp', 'tm')), parts along dimension 0
There are 2 independent parts, one for each index of `grp`. A program takes and returns all parts, laid end to end along the dimension named above; each array names one. Nothing has to cross between parts.
Inputs may be any that keep to these rules, and one draw needn't show every extreme that they name: Row s of scale_slot names every number 0 to 5 once.
All inputs are finite; a program needn't handle non-finite values.
Results may differ from a plain program's by a relative error of at most 0.0019.
The roundings to bfloat16 on the way count: a program that leaves them out, or rounds other values in their place, can miss the bound.
Values may be sent and summed in bfloat16 or wider, within the bound.
No kernel may reach another device: no remote copies, remote signals or barrier semaphores. Data moves between devices by JAX's collectives and lax.ppermute only.
A program may use at most 64 MiB of HBM per device.

v0:
```python
import jax
import jax.numpy as jnp
from jax import lax
from jax.sharding import PartitionSpec as P

HEAD_DIM = 128
TILE_TOKENS = 256
ROW_TILES = 4


big_negative = -1e30
offsets_list = [(frame_step, row_step) for frame_step in (-1, 0, 1) for row_step in (-1, 0, 1)]


def shifted(value, axis, steps):
    count = lax.axis_size(axis)
    first, last = (max(0, -steps), min(count, count - steps))
    return lax.ppermute(value, axis, [(source, source + steps) for source in range(first, last)])


def dequantize(code_block, scale_part, slot_row):
    blocks_dev = scale_part.shape[0]
    picker = slot_row[:, None] == jnp.arange(blocks_dev, dtype=jnp.int32)[None, :]
    picked = jnp.sum(jnp.where(picker, scale_part[None, :], 0.0), axis=1)
    tokens_dev, head_dim = code_block.shape
    blocked = code_block.astype(jnp.float32).reshape(blocks_dev, tokens_dev // blocks_dev, head_dim)
    return (blocked * picked[:, None, None]).astype(jnp.bfloat16).reshape(tokens_dev, head_dim)


def fetch_direct(key_value, row_tiles):
    gathered = []
    for frame_step, row_step in offsets_list:
        if frame_step == 0 and row_step == 0:
            gathered.append(key_value)
        else:
            gathered.append(shifted(key_value, "tm", -(frame_step * row_tiles + row_step)))
    return jnp.stack(gathered)


def return_direct(partials, row_tiles):
    summed = partials[4].astype(jnp.float32)
    for position, (frame_step, row_step) in enumerate(offsets_list):
        if position != 4:
            arrived = shifted(partials[position], "tm", frame_step * row_tiles + row_step)
            summed = summed + arrived.astype(jnp.float32)
    return summed


def per_device(queries, key_codes, value_codes, key_scales, value_scales, scale_slot, grad_out):
    slot_row = scale_slot[0]
    keys_own = dequantize(key_codes, key_scales, slot_row)
    values_own = dequantize(value_codes, value_scales, slot_row)
    key_value = jnp.stack([keys_own, values_own])
    gathered = fetch_direct(key_value, ROW_TILES)
    keys_all = gathered[:, 0]
    values_all = gathered[:, 1]
    device_index = lax.axis_index("tm")
    frame_tiles = lax.axis_size("tm") // ROW_TILES
    frame_idx = device_index // ROW_TILES
    row_idx = device_index % ROW_TILES
    slab_valid = jnp.stack(
        [
            (frame_idx + frame_step >= 0)
            & (frame_idx + frame_step < frame_tiles)
            & (row_idx + row_step >= 0)
            & (row_idx + row_step < ROW_TILES)
            for frame_step, row_step in offsets_list
        ]
    )
    tokens_dev = queries.shape[0]
    tile_of = jnp.arange(tokens_dev, dtype=jnp.int32) // TILE_TOKENS
    near_cols = jnp.abs(tile_of[:, None] - tile_of[None, :]) <= 1
    inverse = HEAD_DIM ** (-0.5)

    def first_pass(running, inputs):
        row_top, row_total, weighted = running
        key_block, value_block, slab_ok = inputs
        allowed = near_cols & slab_ok
        scores = (
            jnp.einsum("qd,kd->qk", queries, key_block, preferred_element_type=jnp.float32)
            * inverse
        )
        scores = jnp.where(allowed, scores, big_negative)
        new_top = jnp.maximum(row_top, jnp.max(scores, axis=1))
        unscaled = jnp.where(allowed, jnp.exp(scores - new_top[:, None]), 0.0)
        grad_prob = jnp.einsum(
            "qd,kd->qk", grad_out, value_block, preferred_element_type=jnp.float32
        )
        rescale = jnp.exp(row_top - new_top)
        row_total = row_total * rescale + jnp.sum(unscaled, axis=1)
        weighted = weighted * rescale + jnp.sum(unscaled * grad_prob, axis=1)
        return ((new_top, row_total, weighted), None)

    start_state = (
        jnp.full((tokens_dev,), big_negative, jnp.float32),
        jnp.zeros((tokens_dev,), jnp.float32),
        jnp.zeros((tokens_dev,), jnp.float32),
    )
    (row_top, row_total, weighted), unused = lax.scan(
        first_pass, start_state, (keys_all, values_all, slab_valid)
    )
    log_total = row_top + jnp.log(row_total)
    row_delta = weighted / row_total

    def second_pass(query_sum, inputs):
        key_block, value_block, slab_ok = inputs
        allowed = near_cols & slab_ok
        scores = (
            jnp.einsum("qd,kd->qk", queries, key_block, preferred_element_type=jnp.float32)
            * inverse
        )
        attn_prob = jnp.where(
            allowed, jnp.exp(jnp.where(allowed, scores, big_negative) - log_total[:, None]), 0.0
        )
        grad_prob = jnp.einsum(
            "qd,kd->qk", grad_out, value_block, preferred_element_type=jnp.float32
        )
        dscore = (attn_prob * (grad_prob - row_delta[:, None])).astype(jnp.bfloat16)
        query_sum = query_sum + jnp.dot(dscore, key_block, preferred_element_type=jnp.float32)
        key_part = (
            jnp.einsum("qk,qd->kd", dscore, queries, preferred_element_type=jnp.float32) * inverse
        )
        value_part = jnp.einsum(
            "qk,qd->kd",
            attn_prob.astype(jnp.bfloat16),
            grad_out,
            preferred_element_type=jnp.float32,
        )
        return (query_sum, jnp.stack([key_part, value_part]).astype(jnp.bfloat16))

    query_sum, partials = lax.scan(
        second_pass, jnp.zeros(queries.shape, jnp.float32), (keys_all, values_all, slab_valid)
    )
    query_grad = (query_sum * inverse).astype(jnp.bfloat16)
    summed = return_direct(partials, ROW_TILES)
    return (query_grad, summed[0].astype(jnp.bfloat16), summed[1].astype(jnp.bfloat16))


def solution(mesh):
    in_specs = (
        P(("grp", "tm"), None),
        P(("grp", "tm"), None),
        P(("grp", "tm"), None),
        P(("grp", "tm")),
        P(("grp", "tm")),
        P(("grp", "tm"), None),
        P(("grp", "tm"), None),
    )
    out_specs = (P(("grp", "tm"), None), P(("grp", "tm"), None), P(("grp", "tm"), None))
    return jax.shard_map(
        per_device, mesh=mesh, in_specs=in_specs, out_specs=out_specs, check_vma=False
    )
```

profile of v0, /device:TPU:20, one launch (start us, length us, event | category | flops | bytes accessed | tf_op | source)
XLA Modules:
  0.0 236.6 jit_solution(1460597930772862526)
XLA Ops:
  3.9 2.9 %collective-permute-start = (bf16[2,768,128]{2,1,0:T(8,128)(2,1)S(1)}, bf16[2,768,128]{2,1,0:T(8,128)(2,1)S(1)}, u32[]{:S(2)}, u32[]{:S(2)}) collective-permute-start(bf16[2,768,128]{2,1,0:T(8,128)(2,1)S(1)} %pad_maximum_fusion), channel_id=1, source_target_pairs={{0,5},{1,6},{2,7},{3,8},{4,9},{5,10},{6,11},{7,12},{8,13},{9,14},{... | collective-permute-start | bytes 1179656 | tf_op jit(solution)/shard_map/ppermute | solution.py:18
  8.7 3.9 %collective-permute-start.6 = (bf16[2,768,128]{2,1,0:T(8,128)(2,1)S(1)}, bf16[2,768,128]{2,1,0:T(8,128)(2,1)S(1)}, u32[]{:S(2)}, u32[]{:S(2)}) collective-permute-start(bf16[2,768,128]{2,1,0:T(8,128)(2,1)S(1)} %pad_maximum_fusion), channel_id=1, source_target_pairs={{4,0},{5,1},{6,2},{7,3},{8,4},{9,5},{10,6},{11,7},{12,8},{13,9},{1... | collective-permute-start | bytes 1179656 | tf_op jit(solution)/shard_map/ppermute | solution.py:18
  12.6 3.1 %collective-permute-start.5 = (bf16[2,768,128]{2,1,0:T(8,128)(2,1)S(1)}, bf16[2,768,128]{2,1,0:T(8,128)(2,1)S(1)}, u32[]{:S(2)}, u32[]{:S(2)}) collective-permute-start(bf16[2,768,128]{2,1,0:T(8,128)(2,1)S(1)} %pad_maximum_fusion), channel_id=1, source_target_pairs={{3,0},{4,1},{5,2},{6,3},{7,4},{8,5},{9,6},{10,7},{11,8},{12,9},{13... | collective-permute-start | bytes 1179656 | tf_op jit(solution)/shard_map/ppermute | solution.py:18
  18.4 3.0 %collective-permute-start.2 = (bf16[2,768,128]{2,1,0:T(8,128)(2,1)S(1)}, bf16[2,768,128]{2,1,0:T(8,128)(2,1)S(1)}, u32[]{:S(2)}, u32[]{:S(2)}) collective-permute-start(bf16[2,768,128]{2,1,0:T(8,128)(2,1)S(1)} %pad_maximum_fusion), channel_id=1, source_target_pairs={{0,3},{1,4},{2,5},{3,6},{4,7},{5,8},{6,9},{7,10},{8,11},{9,12},{10... | collective-permute-start | bytes 1179656 | tf_op jit(solution)/shard_map/ppermute | solution.py:18
  21.5 7.4 %collective-permute-done.1 = bf16[2,768,128]{2,1,0:T(8,128)(2,1)S(1)} collective-permute-done((bf16[2,768,128]{2,1,0:T(8,128)(2,1)S(1)}, bf16[2,768,128]{2,1,0:T(8,128)(2,1)S(1)}, u32[]{:S(2)}, u32[]{:S(2)}) %collective-permute-start.1) | collective-permute-done | bytes 393248 | tf_op jit(solution)/shard_map/ppermute | solution.py:18
  28.9 3.9 %collective-permute-start.3 = (bf16[2,768,128]{2,1,0:T(8,128)(2,1)S(1)}, bf16[2,768,128]{2,1,0:T(8,128)(2,1)S(1)}, u32[]{:S(2)}, u32[]{:S(2)}) collective-permute-start(bf16[2,768,128]{2,1,0:T(8,128)(2,1)S(1)} %pad_maximum_fusion), channel_id=1, source_target_pairs={{0,1},{1,2},{2,3},{3,4},{4,5},{5,6},{6,7},{7,8},{8,9},{9,10},{10,1... | collective-permute-start | bytes 1179656 | tf_op jit(solution)/shard_map/ppermute | solution.py:18
  32.8 5.4 %collective-permute-done.2 = bf16[2,768,128]{2,1,0:T(8,128)(2,1)S(1)} collective-permute-done((bf16[2,768,128]{2,1,0:T(8,128)(2,1)S(1)}, bf16[2,768,128]{2,1,0:T(8,128)(2,1)S(1)}, u32[]{:S(2)}, u32[]{:S(2)}) %collective-permute-start.2) | collective-permute-done | bytes 393248 | tf_op jit(solution)/shard_map/ppermute | solution.py:18
  41.6 9.9 %collective-permute-done.7 = bf16[2,768,128]{2,1,0:T(8,128)(2,1)S(1)} collective-permute-done((bf16[2,768,128]{2,1,0:T(8,128)(2,1)S(1)}, bf16[2,768,128]{2,1,0:T(8,128)(2,1)S(1)}, u32[]{:S(2)}, u32[]{:S(2)}) %collective-permute-start.7) | collective-permute-done | bytes 393248 | tf_op jit(solution)/shard_map/ppermute | solution.py:18
  53.1 63.8 %while.28 = (s32[]{:T(128)}, f32[768]{0:T(1024)S(1)}, f32[768]{0:T(1024)S(1)}, f32[768]{0:T(1024)S(1)}, pred[9]{0:T(512)(128)(4,1)S(1)}, /*index=5*/bf16[9,768,1...) while((s32[]{:T(128)}, f32[768]{0:T(1024)S(1)}, ...), condition=%wide.region_6.7_spmd.clone, body=%wide.region_2.6_spmd.clone.sunk | while | flops 317330688 | bytes 7940760 | solution.py:99
  53.7 2.6 %fusion.87 = (f32[768]{0:T(1024)S(1)}, f32[768,768]{1,0:T(8,128)S(1)}) fusion(pred[]{:T(512)} %bitcast.166, s32[768]{0:T(1024)S(1)} %get-tuple-element.428, bf16[768,128]{1,0:T(8,128)(2,1)S(1)} %get-tuple-element.425, bf16[9,768,128]{2,1,0:T(8,128)(2,1)} %get-tuple-element.424, s32[]{:T(128)S(6)} %copy.39), kind=kOutput, calls=%fused_computation.8.clone.1 | convolution fusion | flops 155122944 | bytes 2764292 | tf_op jit(solution)/shard_map/while/body/eval_jaxpr/qd,kd->qk/dot_general | solution.py:80
  60.8 2.5 %fusion.87 = (f32[768]{0:T(1024)S(1)}, f32[768,768]{1,0:T(8,128)S(1)}) fusion(pred[]{:T(512)} %bitcast.166, s32[768]{0:T(1024)S(1)} %get-tuple-element.428, bf16[768,128]{1,0:T(8,128)(2,1)S(1)} %get-tuple-element.425, bf16[9,768,128]{2,1,0:T(8,128)(2,1)} %get-tuple-element.424, s32[]{:T(128)S(6)} %copy.39), kind=kOutput, calls=%fused_computation.8.clone.1 | convolution fusion | flops 155122944 | bytes 2764292 | tf_op jit(solution)/shard_map/while/body/eval_jaxpr/qd,kd->qk/dot_general | solution.py:80
  67.9 2.5 %fusion.87 = (f32[768]{0:T(1024)S(1)}, f32[768,768]{1,0:T(8,128)S(1)}) fusion(pred[]{:T(512)} %bitcast.166, s32[768]{0:T(1024)S(1)} %get-tuple-element.428, bf16[768,128]{1,0:T(8,128)(2,1)S(1)} %get-tuple-element.425, bf16[9,768,128]{2,1,0:T(8,128)(2,1)} %get-tuple-element.424, s32[]{:T(128)S(6)} %copy.39), kind=kOutput, calls=%fused_computation.8.clone.1 | convolution fusion | flops 155122944 | bytes 2764292 | tf_op jit(solution)/shard_map/while/body/eval_jaxpr/qd,kd->qk/dot_general | solution.py:80
  75.0 2.5 %fusion.87 = (f32[768]{0:T(1024)S(1)}, f32[768,768]{1,0:T(8,128)S(1)}) fusion(pred[]{:T(512)} %bitcast.166, s32[768]{0:T(1024)S(1)} %get-tuple-element.428, bf16[768,128]{1,0:T(8,128)(2,1)S(1)} %get-tuple-element.425, bf16[9,768,128]{2,1,0:T(8,128)(2,1)} %get-tuple-element.424, s32[]{:T(128)S(6)} %copy.39), kind=kOutput, calls=%fused_computation.8.clone.1 | convolution fusion | flops 155122944 | bytes 2764292 | tf_op jit(solution)/shard_map/while/body/eval_jaxpr/qd,kd->qk/dot_general | solution.py:80
  82.1 2.5 %fusion.87 = (f32[768]{0:T(1024)S(1)}, f32[768,768]{1,0:T(8,128)S(1)}) fusion(pred[]{:T(512)} %bitcast.166, s32[768]{0:T(1024)S(1)} %get-tuple-element.428, bf16[768,128]{1,0:T(8,128)(2,1)S(1)} %get-tuple-element.425, bf16[9,768,128]{2,1,0:T(8,128)(2,1)} %get-tuple-element.424, s32[]{:T(128)S(6)} %copy.39), kind=kOutput, calls=%fused_computation.8.clone.1 | convolution fusion | flops 155122944 | bytes 2764292 | tf_op jit(solution)/shard_map/while/body/eval_jaxpr/qd,kd->qk/dot_general | solution.py:80
  103.3 2.5 %fusion.87 = (f32[768]{0:T(1024)S(1)}, f32[768,768]{1,0:T(8,128)S(1)}) fusion(pred[]{:T(512)} %bitcast.166, s32[768]{0:T(1024)S(1)} %get-tuple-element.428, bf16[768,128]{1,0:T(8,128)(2,1)S(1)} %get-tuple-element.425, bf16[9,768,128]{2,1,0:T(8,128)(2,1)} %get-tuple-element.424, s32[]{:T(128)S(6)} %copy.39), kind=kOutput, calls=%fused_computation.8.clone.1 | convolution fusion | flops 155122944 | bytes 2764292 | tf_op jit(solution)/shard_map/while/body/eval_jaxpr/qd,kd->qk/dot_general | solution.py:80
  116.9 64.4 %while.29 = (s32[]{:T(128)}, f32[768,128]{1,0:T(8,128)S(1)}, bf16[9,2,768,128]{3,2,1,0:T(8,128)(2,1)}, pred[9]{0:T(512)(128)(4,1)S(1)}, bf16[9,768,128]{2,1,0:T(...) while((s32[]{:T(128)}, f32[768,128]{1,0:T(8,128)S(1)}, ...), condition=%wide.region_8.9_spmd.clone, body=%wide.region_7.8_spmd.clone.sunk | while | flops 763330560 | bytes 13976229 | solution.py:131
  117.5 2.8 %fusion.101 = f32[768,768]{0,1:T(8,128)S(1)} fusion(bf16[768,128]{1,0:T(8,128)(2,1)S(1)} %get-tuple-element.462, s32[768]{0:T(1024)S(1)} %get-tuple-element.467, f32[768]{0:T(1024)S(1)} %get-tuple-element.463, pred[]{:T(512)} %bitcast.180, bf16[9,768,128]{2,1,0:T(8,128)(2,1)} %get-tuple-element.461, s32[]{:T(128)S(6)} %copy.50), kind=kOutput, calls=%fused_computation.28.clone.1 | convolution fusion | flops 155713536 | bytes 2765316 | tf_op jit(solution)/shard_map/while/body/eval_jaxpr/qd,kd->qk/dot_general | solution.py:109
  124.7 2.8 %fusion.101 = f32[768,768]{0,1:T(8,128)S(1)} fusion(bf16[768,128]{1,0:T(8,128)(2,1)S(1)} %get-tuple-element.462, s32[768]{0:T(1024)S(1)} %get-tuple-element.467, f32[768]{0:T(1024)S(1)} %get-tuple-element.463, pred[]{:T(512)} %bitcast.180, bf16[9,768,128]{2,1,0:T(8,128)(2,1)} %get-tuple-element.461, s32[]{:T(128)S(6)} %copy.50), kind=kOutput, calls=%fused_computation.28.clone.1 | convolution fusion | flops 155713536 | bytes 2765316 | tf_op jit(solution)/shard_map/while/body/eval_jaxpr/qd,kd->qk/dot_general | solution.py:109
  131.8 2.8 %fusion.101 = f32[768,768]{0,1:T(8,128)S(1)} fusion(bf16[768,128]{1,0:T(8,128)(2,1)S(1)} %get-tuple-element.462, s32[768]{0:T(1024)S(1)} %get-tuple-element.467, f32[768]{0:T(1024)S(1)} %get-tuple-element.463, pred[]{:T(512)} %bitcast.180, bf16[9,768,128]{2,1,0:T(8,128)(2,1)} %get-tuple-element.461, s32[]{:T(128)S(6)} %copy.50), kind=kOutput, calls=%fused_computation.28.clone.1 | convolution fusion | flops 155713536 | bytes 2765316 | tf_op jit(solution)/shard_map/while/body/eval_jaxpr/qd,kd->qk/dot_general | solution.py:109
  139.0 2.8 %fusion.101 = f32[768,768]{0,1:T(8,128)S(1)} fusion(bf16[768,128]{1,0:T(8,128)(2,1)S(1)} %get-tuple-element.462, s32[768]{0:T(1024)S(1)} %get-tuple-element.467, f32[768]{0:T(1024)S(1)} %get-tuple-element.463, pred[]{:T(512)} %bitcast.180, bf16[9,768,128]{2,1,0:T(8,128)(2,1)} %get-tuple-element.461, s32[]{:T(128)S(6)} %copy.50), kind=kOutput, calls=%fused_computation.28.clone.1 | convolution fusion | flops 155713536 | bytes 2765316 | tf_op jit(solution)/shard_map/while/body/eval_jaxpr/qd,kd->qk/dot_general | solution.py:109
  146.2 2.8 %fusion.101 = f32[768,768]{0,1:T(8,128)S(1)} fusion(bf16[768,128]{1,0:T(8,128)(2,1)S(1)} %get-tuple-element.462, s32[768]{0:T(1024)S(1)} %get-tuple-element.467, f32[768]{0:T(1024)S(1)} %get-tuple-element.463, pred[]{:T(512)} %bitcast.180, bf16[9,768,128]{2,1,0:T(8,128)(2,1)} %get-tuple-element.461, s32[]{:T(128)S(6)} %copy.50), kind=kOutput, calls=%fused_computation.28.clone.1 | convolution fusion | flops 155713536 | bytes 2765316 | tf_op jit(solution)/shard_map/while/body/eval_jaxpr/qd,kd->qk/dot_general | solution.py:109
  153.3 2.8 %fusion.101 = f32[768,768]{0,1:T(8,128)S(1)} fusion(bf16[768,128]{1,0:T(8,128)(2,1)S(1)} %get-tuple-element.462, s32[768]{0:T(1024)S(1)} %get-tuple-element.467, f32[768]{0:T(1024)S(1)} %get-tuple-element.463, pred[]{:T(512)} %bitcast.180, bf16[9,768,128]{2,1,0:T(8,128)(2,1)} %get-tuple-element.461, s32[]{:T(128)S(6)} %copy.50), kind=kOutput, calls=%fused_computation.28.clone.1 | convolution fusion | flops 155713536 | bytes 2765316 | tf_op jit(solution)/shard_map/while/body/eval_jaxpr/qd,kd->qk/dot_general | solution.py:109
  160.4 2.8 %fusion.101 = f32[768,768]{0,1:T(8,128)S(1)} fusion(bf16[768,128]{1,0:T(8,128)(2,1)S(1)} %get-tuple-element.462, s32[768]{0:T(1024)S(1)} %get-tuple-element.467, f32[768]{0:T(1024)S(1)} %get-tuple-element.463, pred[]{:T(512)} %bitcast.180, bf16[9,768,128]{2,1,0:T(8,128)(2,1)} %get-tuple-element.461, s32[]{:T(128)S(6)} %copy.50), kind=kOutput, calls=%fused_computation.28.clone.1 | convolution fusion | flops 155713536 | bytes 2765316 | tf_op jit(solution)/shard_map/while/body/eval_jaxpr/qd,kd->qk/dot_general | solution.py:109
  167.6 2.8 %fusion.101 = f32[768,768]{0,1:T(8,128)S(1)} fusion(bf16[768,128]{1,0:T(8,128)(2,1)S(1)} %get-tuple-element.462, s32[768]{0:T(1024)S(1)} %get-tuple-element.467, f32[768]{0:T(1024)S(1)} %get-tuple-element.463, pred[]{:T(512)} %bitcast.180, bf16[9,768,128]{2,1,0:T(8,128)(2,1)} %get-tuple-element.461, s32[]{:T(128)S(6)} %copy.50), kind=kOutput, calls=%fused_computation.28.clone.1 | convolution fusion | flops 155713536 | bytes 2765316 | tf_op jit(solution)/shard_map/while/body/eval_jaxpr/qd,kd->qk/dot_general | solution.py:109
  174.8 2.8 %fusion.101 = f32[768,768]{0,1:T(8,128)S(1)} fusion(bf16[768,128]{1,0:T(8,128)(2,1)S(1)} %get-tuple-element.462, s32[768]{0:T(1024)S(1)} %get-tuple-element.467, f32[768]{0:T(1024)S(1)} %get-tuple-element.463, pred[]{:T(512)} %bitcast.180, bf16[9,768,128]{2,1,0:T(8,128)(2,1)} %get-tuple-element.461, s32[]{:T(128)S(6)} %copy.50), kind=kOutput, calls=%fused_computation.28.clone.1 | convolution fusion | flops 155713536 | bytes 2765316 | tf_op jit(solution)/shard_map/while/body/eval_jaxpr/qd,kd->qk/dot_general | solution.py:109
  185.5 4.9 %collective-permute-start.13 = (bf16[2,768,128]{2,1,0:T(8,128)(2,1)S(1)}, bf16[2,768,128]{2,1,0:T(8,128)(2,1)S(1)}, u32[]{:S(2)}, u32[]{:S(2)}) collective-permute-start(bf16[2,768,128]{2,1,0:T(8,128)(2,1)S(1)} %get-tuple-element.244), channel_id=1, source_target_pairs={{0,3},{1,4},{2,5},{3,6},{4,7},{5,8},{6,9},{7,10},{8,11},{9,12},{10... | collective-permute-start | bytes 1179656 | tf_op jit(solution)/shard_map/ppermute | solution.py:18
  192.9 3.1 %collective-permute-start.11 = (bf16[2,768,128]{2,1,0:T(8,128)(2,1)S(1)}, bf16[2,768,128]{2,1,0:T(8,128)(2,1)S(1)}, u32[]{:S(2)}, u32[]{:S(2)}) collective-permute-start(bf16[2,768,128]{2,1,0:T(8,128)(2,1)S(1)} %get-tuple-element.246), channel_id=1, source_target_pairs={{1,0},{2,1},{3,2},{4,3},{5,4},{6,5},{7,6},{8,7},{9,8},{10,9},{11,1... | collective-permute-start | bytes 1179656 | tf_op jit(solution)/shard_map/ppermute | solution.py:18
  196.0 3.8 %collective-permute-start.10 = (bf16[2,768,128]{2,1,0:T(8,128)(2,1)S(1)}, bf16[2,768,128]{2,1,0:T(8,128)(2,1)S(1)}, u32[]{:S(2)}, u32[]{:S(2)}) collective-permute-start(bf16[2,768,128]{2,1,0:T(8,128)(2,1)S(1)} %get-tuple-element.247), channel_id=1, source_target_pairs={{3,0},{4,1},{5,2},{6,3},{7,4},{8,5},{9,6},{10,7},{11,8},{12,9},{13... | collective-permute-start | bytes 1179656 | tf_op jit(solution)/shard_map/ppermute | solution.py:18
  199.9 2.8 %collective-permute-start.9 = (bf16[2,768,128]{2,1,0:T(8,128)(2,1)S(1)}, bf16[2,768,128]{2,1,0:T(8,128)(2,1)S(1)}, u32[]{:S(2)}, u32[]{:S(2)}) collective-permute-start(bf16[2,768,128]{2,1,0:T(8,128)(2,1)S(1)} %get-tuple-element.248), channel_id=1, source_target_pairs={{4,0},{5,1},{6,2},{7,3},{8,4},{9,5},{10,6},{11,7},{12,8},{13,9},{1... | collective-permute-start | bytes 1179656 | tf_op jit(solution)/shard_map/ppermute | solution.py:18
  202.7 3.9 %collective-permute-start.15 = (bf16[2,768,128]{2,1,0:T(8,128)(2,1)S(1)}, bf16[2,768,128]{2,1,0:T(8,128)(2,1)S(1)}, u32[]{:S(2)}, u32[]{:S(2)}) collective-permute-start(bf16[2,768,128]{2,1,0:T(8,128)(2,1)S(1)} %get-tuple-element.249), channel_id=1, source_target_pairs={{0,5},{1,6},{2,7},{3,8},{4,9},{5,10},{6,11},{7,12},{8,13},{9,14},{... | collective-permute-start | bytes 1179656 | tf_op jit(solution)/shard_map/ppermute | solution.py:18
  206.6 8.4 %collective-permute-done.12 = bf16[2,768,128]{2,1,0:T(8,128)(2,1)S(1)} collective-permute-done((bf16[2,768,128]{2,1,0:T(8,128)(2,1)S(1)}, bf16[2,768,128]{2,1,0:T(8,128)(2,1)S(1)}, u32[]{:S(2)}, u32[]{:S(2)}) %collective-permute-start.12) | collective-permute-done | bytes 393248 | tf_op jit(solution)/shard_map/ppermute | solution.py:18
  217.7 16.7 %collective-permute-done.14 = bf16[2,768,128]{2,1,0:T(8,128)(2,1)S(1)} collective-permute-done((bf16[2,768,128]{2,1,0:T(8,128)(2,1)S(1)}, bf16[2,768,128]{2,1,0:T(8,128)(2,1)S(1)}, u32[]{:S(2)}, u32[]{:S(2)}) %collective-permute-start.14) | collective-permute-done | bytes 393248 | tf_op jit(solution)/shard_map/ppermute | solution.py:18
  (159 shorter events, 111.0 us)
Async XLA Ops:
  3.9 14.5 %collective-permute-start = (bf16[2,768,128]{2,1,0:T(8,128)(2,1)S(1)}, bf16[2,768,128]{2,1,0:T(8,128)(2,1)S(1)}, u32[]{:S(2)}, u32[]{:S(2)}) collective-permute-start(bf16[2,768,128]{2,1,0:T(8,128)(2,1)S(1)} %pad_maximum_fusion), channel_id=1, source_target_pairs={{0,5},{1,6},{2,7},{3,8},{4,9},{5,10},{6,11},{7,12},{8,13},{9,14},{... | collective-permute-start | bytes 1179656 | tf_op jit(solution)/shard_map/ppermute | solution.py:18
  6.8 22.1 %collective-permute-start.1 = (bf16[2,768,128]{2,1,0:T(8,128)(2,1)S(1)}, bf16[2,768,128]{2,1,0:T(8,128)(2,1)S(1)}, u32[]{:S(2)}, u32[]{:S(2)}) collective-permute-start(bf16[2,768,128]{2,1,0:T(8,128)(2,1)S(1)} %pad_maximum_fusion), channel_id=1, source_target_pairs={{0,4},{1,5},{2,6},{3,7},{4,8},{5,9},{6,10},{7,11},{8,12},{9,13},{1... | collective-permute-start | bytes 1179656 | tf_op jit(solution)/shard_map/ppermute | solution.py:18
  8.7 32.8 %collective-permute-start.6 = (bf16[2,768,128]{2,1,0:T(8,128)(2,1)S(1)}, bf16[2,768,128]{2,1,0:T(8,128)(2,1)S(1)}, u32[]{:S(2)}, u32[]{:S(2)}) collective-permute-start(bf16[2,768,128]{2,1,0:T(8,128)(2,1)S(1)} %pad_maximum_fusion), channel_id=1, source_target_pairs={{4,0},{5,1},{6,2},{7,3},{8,4},{9,5},{10,6},{11,7},{12,8},{13,9},{1... | collective-permute-start | bytes 1179656 | tf_op jit(solution)/shard_map/ppermute | solution.py:18
  12.6 28.8 %collective-permute-start.5 = (bf16[2,768,128]{2,1,0:T(8,128)(2,1)S(1)}, bf16[2,768,128]{2,1,0:T(8,128)(2,1)S(1)}, u32[]{:S(2)}, u32[]{:S(2)}) collective-permute-start(bf16[2,768,128]{2,1,0:T(8,128)(2,1)S(1)} %pad_maximum_fusion), channel_id=1, source_target_pairs={{3,0},{4,1},{5,2},{6,3},{7,4},{8,5},{9,6},{10,7},{11,8},{12,9},{13... | collective-permute-start | bytes 1179656 | tf_op jit(solution)/shard_map/ppermute | solution.py:18
  15.7 25.7 %collective-permute-start.4 = (bf16[2,768,128]{2,1,0:T(8,128)(2,1)S(1)}, bf16[2,768,128]{2,1,0:T(8,128)(2,1)S(1)}, u32[]{:S(2)}, u32[]{:S(2)}) collective-permute-start(bf16[2,768,128]{2,1,0:T(8,128)(2,1)S(1)} %pad_maximum_fusion), channel_id=1, source_target_pairs={{1,0},{2,1},{3,2},{4,3},{5,4},{6,5},{7,6},{8,7},{9,8},{10,9},{11,1... | collective-permute-start | bytes 1179656 | tf_op jit(solution)/shard_map/ppermute | solution.py:18
  18.4 19.8 %collective-permute-start.2 = (bf16[2,768,128]{2,1,0:T(8,128)(2,1)S(1)}, bf16[2,768,128]{2,1,0:T(8,128)(2,1)S(1)}, u32[]{:S(2)}, u32[]{:S(2)}) collective-permute-start(bf16[2,768,128]{2,1,0:T(8,128)(2,1)S(1)} %pad_maximum_fusion), channel_id=1, source_target_pairs={{0,3},{1,4},{2,5},{3,6},{4,7},{5,8},{6,9},{7,10},{8,11},{9,12},{10... | collective-permute-start | bytes 1179656 | tf_op jit(solution)/shard_map/ppermute | solution.py:18
  28.9 12.4 %collective-permute-start.3 = (bf16[2,768,128]{2,1,0:T(8,128)(2,1)S(1)}, bf16[2,768,128]{2,1,0:T(8,128)(2,1)S(1)}, u32[]{:S(2)}, u32[]{:S(2)}) collective-permute-start(bf16[2,768,128]{2,1,0:T(8,128)(2,1)S(1)} %pad_maximum_fusion), channel_id=1, source_target_pairs={{0,1},{1,2},{2,3},{3,4},{4,5},{5,6},{6,7},{7,8},{8,9},{9,10},{10,1... | collective-permute-start | bytes 1179656 | tf_op jit(solution)/shard_map/ppermute | solution.py:18
  38.2 13.3 %collective-permute-start.7 = (bf16[2,768,128]{2,1,0:T(8,128)(2,1)S(1)}, bf16[2,768,128]{2,1,0:T(8,128)(2,1)S(1)}, u32[]{:S(2)}, u32[]{:S(2)}) collective-permute-start(bf16[2,768,128]{2,1,0:T(8,128)(2,1)S(1)} %pad_maximum_fusion), channel_id=1, source_target_pairs={{5,0},{6,1},{7,2},{8,3},{9,4},{10,5},{11,6},{12,7},{13,8},{14,9},{... | collective-permute-start | bytes 1179656 | tf_op jit(solution)/shard_map/ppermute | solution.py:18
  51.6 1.5 copy-start
  51.6 1.5 copy-start.1
  183.4 16.4 %collective-permute-start.8 = (bf16[2,768,128]{2,1,0:T(8,128)(2,1)S(1)}, bf16[2,768,128]{2,1,0:T(8,128)(2,1)S(1)}, u32[]{:S(2)}, u32[]{:S(2)}) collective-permute-start(bf16[2,768,128]{2,1,0:T(8,128)(2,1)S(1)} %get-tuple-element.243), channel_id=1, source_target_pairs={{5,0},{6,1},{7,2},{8,3},{9,4},{10,5},{11,6},{12,7},{13,8},{14,9},{... | collective-permute-start | bytes 1179656 | tf_op jit(solution)/shard_map/ppermute | solution.py:18
  185.5 17.2 %collective-permute-start.13 = (bf16[2,768,128]{2,1,0:T(8,128)(2,1)S(1)}, bf16[2,768,128]{2,1,0:T(8,128)(2,1)S(1)}, u32[]{:S(2)}, u32[]{:S(2)}) collective-permute-start(bf16[2,768,128]{2,1,0:T(8,128)(2,1)S(1)} %get-tuple-element.244), channel_id=1, source_target_pairs={{0,3},{1,4},{2,5},{3,6},{4,7},{5,8},{6,9},{7,10},{8,11},{9,12},{10... | collective-permute-start | bytes 1179656 | tf_op jit(solution)/shard_map/ppermute | solution.py:18
  190.5 24.6 %collective-permute-start.12 = (bf16[2,768,128]{2,1,0:T(8,128)(2,1)S(1)}, bf16[2,768,128]{2,1,0:T(8,128)(2,1)S(1)}, u32[]{:S(2)}, u32[]{:S(2)}) collective-permute-start(bf16[2,768,128]{2,1,0:T(8,128)(2,1)S(1)} %get-tuple-element.245), channel_id=1, source_target_pairs={{0,1},{1,2},{2,3},{3,4},{4,5},{5,6},{6,7},{7,8},{8,9},{9,10},{10,1... | collective-permute-start | bytes 1179656 | tf_op jit(solution)/shard_map/ppermute | solution.py:18
  192.9 24.8 %collective-permute-start.11 = (bf16[2,768,128]{2,1,0:T(8,128)(2,1)S(1)}, bf16[2,768,128]{2,1,0:T(8,128)(2,1)S(1)}, u32[]{:S(2)}, u32[]{:S(2)}) collective-permute-start(bf16[2,768,128]{2,1,0:T(8,128)(2,1)S(1)} %get-tuple-element.246), channel_id=1, source_target_pairs={{1,0},{2,1},{3,2},{4,3},{5,4},{6,5},{7,6},{8,7},{9,8},{10,9},{11,1... | collective-permute-start | bytes 1179656 | tf_op jit(solution)/shard_map/ppermute | solution.py:18
  196.0 21.6 %collective-permute-start.10 = (bf16[2,768,128]{2,1,0:T(8,128)(2,1)S(1)}, bf16[2,768,128]{2,1,0:T(8,128)(2,1)S(1)}, u32[]{:S(2)}, u32[]{:S(2)}) collective-permute-start(bf16[2,768,128]{2,1,0:T(8,128)(2,1)S(1)} %get-tuple-element.247), channel_id=1, source_target_pairs={{3,0},{4,1},{5,2},{6,3},{7,4},{8,5},{9,6},{10,7},{11,8},{12,9},{13... | collective-permute-start | bytes 1179656 | tf_op jit(solution)/shard_map/ppermute | solution.py:18
  199.9 17.8 %collective-permute-start.9 = (bf16[2,768,128]{2,1,0:T(8,128)(2,1)S(1)}, bf16[2,768,128]{2,1,0:T(8,128)(2,1)S(1)}, u32[]{:S(2)}, u32[]{:S(2)}) collective-permute-start(bf16[2,768,128]{2,1,0:T(8,128)(2,1)S(1)} %get-tuple-element.248), channel_id=1, source_target_pairs={{4,0},{5,1},{6,2},{7,3},{8,4},{9,5},{10,6},{11,7},{12,8},{13,9},{1... | collective-permute-start | bytes 1179656 | tf_op jit(solution)/shard_map/ppermute | solution.py:18
  202.7 15.0 %collective-permute-start.15 = (bf16[2,768,128]{2,1,0:T(8,128)(2,1)S(1)}, bf16[2,768,128]{2,1,0:T(8,128)(2,1)S(1)}, u32[]{:S(2)}, u32[]{:S(2)}) collective-permute-start(bf16[2,768,128]{2,1,0:T(8,128)(2,1)S(1)} %get-tuple-element.249), channel_id=1, source_target_pairs={{0,5},{1,6},{2,7},{3,8},{4,9},{5,10},{6,11},{7,12},{8,13},{9,14},{... | collective-permute-start | bytes 1179656 | tf_op jit(solution)/shard_map/ppermute | solution.py:18
  215.0 19.3 %collective-permute-start.14 = (bf16[2,768,128]{2,1,0:T(8,128)(2,1)S(1)}, bf16[2,768,128]{2,1,0:T(8,128)(2,1)S(1)}, u32[]{:S(2)}, u32[]{:S(2)}) collective-permute-start(bf16[2,768,128]{2,1,0:T(8,128)(2,1)S(1)} %get-tuple-element.250), channel_id=1, source_target_pairs={{0,4},{1,5},{2,6},{3,7},{4,8},{5,9},{6,10},{7,11},{8,12},{9,13},{1... | collective-permute-start | bytes 1179656 | tf_op jit(solution)/shard_map/ppermute | solution.py:18
where the time goes:
time: 238 us; the launch traced here: 237 us
  matrix products  92.8 us (39%)
  waiting for transfers between devices  48.9 us (21%)
  starting transfers between devices  48.1 us (20%)
  other arithmetic  29.4 us (12%)
  local copies, waits for them, and re-layouts  15.5 us (7%)
    ppermute x16, waiting for transfers between devices, shifted(): lax.ppermute(value, axis, [(source, source + steps) for source in range(f...  48.9 us
    ppermute x16, starting transfers between devices, shifted(): lax.ppermute(value, axis, [(source, source + steps) for source in range(f...  48.1 us
    dot_general x9, matrix products, second_pass(): jnp.einsum('qd,kd->qk', queries, key_block, preferred_element_type=jnp.fl...  25.2 us
    dot_general x9, matrix products, first_pass(): jnp.einsum('qd,kd->qk', queries, key_block, preferred_element_type=jnp.fl...  22.9 us
    dot_general x9, matrix products, first_pass(): jnp.einsum('qd,kd->qk', grad_out, value_block, preferred_element_type=jnp...  18.1 us
    reduce_sum x9, other arithmetic, first_pass(): row_total = row_total * rescale + jnp.sum(unscaled, axis=1)  16.8 us
    dot_general x9, matrix products, second_pass(): jnp.dot(dscore, key_block, preferred_element_type=jnp.float32)  13.7 us
    dynamic_slice x18, local copies, waits for them, and re-layouts, per_device(): lax.scan(first_pass, start_state, (keys_all, values_all, slab_valid))  10.6 us
  transfers between devices with their start and end apart: 16, of which 6 were waited for; matrix products, arithmetic and copies ran while one was open for 1% of the time, Pallas kernels for 0%

commit v1 on v0

v1 whole, which is shorter than its diff:
```python
import functools
import math

import jax
import jax.numpy as jnp
from jax import lax
from jax.experimental import pallas as pl
from jax.experimental.pallas import tpu as pltpu
from jax.sharding import PartitionSpec as P

HEAD_DIM = 128
TILE_TOKENS = 256
ROW_TILES = 4
CHIP_ROWS = 2

SCALE = HEAD_DIM ** (-0.5)
SCALE2 = SCALE * math.log2(math.e)
BIG_NEGATIVE = -1e30
VMEM_LIMIT = 48 * 2**20

F32 = jnp.float32
BF16 = jnp.bfloat16
NT = (((1,), (1,)), ((), ()))
TN = (((0,), (0,)), ((), ()))
NN = (((1,), (0,)), ((), ()))


def dot(left, right, dims):
    return lax.dot_general(left, right, dims, preferred_element_type=F32)


def near(tile, tokens):
    return max(0, tile - 1) * TILE_TOKENS, min(tokens, (tile + 2) * TILE_TOKENS)


def whole(*shape):
    return pl.BlockSpec(shape, lambda j, valid: (0,) * len(shape))


def stacked(*shape):
    return pl.BlockSpec((1,) + shape, lambda j, valid: (j,) + (0,) * len(shape))


def params():
    return pltpu.CompilerParams(vmem_limit_bytes=VMEM_LIMIT)


def prepare_kernel(key_scales, value_scales, slots, queries, key_codes, value_codes, grad_out, kv, qg):
    blocks = slots.shape[1]
    size = queries.shape[0] // blocks
    for block in range(blocks):
        rows = slice(block * size, (block + 1) * size)
        slot = slots[0, block]
        kv[0, rows] = (key_codes[rows].astype(F32) * key_scales[slot]).astype(BF16)
        kv[1, rows] = (value_codes[rows].astype(F32) * value_scales[slot]).astype(BF16)
    qg[0] = queries[...]
    qg[1] = grad_out[...]


def prepare(queries, key_codes, value_codes, key_scales, value_scales, slots, grad_out):
    smem = pl.BlockSpec(memory_space=pltpu.SMEM)
    vmem = pl.BlockSpec(memory_space=pltpu.VMEM)
    pair = jax.ShapeDtypeStruct((2,) + queries.shape, BF16)
    return pl.pallas_call(
        prepare_kernel,
        in_specs=[smem, smem, smem, vmem, vmem, vmem, vmem],
        out_specs=[vmem, vmem],
        out_shape=[pair, pair],
        compiler_params=params(),
        name="prepare",
    )(key_scales, value_scales, slots, queries, key_codes, value_codes, grad_out)


def stats_kernel(finish, valid, qg, kv, start, out, *final):
    step = pl.program_id(0)
    tokens = qg.shape[1]

    @pl.when(step == 0)
    def _():
        out[...] = start[...]

    @pl.when(valid[step] > 0)
    def _():
        for tile in range(tokens // TILE_TOKENS):
            cols = slice(tile * TILE_TOKENS, (tile + 1) * TILE_TOKENS)
            low, high = near(tile, tokens)
            shape = ((high - low) // 8, 8, TILE_TOKENS)
            scores = (dot(kv[0, 0, low:high], qg[0, cols], NT) * SCALE2).reshape(shape)
            grad_prob = dot(kv[0, 1, low:high], qg[1, cols], NT).reshape(shape)
            top = out[0, :, cols]
            new_top = jnp.maximum(top, jnp.max(scores, axis=0))
            unscaled = jnp.exp2(scores - new_top[None])
            rescale = jnp.exp2(top - new_top)
            out[0, :, cols] = new_top
            out[1, :, cols] = out[1, :, cols] * rescale + jnp.sum(unscaled, axis=0)
            out[2, :, cols] = out[2, :, cols] * rescale + jnp.sum(unscaled * grad_prob, axis=0)

    if finish:

        @pl.when(step == pl.num_programs(0) - 1)
        def _():
            top = out[0]
            row_top = jnp.max(top, axis=0, keepdims=True)
            rescale = jnp.exp2(top - row_top)
            total = jnp.sum(out[1] * rescale, axis=0, keepdims=True)
            weighted = jnp.sum(out[2] * rescale, axis=0, keepdims=True)
            final[0][0:1] = row_top + jnp.log2(total)
            final[0][1:2] = weighted / total


def stats(valid, qg, kv, start, finish):
    count, _, tokens, dim = kv.shape
    shapes = [jax.ShapeDtypeStruct((3, 8, tokens), F32)]
    specs = [whole(3, 8, tokens)]
    if finish:
        shapes.append(jax.ShapeDtypeStruct((2, tokens), F32))
        specs.append(whole(2, tokens))
    return pl.pallas_call(
        functools.partial(stats_kernel, finish),
        grid_spec=pltpu.PrefetchScalarGridSpec(
            num_scalar_prefetch=1,
            grid=(count,),
            in_specs=[whole(2, tokens, dim), stacked(2, tokens, dim), whole(3, 8, tokens)],
            out_specs=specs,
        ),
        out_shape=shapes,
        compiler_params=params(),
        name="row_stats",
    )(valid, qg, kv, start)


def query_kernel(valid, qg, kv, rows, out, total):
    step = pl.program_id(0)
    tokens = qg.shape[1]

    @pl.when(step == 0)
    def _():
        total[...] = jnp.zeros_like(total)

    @pl.when(valid[step] > 0)
    def _():
        for tile in range(tokens // TILE_TOKENS):
            cols = slice(tile * TILE_TOKENS, (tile + 1) * TILE_TOKENS)
            low, high = near(tile, tokens)
            keys = kv[0, 0, low:high]
            scores = dot(keys, qg[0, cols], NT)
            attn_prob = jnp.exp2(scores * SCALE2 - rows[0:1, cols])
            grad_prob = dot(kv[0, 1, low:high], qg[1, cols], NT)
            dscore = (attn_prob * (grad_prob - rows[1:2, cols])).astype(BF16)
            total[:, cols] += dot(keys, dscore, TN)

    @pl.when(step == pl.num_programs(0) - 1)
    def _():
        out[...] = (total[...] * SCALE).T.astype(BF16)


def query_side(valid, qg, kv, rows):
    count, _, tokens, dim = kv.shape
    return pl.pallas_call(
        query_kernel,
        grid_spec=pltpu.PrefetchScalarGridSpec(
            num_scalar_prefetch=1,
            grid=(count,),
            in_specs=[whole(2, tokens, dim), stacked(2, tokens, dim), whole(2, tokens)],
            out_specs=whole(tokens, dim),
            scratch_shapes=[pltpu.VMEM((dim, tokens), F32)],
        ),
        out_shape=jax.ShapeDtypeStruct((tokens, dim), BF16),
        compiler_params=params(),
        name="query_side",
    )(valid, qg, kv, rows)


def key_kernel(valid, kv, qg, rows, key_out, value_out, total):
    step = pl.program_id(0)
    tokens = kv.shape[1]

    @pl.when(step == 0)
    def _():
        total[...] = jnp.zeros_like(total)

    @pl.when(valid[step] > 0)
    def _():
        for tile in range(tokens // TILE_TOKENS):
            cols = slice(tile * TILE_TOKENS, (tile + 1) * TILE_TOKENS)
            low, high = near(tile, tokens)
            queries = qg[0, 0, low:high]
            grads = qg[0, 1, low:high]
            scores = dot(kv[0, cols], queries, NT)
            attn_prob = jnp.exp2(scores * SCALE2 - rows[0, 0:1, low:high])
            grad_prob = dot(kv[1, cols], grads, NT)
            dscore = (attn_prob * (grad_prob - rows[0, 1:2, low:high])).astype(BF16)
            key_part = (dot(dscore, queries, NN) * SCALE).astype(BF16)
            value_part = dot(attn_prob.astype(BF16), grads, NN).astype(BF16)
            total[0, cols] += key_part.astype(F32)
            total[1, cols] += value_part.astype(F32)

    @pl.when(step == pl.num_programs(0) - 1)
    def _():
        key_out[...] = total[0].astype(BF16)
        value_out[...] = total[1].astype(BF16)


def key_side(valid, kv, qg, rows):
    count, _, tokens, dim = qg.shape
    return pl.pallas_call(
        key_kernel,
        grid_spec=pltpu.PrefetchScalarGridSpec(
            num_scalar_prefetch=1,
            grid=(count,),
            in_specs=[whole(2, tokens, dim), stacked(2, tokens, dim), stacked(2, tokens)],
            out_specs=[whole(tokens, dim), whole(tokens, dim)],
            scratch_shapes=[pltpu.VMEM((2, tokens, dim), F32)],
        ),
        out_shape=[jax.ShapeDtypeStruct((tokens, dim), BF16)] * 2,
        compiler_params=params(),
        name="key_side",
    )(valid, kv, qg, rows)


def swap_mate(value):
    count = lax.axis_size("tm")
    return lax.ppermute(value, "tm", [(source, source ^ 1) for source in range(count)])


def swap_cross(value):
    count = lax.axis_size("tm")
    return lax.ppermute(value, "tm", [(s, cross_of(s)) for s in range(count) if has_cross(s % ROW_TILES)])


def cross_of(index):
    return index + 1 if index % CHIP_ROWS == CHIP_ROWS - 1 else index - 1


def has_cross(row):
    return 0 <= cross_of(row) < ROW_TILES


def shift_frame(value, steps, cross_only=False):
    count = lax.axis_size("tm")
    pairs = [(s, s + steps * ROW_TILES) for s in range(count) if 0 <= s + steps * ROW_TILES < count]
    if cross_only:
        pairs = [pair for pair in pairs if has_cross(pair[0] % ROW_TILES)]
    return lax.ppermute(value, "tm", pairs)


def neighbours(value):
    before = shift_frame(value, 1)
    after = shift_frame(value, -1)
    cross = swap_cross(value)
    mate = swap_mate(value)
    cross_before = shift_frame(cross, 1, True)
    cross_after = shift_frame(cross, -1, True)
    mate_before = swap_mate(before)
    mate_after = swap_mate(after)
    return [value, mate, cross, before, after, mate_before, mate_after, cross_before, cross_after]


def row_neighbours(rows):
    trio = jnp.stack([rows, swap_mate(rows), swap_cross(rows)])
    before = shift_frame(trio, 1)
    after = shift_frame(trio, -1)
    return jnp.stack([trio[0], trio[1], trio[2], before[0], after[0], before[1], after[1], before[2], after[2]])


def per_device(queries, key_codes, value_codes, key_scales, value_scales, scale_slot, grad_out):
    index = lax.axis_index("tm")
    frames = lax.axis_size("tm") // ROW_TILES
    frame = index // ROW_TILES
    row = index % ROW_TILES
    before = (frame > 0).astype(jnp.int32)
    after = (frame < frames - 1).astype(jnp.int32)
    cross = functools.reduce(lax.bitwise_or, [row == r for r in range(ROW_TILES) if has_cross(r)]).astype(jnp.int32)
    one = jnp.ones((), jnp.int32)
    valid = jnp.stack([one, one, cross, before, after, before, after, cross * before, cross * after])

    kv, qg = prepare(queries, key_codes, value_codes, key_scales, value_scales, scale_slot, grad_out)
    kv_list = neighbours(kv)
    qg_later, kv_list[3], kv_list[4] = lax.optimization_barrier((qg, kv_list[3], kv_list[4]))
    qg_list = neighbours(qg_later)

    tokens = queries.shape[0]
    zeros = jnp.zeros((8, tokens), F32)
    start = jnp.stack([zeros + BIG_NEGATIVE, zeros, zeros])
    (running,) = stats(valid[:5], qg, jnp.stack(kv_list[:5]), start, False)
    _, rows = stats(valid[5:], qg, jnp.stack(kv_list[5:]), running, True)
    rows_all = row_neighbours(rows)
    query_grad = query_side(valid, qg, jnp.stack(kv_list), rows)
    key_grad, value_grad = key_side(valid, kv, jnp.stack(qg_list), rows_all)
    return query_grad, key_grad, value_grad


def solution(mesh):
    whole_axis = ("grp", "tm")
    flat = P(whole_axis)
    split = P(whole_axis, None)
    return jax.shard_map(
        per_device,
        mesh=mesh,
        in_specs=(split, split, split, flat, flat, split, split),
        out_specs=(split, split, split),
        check_vma=False,
    )
```

time: 238 us -> 96.6 us (0.41)
  the two profiles are of different devices: /device:TPU:20 before, /device:TPU:12 now
where the time goes in v1:
time: 96.6 us; the launch traced here: 96.1 us
  starting transfers between devices  37 us (38%)
  Pallas kernels  35.8 us (37%)
  waiting for transfers between devices  14.5 us (15%)
  local copies, waits for them, and re-layouts  7.21 us (7%)
  between operations  1.12 us (1%)
    ppermute x10, starting transfers between devices, shift_frame(): return lax.ppermute(value, 'tm', pairs)  28.8 us
    ppermute x10, waiting for transfers between devices, shift_frame(): return lax.ppermute(value, 'tm', pairs)  14.4 us
    pallas_call x1, Pallas kernels, key_side(): pl.pallas_call(key_kernel, grid_spec=pltpu.PrefetchScalarGridSpec(num_sca...  13.6 us
    pallas_call x1, Pallas kernels, query_side(): pl.pallas_call(query_kernel, grid_spec=pltpu.PrefetchScalarGridSpec(num_s...  11.6 us
    pallas_call x2, Pallas kernels, stats(): pl.pallas_call(functools.partial(stats_kernel, finish), grid_spec=pltpu.P...  10 us
    ppermute x3, starting transfers between devices, swap_cross(): lax.ppermute(value, 'tm', [(s, cross_of(s)) for s in range(count) if has_...  7.5 us
    unnamed x38, local copies, waits for them, and re-layouts  6.86 us
  transfers between devices with their start and end apart: 20, of which 4 were waited for; matrix products, arithmetic and copies ran while one was open for 2% of the time, Pallas kernels for 23%

profile of v1, /device:TPU:12, one launch (start us, length us, event | category | flops | bytes accessed | tf_op | source)
XLA Modules:
  0.0 96.1 jit_solution(8108034170904896251)
XLA Ops:
  0.6 0.9 copy-done
  1.6 0.9 copy-done.1
  2.5 0.9 copy-done.2
  3.4 0.9 copy-done.3
  4.3 0.7 copy-done.5
  5.0 0.7 copy-done.6
  5.7 0.7 copy-done.7
  6.3 0.6 prepare.1
  7.0 2.5 %collective-permute-start.1 = (bf16[2,768,128]{2,1,0:T(8,128)(2,1)S(1)}, bf16[2,768,128]{2,1,0:T(8,128)(2,1)S(1)}, u32[]{:S(2)}, u32[]{:S(2)}) collective-permute-start(bf16[2,768,128]{2,1,0:T(8,128)(2,1)S(1)} %get-tuple-element.12.kv), channel_id=1, source_target_pairs={{1,2},{2,1},{5,6},{6,5},{9,10},{10,9},{13,14},{14,13},{17,18},{18,... | collective-permute-start | bytes 1179656 | tf_op jit(solution)/shard_map/ppermute | solution.py:228
  9.5 3.5 %collective-permute-start.2 = (bf16[2,768,128]{2,1,0:T(8,128)(2,1)S(1)}, bf16[2,768,128]{2,1,0:T(8,128)(2,1)S(1)}, u32[]{:S(2)}, u32[]{:S(2)}) collective-permute-start(bf16[2,768,128]{2,1,0:T(8,128)(2,1)S(1)} %get-tuple-element.12.kv), channel_id=1, source_target_pairs={{0,4},{1,5},{2,6},{3,7},{4,8},{5,9},{6,10},{7,11},{8,12},{9,13},{1... | collective-permute-start | bytes 1179656 | tf_op jit(solution)/shard_map/ppermute | solution.py:244
  13.0 2.4 %collective-permute-start.3 = (bf16[2,768,128]{2,1,0:T(8,128)(2,1)S(1)}, bf16[2,768,128]{2,1,0:T(8,128)(2,1)S(1)}, u32[]{:S(2)}, u32[]{:S(2)}) collective-permute-start(bf16[2,768,128]{2,1,0:T(8,128)(2,1)S(1)} %get-tuple-element.12.kv), channel_id=1, source_target_pairs={{4,0},{5,1},{6,2},{7,3},{8,4},{9,5},{10,6},{11,7},{12,8},{13,9},{1... | collective-permute-start | bytes 1179656 | tf_op jit(solution)/shard_map/ppermute | solution.py:244
  15.8 5.3 %collective-permute-done.2 = bf16[2,768,128]{2,1,0:T(8,128)(2,1)S(1)} collective-permute-done((bf16[2,768,128]{2,1,0:T(8,128)(2,1)S(1)}, bf16[2,768,128]{2,1,0:T(8,128)(2,1)S(1)}, u32[]{:S(2)}, u32[]{:S(2)}) %collective-permute-start.2) | collective-permute-done | bytes 393248 | tf_op jit(solution)/shard_map/ppermute | solution.py:244
  21.1 3.2 %collective-permute-done.3 = bf16[2,768,128]{2,1,0:T(8,128)(2,1)S(1)} collective-permute-done((bf16[2,768,128]{2,1,0:T(8,128)(2,1)S(1)}, bf16[2,768,128]{2,1,0:T(8,128)(2,1)S(1)}, u32[]{:S(2)}, u32[]{:S(2)}) %collective-permute-start.3) | collective-permute-done | bytes 393248 | tf_op jit(solution)/shard_map/ppermute | solution.py:244
  24.3 3.5 %collective-permute-start.6 = (bf16[2,768,128]{2,1,0:T(8,128)(2,1)S(1)}, bf16[2,768,128]{2,1,0:T(8,128)(2,1)S(1)}, u32[]{:S(2)}, u32[]{:S(2)}) collective-permute-start(bf16[2,768,128]{2,1,0:T(8,128)(2,1)S(1)} %collective-permute-done.1), channel_id=1, source_target_pairs={{1,5},{2,6},{5,9},{6,10},{9,13},{10,14},{17,21},{18,22},{21,25},{2... | collective-permute-start | bytes 1179656 | tf_op jit(solution)/shard_map/ppermute | solution.py:244
  27.8 2.4 %collective-permute-start.7 = (bf16[2,768,128]{2,1,0:T(8,128)(2,1)S(1)}, bf16[2,768,128]{2,1,0:T(8,128)(2,1)S(1)}, u32[]{:S(2)}, u32[]{:S(2)}) collective-permute-start(bf16[2,768,128]{2,1,0:T(8,128)(2,1)S(1)} %collective-permute-done.1), channel_id=1, source_target_pairs={{5,1},{6,2},{9,5},{10,6},{13,9},{14,10},{21,17},{22,18},{25,21},{2... | collective-permute-start | bytes 1179656 | tf_op jit(solution)/shard_map/ppermute | solution.py:244
  30.3 0.5 collective-permute-start.5
  31.1 0.2 bitcast_dynamic-update-slice_fusion.11
  31.5 5.1 %row_stats.2.start = f32[3,8,768]{2,1,0:T(8,128)S(1)} custom-call(s32[5]{0:T(128)S(1)} %pad_add_fusion.1.valid, bf16[2,768,128]{2,1,0:T(8,128)(2,1)S(1)} %get-tuple-element.16.qg, bf16[5,2,768,128]{3,2,1,0:T(8,128)(2,1)S(1)} %get-tuple-element.19.kv, f32[3,8,768]{2,1,0:T(8,128)S(1)} %copy-done.4), custom_call_target="tpu_custom_call" | custom-call | tf_op jit(solution)/shard_map/row_stats/pallas_call | solution.py:118
  36.6 2.0 %collective-permute-start.9 = (bf16[2,768,128]{2,1,0:T(8,128)(2,1)S(1)}, bf16[2,768,128]{2,1,0:T(8,128)(2,1)S(1)}, u32[]{:S(2)}, u32[]{:S(2)}) collective-permute-start(bf16[2,768,128]{2,1,0:T(8,128)(2,1)S(1)} %get-tuple-element.16.qg), channel_id=1, source_target_pairs={{1,2},{2,1},{5,6},{6,5},{9,10},{10,9},{13,14},{14,13},{17,18},{18,... | collective-permute-start | bytes 1179656 | tf_op jit(solution)/shard_map/ppermute | solution.py:228
  38.7 3.5 %collective-permute-start.10 = (bf16[2,768,128]{2,1,0:T(8,128)(2,1)S(1)}, bf16[2,768,128]{2,1,0:T(8,128)(2,1)S(1)}, u32[]{:S(2)}, u32[]{:S(2)}) collective-permute-start(bf16[2,768,128]{2,1,0:T(8,128)(2,1)S(1)} %get-tuple-element.16.qg), channel_id=1, source_target_pairs={{0,4},{1,5},{2,6},{3,7},{4,8},{5,9},{6,10},{7,11},{8,12},{9,13},{1... | collective-permute-start | bytes 1179656 | tf_op jit(solution)/shard_map/ppermute | solution.py:244
  42.2 2.4 %collective-permute-start.11 = (bf16[2,768,128]{2,1,0:T(8,128)(2,1)S(1)}, bf16[2,768,128]{2,1,0:T(8,128)(2,1)S(1)}, u32[]{:S(2)}, u32[]{:S(2)}) collective-permute-start(bf16[2,768,128]{2,1,0:T(8,128)(2,1)S(1)} %get-tuple-element.16.qg), channel_id=1, source_target_pairs={{4,0},{5,1},{6,2},{7,3},{8,4},{9,5},{10,6},{11,7},{12,8},{13,9},{1... | collective-permute-start | bytes 1179656 | tf_op jit(solution)/shard_map/ppermute | solution.py:244
  44.6 0.2 pad_maximum_fusion.kv
  44.8 4.9 %row_stats.3 = (f32[3,8,768]{2,1,0:T(8,128)}, f32[2,768]{1,0:T(2,128)S(1)}) custom-call(s32[4]{0:T(128)S(1)} %pad_add_fusion.valid, bf16[2,768,128]{2,1,0:T(8,128)(2,1)S(1)} %get-tuple-element.16.qg, bf16[4,2,768,128]{3,2,1,0:T(8,128)(2,1)S(1)} %pad_maximum_fusion.kv, f32[3,8,768]{2,1,0:T(8,128)S(1)} %row_stats.2.start), custom_call_target="tpu_custom_call" | custom-call | tf_op jit(solution)/shard_map/row_stats/pallas_call | solution.py:118
  49.9 11.6 %query_side.1 = bf16[768,128]{1,0:T(8,128)(2,1)} custom-call(s32[9]{0:T(128)S(1)} %stack.127.valid, bf16[2,768,128]{2,1,0:T(8,128)(2,1)S(1)} %get-tuple-element.16.qg, bf16[9,2,768,128]{3,2,1,0:T(8,128)(2,1)S(1)} %constant_dynamic-update-slice_fusion.kv, f32[2,768]{1,0:T(2,128)S(1)} %get-tuple-element.15.rows), custom_call_target="tpu_custom_call" | custom-call | tf_op jit(solution)/shard_map/query_side/pallas_call | solution.py:159
  61.5 2.9 %collective-permute-start.17 = (f32[2,768]{1,0:T(2,128)S(1)}, f32[2,768]{1,0:T(2,128)S(1)}, u32[]{:S(2)}, u32[]{:S(2)}) collective-permute-start(f32[2,768]{1,0:T(2,128)S(1)} %get-tuple-element.15.rows), channel_id=1, source_target_pairs={{1,2},{2,1},{5,6},{6,5},{9,10},{10,9},{13,14},{14,13},{17,18},{18,... | collective-permute-start | bytes 18440 | tf_op jit(solution)/shard_map/ppermute | solution.py:228
  64.6 3.4 %collective-permute-start.14 = (bf16[2,768,128]{2,1,0:T(8,128)(2,1)S(1)}, bf16[2,768,128]{2,1,0:T(8,128)(2,1)S(1)}, u32[]{:S(2)}, u32[]{:S(2)}) collective-permute-start(bf16[2,768,128]{2,1,0:T(8,128)(2,1)S(1)} %collective-permute-done.9), channel_id=1, source_target_pairs={{1,5},{2,6},{5,9},{6,10},{9,13},{10,14},{17,21},{18,22},{21,25},{2... | collective-permute-start | bytes 1179656 | tf_op jit(solution)/shard_map/ppermute | solution.py:244
  68.4 2.4 %collective-permute-start.15 = (bf16[2,768,128]{2,1,0:T(8,128)(2,1)S(1)}, bf16[2,768,128]{2,1,0:T(8,128)(2,1)S(1)}, u32[]{:S(2)}, u32[]{:S(2)}) collective-permute-start(bf16[2,768,128]{2,1,0:T(8,128)(2,1)S(1)} %collective-permute-done.9), channel_id=1, source_target_pairs={{5,1},{6,2},{9,5},{10,6},{13,9},{14,10},{21,17},{22,18},{25,21},{2... | collective-permute-start | bytes 1179656 | tf_op jit(solution)/shard_map/ppermute | solution.py:244
  70.9 3.4 %collective-permute-start.18 = (f32[3,2,768]{2,1,0:T(2,128)S(1)}, f32[3,2,768]{2,1,0:T(2,128)S(1)}, u32[]{:S(2)}, u32[]{:S(2)}) collective-permute-start(f32[3,2,768]{2,1,0:T(2,128)S(1)} %pad_maximum_fusion.1), channel_id=1, source_target_pairs={{0,4},{1,5},{2,6},{3,7},{4,8},{5,9},{6,10},{7,11},{8,12},{9,13},{1... | collective-permute-start | bytes 55304 | tf_op jit(solution)/shard_map/ppermute | solution.py:244
  74.3 2.2 %collective-permute-done.18 = f32[3,2,768]{2,1,0:T(2,128)S(1)} collective-permute-done((f32[3,2,768]{2,1,0:T(2,128)S(1)}, f32[3,2,768]{2,1,0:T(2,128)S(1)}, u32[]{:S(2)}, u32[]{:S(2)}) %collective-permute-start.18) | collective-permute-done | bytes 18464 | tf_op jit(solution)/shard_map/ppermute | solution.py:244
  76.5 1.9 %collective-permute-start.19 = (f32[3,2,768]{2,1,0:T(2,128)S(1)}, f32[3,2,768]{2,1,0:T(2,128)S(1)}, u32[]{:S(2)}, u32[]{:S(2)}) collective-permute-start(f32[3,2,768]{2,1,0:T(2,128)S(1)} %pad_maximum_fusion.1), channel_id=1, source_target_pairs={{4,0},{5,1},{6,2},{7,3},{8,4},{9,5},{10,6},{11,7},{12,8},{13,9},{1... | collective-permute-start | bytes 55304 | tf_op jit(solution)/shard_map/ppermute | solution.py:244
  78.4 3.7 %collective-permute-done.19 = f32[3,2,768]{2,1,0:T(2,128)S(1)} collective-permute-done((f32[3,2,768]{2,1,0:T(2,128)S(1)}, f32[3,2,768]{2,1,0:T(2,128)S(1)}, u32[]{:S(2)}, u32[]{:S(2)}) %collective-permute-start.19) | collective-permute-done | bytes 18464 | tf_op jit(solution)/shard_map/ppermute | solution.py:244
  82.5 13.6 %key_side.1 = (bf16[768,128]{1,0:T(8,128)(2,1)}, bf16[768,128]{1,0:T(8,128)(2,1)}) custom-call(s32[9]{0:T(128)S(1)} %stack.127.valid, bf16[2,768,128]{2,1,0:T(8,128)(2,1)S(1)} %get-tuple-element.12.kv, bf16[9,2,768,128]{3,2,1,0:T(8,128)(2,1)S(1)} %bitcast_dynamic-update-slice_fusion.qg, f32[9,2,768]{2,1,0:T(2,128)S(1)} %constant_dynamic-update-slice_fusion.4.rows), custom_call_target="tpu_custom_call" | custom-call | tf_op jit(solution)/shard_map/key_side/pallas_call | solution.py:206
  (61 shorter events, 1.9 us)
Async XLA Ops:
  0.6 0.9 copy-start
  1.6 0.9 copy-start.1
  2.5 0.9 copy-start.2
  3.4 0.9 copy-start.3
  4.3 0.7 copy-start.5
  5.0 0.7 copy-start.6
  5.7 0.7 copy-start.7
  6.9 24.5 %copy-start.4 = (f32[3,8,768]{2,1,0:T(8,128)S(1)}, f32[3,8,768]{2,1,0:T(8,128)}, u32[]{:S(2)}) copy-start(f32[3,8,768]{2,1,0:T(8,128)} %constant.38.clone.1.start) | copy-start | bytes 221188
  7.0 23.3 %collective-permute-start = (bf16[2,768,128]{2,1,0:T(8,128)(2,1)S(1)}, bf16[2,768,128]{2,1,0:T(8,128)(2,1)S(1)}, u32[]{:S(2)}, u32[]{:S(2)}) collective-permute-start(bf16[2,768,128]{2,1,0:T(8,128)(2,1)S(1)} %get-tuple-element.12.kv), channel_id=1, source_target_pairs={{0,1},{1,0},{2,3},{3,2},{4,5},{5,4},{6,7},{7,6},{8,9},{9,8},{10,11... | collective-permute-start | bytes 1179656 | tf_op jit(solution)/shard_map/ppermute | solution.py:223
  7.0 17.3 %collective-permute-start.1 = (bf16[2,768,128]{2,1,0:T(8,128)(2,1)S(1)}, bf16[2,768,128]{2,1,0:T(8,128)(2,1)S(1)}, u32[]{:S(2)}, u32[]{:S(2)}) collective-permute-start(bf16[2,768,128]{2,1,0:T(8,128)(2,1)S(1)} %get-tuple-element.12.kv), channel_id=1, source_target_pairs={{1,2},{2,1},{5,6},{6,5},{9,10},{10,9},{13,14},{14,13},{17,18},{18,... | collective-permute-start | bytes 1179656 | tf_op jit(solution)/shard_map/ppermute | solution.py:228
  9.5 11.6 %collective-permute-start.2 = (bf16[2,768,128]{2,1,0:T(8,128)(2,1)S(1)}, bf16[2,768,128]{2,1,0:T(8,128)(2,1)S(1)}, u32[]{:S(2)}, u32[]{:S(2)}) collective-permute-start(bf16[2,768,128]{2,1,0:T(8,128)(2,1)S(1)} %get-tuple-element.12.kv), channel_id=1, source_target_pairs={{0,4},{1,5},{2,6},{3,7},{4,8},{5,9},{6,10},{7,11},{8,12},{9,13},{1... | collective-permute-start | bytes 1179656 | tf_op jit(solution)/shard_map/ppermute | solution.py:244
  13.0 11.3 %collective-permute-start.3 = (bf16[2,768,128]{2,1,0:T(8,128)(2,1)S(1)}, bf16[2,768,128]{2,1,0:T(8,128)(2,1)S(1)}, u32[]{:S(2)}, u32[]{:S(2)}) collective-permute-start(bf16[2,768,128]{2,1,0:T(8,128)(2,1)S(1)} %get-tuple-element.12.kv), channel_id=1, source_target_pairs={{4,0},{5,1},{6,2},{7,3},{8,4},{9,5},{10,6},{11,7},{12,8},{13,9},{1... | collective-permute-start | bytes 1179656 | tf_op jit(solution)/shard_map/ppermute | solution.py:244
  24.3 37.2 %collective-permute-start.8 = (bf16[2,768,128]{2,1,0:T(8,128)(2,1)S(1)}, bf16[2,768,128]{2,1,0:T(8,128)(2,1)S(1)}, u32[]{:S(2)}, u32[]{:S(2)}) collective-permute-start(bf16[2,768,128]{2,1,0:T(8,128)(2,1)S(1)} %get-tuple-element.16.qg), channel_id=1, source_target_pairs={{0,1},{1,0},{2,3},{3,2},{4,5},{5,4},{6,7},{7,6},{8,9},{9,8},{10,11... | collective-permute-start | bytes 1179656 | tf_op jit(solution)/shard_map/ppermute | solution.py:223
  24.3 12.3 %collective-permute-start.6 = (bf16[2,768,128]{2,1,0:T(8,128)(2,1)S(1)}, bf16[2,768,128]{2,1,0:T(8,128)(2,1)S(1)}, u32[]{:S(2)}, u32[]{:S(2)}) collective-permute-start(bf16[2,768,128]{2,1,0:T(8,128)(2,1)S(1)} %collective-permute-done.1), channel_id=1, source_target_pairs={{1,5},{2,6},{5,9},{6,10},{9,13},{10,14},{17,21},{18,22},{21,25},{2... | collective-permute-start | bytes 1179656 | tf_op jit(solution)/shard_map/ppermute | solution.py:244
  27.8 10.8 %collective-permute-start.7 = (bf16[2,768,128]{2,1,0:T(8,128)(2,1)S(1)}, bf16[2,768,128]{2,1,0:T(8,128)(2,1)S(1)}, u32[]{:S(2)}, u32[]{:S(2)}) collective-permute-start(bf16[2,768,128]{2,1,0:T(8,128)(2,1)S(1)} %collective-permute-done.1), channel_id=1, source_target_pairs={{5,1},{6,2},{9,5},{10,6},{13,9},{14,10},{21,17},{22,18},{25,21},{2... | collective-permute-start | bytes 1179656 | tf_op jit(solution)/shard_map/ppermute | solution.py:244
  30.2 11.9 %collective-permute-start.4 = (bf16[2,768,128]{2,1,0:T(8,128)(2,1)S(1)}, bf16[2,768,128]{2,1,0:T(8,128)(2,1)S(1)}, u32[]{:S(2)}, u32[]{:S(2)}) collective-permute-start(bf16[2,768,128]{2,1,0:T(8,128)(2,1)S(1)} %collective-permute-done.2), channel_id=1, source_target_pairs={{0,1},{1,0},{2,3},{3,2},{4,5},{5,4},{6,7},{7,6},{8,9},{9,8},{10,11... | collective-permute-start | bytes 1179656 | tf_op jit(solution)/shard_map/ppermute | solution.py:223
  30.3 14.3 %collective-permute-start.5 = (bf16[2,768,128]{2,1,0:T(8,128)(2,1)S(1)}, bf16[2,768,128]{2,1,0:T(8,128)(2,1)S(1)}, u32[]{:S(2)}, u32[]{:S(2)}) collective-permute-start(bf16[2,768,128]{2,1,0:T(8,128)(2,1)S(1)} %collective-permute-done.3), channel_id=1, source_target_pairs={{0,1},{1,0},{2,3},{3,2},{4,5},{5,4},{6,7},{7,6},{8,9},{9,8},{10,11... | collective-permute-start | bytes 1179656 | tf_op jit(solution)/shard_map/ppermute | solution.py:223
  36.6 28.0 %collective-permute-start.9 = (bf16[2,768,128]{2,1,0:T(8,128)(2,1)S(1)}, bf16[2,768,128]{2,1,0:T(8,128)(2,1)S(1)}, u32[]{:S(2)}, u32[]{:S(2)}) collective-permute-start(bf16[2,768,128]{2,1,0:T(8,128)(2,1)S(1)} %get-tuple-element.16.qg), channel_id=1, source_target_pairs={{1,2},{2,1},{5,6},{6,5},{9,10},{10,9},{13,14},{14,13},{17,18},{18,... | collective-permute-start | bytes 1179656 | tf_op jit(solution)/shard_map/ppermute | solution.py:228
  38.7 25.8 %collective-permute-start.10 = (bf16[2,768,128]{2,1,0:T(8,128)(2,1)S(1)}, bf16[2,768,128]{2,1,0:T(8,128)(2,1)S(1)}, u32[]{:S(2)}, u32[]{:S(2)}) collective-permute-start(bf16[2,768,128]{2,1,0:T(8,128)(2,1)S(1)} %get-tuple-element.16.qg), channel_id=1, source_target_pairs={{0,4},{1,5},{2,6},{3,7},{4,8},{5,9},{6,10},{7,11},{8,12},{9,13},{1... | collective-permute-start | bytes 1179656 | tf_op jit(solution)/shard_map/ppermute | solution.py:244
  42.2 26.1 %collective-permute-start.11 = (bf16[2,768,128]{2,1,0:T(8,128)(2,1)S(1)}, bf16[2,768,128]{2,1,0:T(8,128)(2,1)S(1)}, u32[]{:S(2)}, u32[]{:S(2)}) collective-permute-start(bf16[2,768,128]{2,1,0:T(8,128)(2,1)S(1)} %get-tuple-element.16.qg), channel_id=1, source_target_pairs={{4,0},{5,1},{6,2},{7,3},{8,4},{9,5},{10,6},{11,7},{12,8},{13,9},{1... | collective-permute-start | bytes 1179656 | tf_op jit(solution)/shard_map/ppermute | solution.py:244
  49.7 18.7 %collective-permute-start.16 = (f32[2,768]{1,0:T(2,128)S(1)}, f32[2,768]{1,0:T(2,128)S(1)}, u32[]{:S(2)}, u32[]{:S(2)}) collective-permute-start(f32[2,768]{1,0:T(2,128)S(1)} %get-tuple-element.15.rows), channel_id=1, source_target_pairs={{0,1},{1,0},{2,3},{3,2},{4,5},{5,4},{6,7},{7,6},{8,9},{9,8},{10,11... | collective-permute-start | bytes 18440 | tf_op jit(solution)/shard_map/ppermute | solution.py:223
  61.5 9.3 %collective-permute-start.17 = (f32[2,768]{1,0:T(2,128)S(1)}, f32[2,768]{1,0:T(2,128)S(1)}, u32[]{:S(2)}, u32[]{:S(2)}) collective-permute-start(f32[2,768]{1,0:T(2,128)S(1)} %get-tuple-element.15.rows), channel_id=1, source_target_pairs={{1,2},{2,1},{5,6},{6,5},{9,10},{10,9},{13,14},{14,13},{17,18},{18,... | collective-permute-start | bytes 18440 | tf_op jit(solution)/shard_map/ppermute | solution.py:228
  64.5 17.7 %collective-permute-start.12 = (bf16[2,768,128]{2,1,0:T(8,128)(2,1)S(1)}, bf16[2,768,128]{2,1,0:T(8,128)(2,1)S(1)}, u32[]{:S(2)}, u32[]{:S(2)}) collective-permute-start(bf16[2,768,128]{2,1,0:T(8,128)(2,1)S(1)} %collective-permute-done.10), channel_id=1, source_target_pairs={{0,1},{1,0},{2,3},{3,2},{4,5},{5,4},{6,7},{7,6},{8,9},{9,8},{10,11... | collective-permute-start | bytes 1179656 | tf_op jit(solution)/shard_map/ppermute | solution.py:223
  64.6 17.7 %collective-permute-start.14 = (bf16[2,768,128]{2,1,0:T(8,128)(2,1)S(1)}, bf16[2,768,128]{2,1,0:T(8,128)(2,1)S(1)}, u32[]{:S(2)}, u32[]{:S(2)}) collective-permute-start(bf16[2,768,128]{2,1,0:T(8,128)(2,1)S(1)} %collective-permute-done.9), channel_id=1, source_target_pairs={{1,5},{2,6},{5,9},{6,10},{9,13},{10,14},{17,21},{18,22},{21,25},{2... | collective-permute-start | bytes 1179656 | tf_op jit(solution)/shard_map/ppermute | solution.py:244
  68.2 14.0 %collective-permute-start.13 = (bf16[2,768,128]{2,1,0:T(8,128)(2,1)S(1)}, bf16[2,768,128]{2,1,0:T(8,128)(2,1)S(1)}, u32[]{:S(2)}, u32[]{:S(2)}) collective-permute-start(bf16[2,768,128]{2,1,0:T(8,128)(2,1)S(1)} %collective-permute-done.11), channel_id=1, source_target_pairs={{0,1},{1,0},{2,3},{3,2},{4,5},{5,4},{6,7},{7,6},{8,9},{9,8},{10,11... | collective-permute-start | bytes 1179656 | tf_op jit(solution)/shard_map/ppermute | solution.py:223
  68.4 14.0 %collective-permute-start.15 = (bf16[2,768,128]{2,1,0:T(8,128)(2,1)S(1)}, bf16[2,768,128]{2,1,0:T(8,128)(2,1)S(1)}, u32[]{:S(2)}, u32[]{:S(2)}) collective-permute-start(bf16[2,768,128]{2,1,0:T(8,128)(2,1)S(1)} %collective-permute-done.9), channel_id=1, source_target_pairs={{5,1},{6,2},{9,5},{10,6},{13,9},{14,10},{21,17},{22,18},{25,21},{2... | collective-permute-start | bytes 1179656 | tf_op jit(solution)/shard_map/ppermute | solution.py:244
  70.9 5.7 %collective-permute-start.18 = (f32[3,2,768]{2,1,0:T(2,128)S(1)}, f32[3,2,768]{2,1,0:T(2,128)S(1)}, u32[]{:S(2)}, u32[]{:S(2)}) collective-permute-start(f32[3,2,768]{2,1,0:T(2,128)S(1)} %pad_maximum_fusion.1), channel_id=1, source_target_pairs={{0,4},{1,5},{2,6},{3,7},{4,8},{5,9},{6,10},{7,11},{8,12},{9,13},{1... | collective-permute-start | bytes 55304 | tf_op jit(solution)/shard_map/ppermute | solution.py:244
  76.5 5.6 %collective-permute-start.19 = (f32[3,2,768]{2,1,0:T(2,128)S(1)}, f32[3,2,768]{2,1,0:T(2,128)S(1)}, u32[]{:S(2)}, u32[]{:S(2)}) collective-permute-start(f32[3,2,768]{2,1,0:T(2,128)S(1)} %pad_maximum_fusion.1), channel_id=1, source_target_pairs={{4,0},{5,1},{6,2},{7,3},{8,4},{9,5},{10,6},{11,7},{12,8},{13,9},{1... | collective-permute-start | bytes 55304 | tf_op jit(solution)/shard_map/ppermute | solution.py:244

commit v2 on v1

v2 whole, which is shorter than its diff:
```python
import functools
import math

import jax
import jax.numpy as jnp
from jax import lax
from jax.experimental import pallas as pl
from jax.experimental.pallas import tpu as pltpu
from jax.sharding import PartitionSpec as P

HEAD_DIM = 128
TILE_TOKENS = 256
ROW_TILES = 4
CHIP_ROWS = 2

SCALE = HEAD_DIM ** (-0.5)
SCALE2 = SCALE * math.log2(math.e)
BIG_NEGATIVE = -1e30
STATS_KEYS = 128
VMEM_LIMIT = 48 * 2**20

F32 = jnp.float32
BF16 = jnp.bfloat16
NT = (((1,), (1,)), ((), ()))
TN = (((0,), (0,)), ((), ()))
NN = (((1,), (0,)), ((), ()))


def dot(left, right, dims):
    return lax.dot_general(left, right, dims, preferred_element_type=F32)


def near(tile, tokens):
    return max(0, tile - 1) * TILE_TOKENS, min(tokens, (tile + 2) * TILE_TOKENS)


def params():
    return pltpu.CompilerParams(vmem_limit_bytes=VMEM_LIMIT)


def cost(products, slabs, tokens, dim):
    pairs = slabs * tokens * tokens
    return pl.CostEstimate(flops=8 * products * pairs * dim, bytes_accessed=slabs * 4 * tokens * dim, transcendentals=pairs)


def prepare_kernel(key_scales, value_scales, slots, queries, key_codes, value_codes, grad_out, kv, qg,
                   scale_mem, slot_mem, codes, packed, sems):
    blocks = slots.shape[1]
    size = queries.shape[0] // blocks
    loads = [
        pltpu.make_async_copy(key_scales, scale_mem.at[0], sems.at[0]),
        pltpu.make_async_copy(value_scales, scale_mem.at[1], sems.at[1]),
        pltpu.make_async_copy(slots.at[0], slot_mem, sems.at[2]),
        pltpu.make_async_copy(key_codes, codes.at[0], sems.at[3]),
        pltpu.make_async_copy(value_codes, codes.at[1], sems.at[4]),
        pltpu.make_async_copy(queries, packed.at[2], sems.at[5]),
        pltpu.make_async_copy(grad_out, packed.at[3], sems.at[6]),
    ]
    for load in loads:
        load.start()
    for load in loads[:5]:
        load.wait()
    for block in range(blocks):
        rows = slice(block * size, (block + 1) * size)
        slot = slot_mem[block]
        for part in range(2):
            packed[part, rows] = (codes[part, rows].astype(F32) * scale_mem[part, slot]).astype(BF16)
    stores = [pltpu.make_async_copy(packed.at[0:2], kv, sems.at[7])]
    stores[0].start()
    for load in loads[5:]:
        load.wait()
    stores.append(pltpu.make_async_copy(packed.at[2:4], qg, sems.at[8]))
    stores[1].start()
    for store in stores:
        store.wait()


def prepare(queries, key_codes, value_codes, key_scales, value_scales, slots, grad_out):
    blocks = slots.shape[1]
    anywhere = pl.BlockSpec(memory_space=pl.ANY)
    return pl.pallas_call(
        prepare_kernel,
        in_specs=[anywhere] * 7,
        out_specs=[anywhere] * 2,
        out_shape=[jax.ShapeDtypeStruct((n,) + queries.shape, BF16) for n in (2, 2)],
        scratch_shapes=[
            pltpu.SMEM((2, blocks), F32),
            pltpu.SMEM((blocks,), jnp.int32),
            pltpu.VMEM((2,) + queries.shape, BF16),
            pltpu.VMEM((4,) + queries.shape, BF16),
            pltpu.SemaphoreType.DMA((9,)),
        ],
        compiler_params=pltpu.CompilerParams(vmem_limit_bytes=60 * 2**20),
        name="prepare",
    )(key_scales, value_scales, slots, queries, key_codes, value_codes, grad_out)


def vmem_call(kernel, name, products, slabs, outs, scratch, *operands):
    tokens, dim = operands[1].shape[1:]
    vmem = pl.BlockSpec(memory_space=pltpu.VMEM)
    return pl.pallas_call(
        kernel,
        in_specs=[pl.BlockSpec(memory_space=pltpu.SMEM)] + [vmem] * (len(operands) - 1),
        out_specs=[vmem] * len(outs),
        out_shape=outs,
        scratch_shapes=scratch,
        cost_estimate=cost(products, slabs, tokens, dim),
        compiler_params=params(),
        name=name,
    )(*operands)


def arrays_of(window):
    arrays = []
    for array, _ in window:
        if not any(array is other for other in arrays):
            arrays.append(array)
    places = [([array is other for other in arrays].index(True), offset) for array, offset in window]
    return arrays, places


def for_each_slab(valid, first, places, refs, body):
    for number, (place, offset) in enumerate(places):

        @pl.when(valid[first + number] > 0)
        def _(ref=refs[place], offset=offset, number=number):
            body(number, lambda part, rows: ref[offset + part, rows])


def stats_kernel(first, places, finish, valid, qg, start, *refs):
    tokens = qg.shape[1]
    running = refs[-1]
    running[...] = start[...]

    def body(number, part):
        for tile in range(tokens // TILE_TOKENS):
            cols = slice(tile * TILE_TOKENS, (tile + 1) * TILE_TOKENS)
            low, high = near(tile, tokens)
            shape = (STATS_KEYS // 8, 8, TILE_TOKENS)
            top, total, weighted = running[0, :, cols], running[1, :, cols], running[2, :, cols]
            for key in range(low, high, STATS_KEYS):
                keys = slice(key, key + STATS_KEYS)
                scores = (dot(part(0, keys), qg[0, cols], NT) * SCALE2).reshape(shape)
                grad_prob = dot(part(1, keys), qg[1, cols], NT).reshape(shape)
                new_top = jnp.maximum(top, jnp.max(scores, axis=0))
                unscaled = jnp.exp2(scores - new_top[None])
                rescale = jnp.exp2(top - new_top)
                top = new_top
                total = total * rescale + jnp.sum(unscaled, axis=0)
                weighted = weighted * rescale + jnp.sum(unscaled * grad_prob, axis=0)
            running[0, :, cols], running[1, :, cols], running[2, :, cols] = top, total, weighted

    for_each_slab(valid, first, places, refs, body)
    if finish:
        final = refs[-2]
        top = running[0]
        row_top = jnp.max(top, axis=0, keepdims=True)
        rescale = jnp.exp2(top - row_top)
        total = jnp.sum(running[1] * rescale, axis=0, keepdims=True)
        weighted = jnp.sum(running[2] * rescale, axis=0, keepdims=True)
        final[0:1] = row_top + jnp.log2(total)
        final[1:2] = weighted / total


def stats(valid, first, qg, window, start, finish):
    tokens = qg.shape[1]
    arrays, places = arrays_of(window)
    running = (3, 8, tokens)
    outs = jax.ShapeDtypeStruct((2, tokens) if finish else running, F32)
    return vmem_call(
        functools.partial(stats_kernel, first, places, finish), "row_stats", 2, len(window),
        [outs], [pltpu.VMEM(running, F32)] if finish else [], valid, qg, start, *arrays,
    )[0]


def query_kernel(places, valid, qg, rows, *refs):
    out, total = refs[-2:]
    tokens = qg.shape[1]
    total[...] = jnp.zeros_like(total)

    def body(number, part):
        for tile in range(tokens // TILE_TOKENS):
            cols = slice(tile * TILE_TOKENS, (tile + 1) * TILE_TOKENS)
            low, high = near(tile, tokens)
            keys = part(0, slice(low, high))
            scores = dot(keys, qg[0, cols], NT)
            attn_prob = jnp.exp2(scores * SCALE2 - rows[0:1, cols])
            grad_prob = dot(part(1, slice(low, high)), qg[1, cols], NT)
            dscore = (attn_prob * (grad_prob - rows[1:2, cols])).astype(BF16)
            total[:, cols] += dot(keys, dscore, TN)

    for_each_slab(valid, 0, places, refs, body)
    out[...] = (total[...] * SCALE).T.astype(BF16)


def query_side(valid, qg, window, rows):
    tokens, dim = qg.shape[1:]
    arrays, places = arrays_of(window)
    return vmem_call(
        functools.partial(query_kernel, places), "query_side", 3, len(window),
        [jax.ShapeDtypeStruct((tokens, dim), BF16)], [pltpu.VMEM((dim, tokens), F32)], valid, qg, rows, *arrays,
    )[0]


def key_kernel(places, valid, kv, rows, *refs):
    key_out, value_out, totals = refs[-3:]
    tokens = kv.shape[1]
    totals[...] = jnp.zeros_like(totals)

    def body(number, part):
        for tile in range(tokens // TILE_TOKENS):
            cols = slice(tile * TILE_TOKENS, (tile + 1) * TILE_TOKENS)
            low, high = near(tile, tokens)
            queries = part(0, slice(low, high))
            grads = part(1, slice(low, high))
            scores = dot(kv[0, cols], queries, NT)
            attn_prob = jnp.exp2(scores * SCALE2 - rows[number, 0:1, low:high])
            grad_prob = dot(kv[1, cols], grads, NT)
            dscore = (attn_prob * (grad_prob - rows[number, 1:2, low:high])).astype(BF16)
            key_part = (dot(dscore, queries, NN) * SCALE).astype(BF16)
            value_part = dot(attn_prob.astype(BF16), grads, NN).astype(BF16)
            totals[0, cols] += key_part.astype(F32)
            totals[1, cols] += value_part.astype(F32)

    for_each_slab(valid, 0, places, refs, body)
    key_out[...] = totals[0].astype(BF16)
    value_out[...] = totals[1].astype(BF16)


def key_side(valid, kv, window, rows):
    tokens, dim = kv.shape[1:]
    arrays, places = arrays_of(window)
    return vmem_call(
        functools.partial(key_kernel, places), "key_side", 4, len(window),
        [jax.ShapeDtypeStruct((tokens, dim), BF16)] * 2, [pltpu.VMEM((2, tokens, dim), F32)], valid, kv, rows, *arrays,
    )


def swap_mate(value):
    count = lax.axis_size("tm")
    return lax.ppermute(value, "tm", [(source, source ^ 1) for source in range(count)])


def swap_cross(value):
    count = lax.axis_size("tm")
    return lax.ppermute(value, "tm", [(s, cross_of(s)) for s in range(count) if has_cross(s % ROW_TILES)])


def cross_of(index):
    return index + 1 if index % CHIP_ROWS == CHIP_ROWS - 1 else index - 1


def has_cross(row):
    return 0 <= cross_of(row) < ROW_TILES


def shift_frame(value, steps, cross_only=False):
    count = lax.axis_size("tm")
    pairs = [(s, s + steps * ROW_TILES) for s in range(count) if 0 <= s + steps * ROW_TILES < count]
    if cross_only:
        pairs = [pair for pair in pairs if has_cross(pair[0] % ROW_TILES)]
    return lax.ppermute(value, "tm", pairs)


def row_neighbours(rows):
    trio = jnp.stack([rows, swap_mate(rows), swap_cross(rows)])
    before = shift_frame(trio, 1)
    after = shift_frame(trio, -1)
    return jnp.stack([trio[0], trio[1], trio[2], before[0], after[0], before[1], after[1], before[2], after[2]])


def per_device(queries, key_codes, value_codes, key_scales, value_scales, scale_slot, grad_out):
    index = lax.axis_index("tm")
    frames = lax.axis_size("tm") // ROW_TILES
    frame = index // ROW_TILES
    row = index % ROW_TILES
    before = (frame > 0).astype(jnp.int32)
    after = (frame < frames - 1).astype(jnp.int32)
    cross = functools.reduce(lax.bitwise_or, [row == r for r in range(ROW_TILES) if has_cross(r)]).astype(jnp.int32)
    one = jnp.ones((), jnp.int32)
    valid = jnp.stack([one, one, cross, before, after, before, after, cross * before, cross * after])

    kv, qg = prepare(queries, key_codes, value_codes, key_scales, value_scales, scale_slot, grad_out)
    kv_before = shift_frame(kv, 1)
    kv_after = shift_frame(kv, -1)
    kv_cross = swap_cross(kv)
    kv_mate = swap_mate(kv)
    qg_cross = swap_cross(qg)
    kv_cross_before = shift_frame(kv_cross, 1, True)
    kv_cross_after = shift_frame(kv_cross, -1, True)
    kv_mate_before = swap_mate(kv_before)
    kv_mate_after = swap_mate(kv_after)

    qg_pair, _, _ = lax.optimization_barrier((jnp.concatenate([qg, qg_cross]), kv_before, kv_after))
    qg_before = shift_frame(qg_pair, 1)
    qg_after = shift_frame(qg_pair, -1)
    qg_mate = swap_mate(qg)
    qg_mate_before = swap_mate(qg_before)
    qg_mate_after = swap_mate(qg_after)
    qg_window = [(qg, 0), (qg_mate, 0), (qg_cross, 0), (qg_before, 0), (qg_after, 0),
                 (qg_mate_before, 0), (qg_mate_after, 0), (qg_before, 2), (qg_after, 2)]

    tokens = queries.shape[0]
    zeros = jnp.zeros((8, tokens), F32)
    running = jnp.stack([zeros + BIG_NEGATIVE, zeros, zeros])
    groups = [
        [(kv, 0), (kv_mate, 0)],
        [(kv_cross, 0), (kv_before, 0), (kv_after, 0)],
        [(kv_mate_before, 0), (kv_mate_after, 0), (kv_cross_before, 0), (kv_cross_after, 0)],
    ]
    running = stats(valid, 0, qg, groups[0], running, False)
    running = stats(valid, 2, qg, groups[1], running, False)
    rows = stats(valid, 5, qg, groups[2], running, True)
    rows_all = row_neighbours(rows)
    query_grad = query_side(valid, qg, groups[0] + groups[1] + groups[2], rows)
    key_grad, value_grad = key_side(valid, kv, qg_window, rows_all)
    return query_grad, key_grad, value_grad


def solution(mesh):
    whole_axis = ("grp", "tm")
    flat = P(whole_axis)
    split = P(whole_axis, None)
    return jax.shard_map(
        per_device,
        mesh=mesh,
        in_specs=(split, split, split, flat, flat, split, split),
        out_specs=(split, split, split),
        check_vma=False,
    )
```

time: 96.6 us -> 76.6 us (0.79)
  the two profiles are of different devices: /device:TPU:12 before, /device:TPU:11 now
where the time goes in v2:
time: 76.6 us; the launch traced here: 75.9 us
  Pallas kernels  35.6 us (46%)
  starting transfers between devices  33.1 us (43%)
  waiting for transfers between devices  4.01 us (5%)
  local copies, waits for them, and re-layouts  2.15 us (3%)
  between operations  0.97 us (1%)
    pallas_call x5, Pallas kernels, vmem_call(): pl.pallas_call(kernel, in_specs=[pl.BlockSpec(memory_space=pltpu.SMEM)] +...  33.5 us
    ppermute x8, starting transfers between devices, shift_frame(): return lax.ppermute(value, 'tm', pairs)  21.3 us
    ppermute x3, starting transfers between devices, swap_cross(): lax.ppermute(value, 'tm', [(s, cross_of(s)) for s in range(count) if has_...  10.5 us
    ppermute x7, waiting for transfers between devices, swap_mate(): lax.ppermute(value, 'tm', [(source, source ^ 1) for source in range(count)])  2.87 us
    pallas_call x1, Pallas kernels, prepare(): pl.pallas_call(prepare_kernel, in_specs=[anywhere] * 7, out_specs=[anywhe...  2.06 us
    unnamed x16, local copies, waits for them, and re-layouts  2.05 us
  transfers between devices with their start and end apart: 18, of which 3 were waited for; matrix products, arithmetic and copies ran while one was open for 0% of the time, Pallas kernels for 26%

profile of v2, /device:TPU:11, one launch (start us, length us, event | category | flops | bytes accessed | tf_op | source)
XLA Modules:
  0.0 75.9 jit_solution(6152759264626037048)
XLA Ops:
  0.6 2.1 %prepare.1 = (bf16[2,768,128]{2,1,0:T(8,128)(2,1)}, bf16[2,768,128]{2,1,0:T(8,128)(2,1)}) custom-call(f32[6]{0:T(128)} %key_scales.1, f32[6]{0:T(128)} %value_scales.1, s32[1,6]{1,0:T(1,128)} %slots.1, bf16[768,128]{1,0:T(8,128)(2,1)} %queries.1, bf16[768,128]{1,0:T(8,128)(2,1)} %key_codes.1, bf16[768,128]{1,0:T(8,128)(2,1)} %value_codes.1, ...), custom_call_target="tpu_custom_call" | custom-call | tf_op jit(solution)/shard_map/prepare/pallas_call | solution.py:81
  2.7 0.0 copy-start.3
  2.7 3.8 %collective-permute-start.1 = (bf16[2,768,128]{2,1,0:T(8,128)(2,1)}, bf16[2,768,128]{2,1,0:T(8,128)(2,1)S(1)}, u32[]{:S(2)}, u32[]{:S(2)}) collective-permute-start(bf16[2,768,128]{2,1,0:T(8,128)(2,1)} %get-tuple-element.9.refs_0_.kv), channel_id=1, source_target_pairs={{1,2},{2,1},{5,6},{6,5},{9,10},{10,9},{13,14},{14,13},{17,18},{18,... | collective-permute-start | bytes 1179656 | tf_op jit(solution)/shard_map/ppermute | solution.py:246
  6.6 0.1 collective-permute-start
  6.6 2.1 %collective-permute-start.3 = (bf16[2,768,128]{2,1,0:T(8,128)(2,1)}, bf16[2,768,128]{2,1,0:T(8,128)(2,1)S(1)}, u32[]{:S(2)}, u32[]{:S(2)}) collective-permute-start(bf16[2,768,128]{2,1,0:T(8,128)(2,1)} %get-tuple-element.9.refs_0_.kv), channel_id=1, source_target_pairs={{4,0},{5,1},{6,2},{7,3},{8,4},{9,5},{10,6},{11,7},{12,8},{13,9},{1... | collective-permute-start | bytes 1179656 | tf_op jit(solution)/shard_map/ppermute | solution.py:262
  8.7 3.2 %collective-permute-start.2 = (bf16[2,768,128]{2,1,0:T(8,128)(2,1)}, bf16[2,768,128]{2,1,0:T(8,128)(2,1)S(1)}, u32[]{:S(2)}, u32[]{:S(2)}) collective-permute-start(bf16[2,768,128]{2,1,0:T(8,128)(2,1)} %get-tuple-element.9.refs_0_.kv), channel_id=1, source_target_pairs={{0,4},{1,5},{2,6},{3,7},{4,8},{5,9},{6,10},{7,11},{8,12},{9,13},{1... | collective-permute-start | bytes 1179656 | tf_op jit(solution)/shard_map/ppermute | solution.py:262
  11.9 2.5 %collective-permute-start.13 = (bf16[2,768,128]{2,1,0:T(8,128)(2,1)}, bf16[2,768,128]{2,1,0:T(8,128)(2,1)S(1)}, u32[]{:S(2)}, u32[]{:S(2)}) collective-permute-start(bf16[2,768,128]{2,1,0:T(8,128)(2,1)} %get-tuple-element.8.qg.refs_0_), channel_id=1, source_target_pairs={{1,2},{2,1},{5,6},{6,5},{9,10},{10,9},{13,14},{14,13},{17,18},{18,... | collective-permute-start | bytes 1179656 | tf_op jit(solution)/shard_map/ppermute | solution.py:246
  14.5 0.1 stack.48.valid
  14.6 0.1 collective-permute-start.12
  14.7 2.1 %collective-permute-start.7 = (bf16[2,768,128]{2,1,0:T(8,128)(2,1)S(1)}, bf16[2,768,128]{2,1,0:T(8,128)(2,1)S(1)}, u32[]{:S(2)}, u32[]{:S(2)}) collective-permute-start(bf16[2,768,128]{2,1,0:T(8,128)(2,1)S(1)} %collective-permute-done.1.refs_0_.refs_2_), channel_id=1, source_target_pairs={{5,1},{6,2},{9,5},{10,6},{13,9},{14,10},{21,17},{22,18},{25,21},{2... | collective-permute-start | bytes 1179656 | tf_op jit(solution)/shard_map/ppermute | solution.py:262
  16.8 1.0 %copy-done = bf16[2,768,128]{2,1,0:T(8,128)(2,1)S(1)} copy-done((bf16[2,768,128]{2,1,0:T(8,128)(2,1)S(1)}, bf16[2,768,128]{2,1,0:T(8,128)(2,1)}, u32[]{:S(2)}) %copy-start) | copy-done | bytes 393240
  17.8 1.0 %copy-done.2 = bf16[2,768,128]{2,1,0:T(8,128)(2,1)S(1)} copy-done((bf16[2,768,128]{2,1,0:T(8,128)(2,1)S(1)}, bf16[2,768,128]{2,1,0:T(8,128)(2,1)}, u32[]{:S(2)}) %copy-start.2) | copy-done | bytes 393240
  18.8 2.0 %row_stats.3.start = f32[3,8,768]{2,1,0:T(8,128)S(1)} custom-call(s32[9]{0:T(128)S(1)} %stack.48.valid, bf16[2,768,128]{2,1,0:T(8,128)(2,1)S(1)} %copy-done, f32[3,8,768]{2,1,0:T(8,128)S(1)} %copy-done.3, bf16[2,768,128]{2,1,0:T(8,128)(2,1)S(1)} %copy-done.2, bf16[2,768,128]{2,1,0:T(8,128)(2,1)S(1)} %collective-permute-done.refs_1_), custom_call_target="tpu_custom_call" | custom-call | flops 2415919104 | bytes 786432 | tf_op jit(solution)/shard_map/row_stats/pallas_call | solution.py:101
  20.8 3.3 %collective-permute-start.6 = (bf16[2,768,128]{2,1,0:T(8,128)(2,1)S(1)}, bf16[2,768,128]{2,1,0:T(8,128)(2,1)S(1)}, u32[]{:S(2)}, u32[]{:S(2)}) collective-permute-start(bf16[2,768,128]{2,1,0:T(8,128)(2,1)S(1)} %collective-permute-done.1.refs_0_.refs_2_), channel_id=1, source_target_pairs={{1,5},{2,6},{5,9},{6,10},{9,13},{10,14},{17,21},{18,22},{21,25},{2... | collective-permute-start | bytes 1179656 | tf_op jit(solution)/shard_map/ppermute | solution.py:262
  24.1 0.1 collective-permute-start.5
  24.2 0.5 collective-permute-start.4
  24.7 0.1 pad_maximum_fusion
  24.8 2.8 %row_stats.4.start = f32[3,8,768]{2,1,0:T(8,128)S(1)} custom-call(s32[9]{0:T(128)S(1)} %stack.48.valid, bf16[2,768,128]{2,1,0:T(8,128)(2,1)S(1)} %copy-done.1, f32[3,8,768]{2,1,0:T(8,128)S(1)} %row_stats.3.start, bf16[2,768,128]{2,1,0:T(8,128)(2,1)S(1)} %collective-permute-done.1.refs_0_.refs_2_, ...), custom_call_target="tpu_custom_call" | custom-call | flops 3623878656 | bytes 1179648 | tf_op jit(solution)/shard_map/row_stats/pallas_call | solution.py:101
  27.6 1.9 %collective-permute-start.15 = (bf16[4,768,128]{2,1,0:T(8,128)(2,1)S(1)}, bf16[4,768,128]{2,1,0:T(8,128)(2,1)S(1)}, u32[]{:S(2)}, u32[]{:S(2)}) collective-permute-start(bf16[4,768,128]{2,1,0:T(8,128)(2,1)S(1)} %pad_maximum_fusion), channel_id=1, source_target_pairs={{4,0},{5,1},{6,2},{7,3},{8,4},{9,5},{10,6},{11,7},{12,8},{13,9},{1... | collective-permute-start | bytes 2359304 | tf_op jit(solution)/shard_map/ppermute | solution.py:262
  29.5 3.4 %collective-permute-start.14 = (bf16[4,768,128]{2,1,0:T(8,128)(2,1)S(1)}, bf16[4,768,128]{2,1,0:T(8,128)(2,1)S(1)}, u32[]{:S(2)}, u32[]{:S(2)}) collective-permute-start(bf16[4,768,128]{2,1,0:T(8,128)(2,1)S(1)} %pad_maximum_fusion), channel_id=1, source_target_pairs={{0,4},{1,5},{2,6},{3,7},{4,8},{5,9},{6,10},{7,11},{8,12},{9,13},{1... | collective-permute-start | bytes 2359304 | tf_op jit(solution)/shard_map/ppermute | solution.py:262
  32.9 3.6 %row_stats.5.rows = f32[2,768]{1,0:T(2,128)S(1)} custom-call(s32[9]{0:T(128)S(1)} %stack.48.valid, bf16[2,768,128]{2,1,0:T(8,128)(2,1)S(1)} %copy-done.1, f32[3,8,768]{2,1,0:T(8,128)S(1)} %row_stats.4.start, bf16[2,768,128]{2,1,0:T(8,128)(2,1)S(1)} %collective-permute-done.4.refs_0_.refs_5_, bf16[2,768,128]{2,1,0:T(8,128)(2,1)S(1)} %collective-permute-done.5.refs_1_.refs_6_, ...), custom_call_target="tpu_custom_call" | custom-call | flops 4831838208 | bytes 1572864 | tf_op jit(solution)/shard_map/row_stats/pallas_call | solution.py:101
  36.5 4.2 %collective-permute-start.9 = (f32[2,768]{1,0:T(2,128)S(1)}, f32[2,768]{1,0:T(2,128)S(1)}, u32[]{:S(2)}, u32[]{:S(2)}) collective-permute-start(f32[2,768]{1,0:T(2,128)S(1)} %row_stats.5.rows), channel_id=1, source_target_pairs={{1,2},{2,1},{5,6},{6,5},{9,10},{10,9},{13,14},{14,13},{17,18},{18,... | collective-permute-start | bytes 18440 | tf_op jit(solution)/shard_map/ppermute | solution.py:246
  40.7 0.1 collective-permute-start.8
  40.8 11.6 %query_side.1 = bf16[768,128]{1,0:T(8,128)(2,1)} custom-call(s32[9]{0:T(128)S(1)} %stack.48.valid, bf16[2,768,128]{2,1,0:T(8,128)(2,1)S(1)} %copy-done.1, f32[2,768]{1,0:T(2,128)S(1)} %row_stats.5.rows, bf16[2,768,128]{2,1,0:T(8,128)(2,1)S(1)} %copy-done.2, bf16[2,768,128]{2,1,0:T(8,128)(2,1)S(1)} %collective-permute-done.refs_1_, ...), custom_call_target="tpu_custom_call" | custom-call | flops 16307453952 | bytes 3538944 | tf_op jit(solution)/shard_map/query_side/pallas_call | solution.py:101
  52.5 1.9 %collective-permute-start.11 = (f32[3,2,768]{2,1,0:T(2,128)S(1)}, f32[3,2,768]{2,1,0:T(2,128)S(1)}, u32[]{:S(2)}, u32[]{:S(2)}) collective-permute-start(f32[3,2,768]{2,1,0:T(2,128)S(1)} %pad_maximum_fusion.1), channel_id=1, source_target_pairs={{4,0},{5,1},{6,2},{7,3},{8,4},{9,5},{10,6},{11,7},{12,8},{13,9},{1... | collective-permute-start | bytes 55304 | tf_op jit(solution)/shard_map/ppermute | solution.py:262
  54.4 3.4 %collective-permute-start.10 = (f32[3,2,768]{2,1,0:T(2,128)S(1)}, f32[3,2,768]{2,1,0:T(2,128)S(1)}, u32[]{:S(2)}, u32[]{:S(2)}) collective-permute-start(f32[3,2,768]{2,1,0:T(2,128)S(1)} %pad_maximum_fusion.1), channel_id=1, source_target_pairs={{0,4},{1,5},{2,6},{3,7},{4,8},{5,9},{6,10},{7,11},{8,12},{9,13},{1... | collective-permute-start | bytes 55304 | tf_op jit(solution)/shard_map/ppermute | solution.py:262
  57.8 1.1 %collective-permute-done.10 = f32[3,2,768]{2,1,0:T(2,128)S(1)} collective-permute-done((f32[3,2,768]{2,1,0:T(2,128)S(1)}, f32[3,2,768]{2,1,0:T(2,128)S(1)}, u32[]{:S(2)}, u32[]{:S(2)}) %collective-permute-start.10) | collective-permute-done | bytes 18464 | tf_op jit(solution)/shard_map/ppermute | solution.py:262
  58.9 0.1 collective-permute-start.17
  59.0 0.5 collective-permute-start.16
  59.5 1.7 %collective-permute-done.17.refs_6_ = bf16[4,768,128]{2,1,0:T(8,128)(2,1)S(1)} collective-permute-done((bf16[4,768,128]{2,1,0:T(8,128)(2,1)S(1)}, bf16[4,768,128]{2,1,0:T(8,128)(2,1)S(1)}, u32[]{:S(2)}, u32[]{:S(2)}) %collective-permute-start.17) | collective-permute-done | bytes 786464 | tf_op jit(solution)/shard_map/ppermute | solution.py:241
  61.3 1.1 %collective-permute-done.16.refs_5_ = bf16[4,768,128]{2,1,0:T(8,128)(2,1)S(1)} collective-permute-done((bf16[4,768,128]{2,1,0:T(8,128)(2,1)S(1)}, bf16[4,768,128]{2,1,0:T(8,128)(2,1)S(1)}, u32[]{:S(2)}, u32[]{:S(2)}) %collective-permute-start.16) | collective-permute-done | bytes 786464 | tf_op jit(solution)/shard_map/ppermute | solution.py:241
  62.4 13.5 %key_side.1 = (bf16[768,128]{1,0:T(8,128)(2,1)}, bf16[768,128]{1,0:T(8,128)(2,1)}) custom-call(s32[9]{0:T(128)S(1)} %stack.48.valid, bf16[2,768,128]{2,1,0:T(8,128)(2,1)S(1)} %copy-done.2, f32[9,2,768]{2,1,0:T(2,128)S(1)} %constant_dynamic-update-slice_fusion.rows, bf16[2,768,128]{2,1,0:T(8,128)(2,1)S(1)} %copy-done.1, ...), custom_call_target="tpu_custom_call" | custom-call | flops 21743271936 | bytes 3538944 | tf_op jit(solution)/shard_map/key_side/pallas_call | solution.py:101
  (31 shorter events, 0.1 us)
Async XLA Ops:
  2.7 14.1 %copy-start.3 = (f32[3,8,768]{2,1,0:T(8,128)S(1)}, f32[3,8,768]{2,1,0:T(8,128)}, u32[]{:S(2)}) copy-start(f32[3,8,768]{2,1,0:T(8,128)} %constant.38.clone.1.start) | copy-start | bytes 221188
  2.7 11.9 %collective-permute-start.1 = (bf16[2,768,128]{2,1,0:T(8,128)(2,1)}, bf16[2,768,128]{2,1,0:T(8,128)(2,1)S(1)}, u32[]{:S(2)}, u32[]{:S(2)}) collective-permute-start(bf16[2,768,128]{2,1,0:T(8,128)(2,1)} %get-tuple-element.9.refs_0_.kv), channel_id=1, source_target_pairs={{1,2},{2,1},{5,6},{6,5},{9,10},{10,9},{13,14},{14,13},{17,18},{18,... | collective-permute-start | bytes 1179656 | tf_op jit(solution)/shard_map/ppermute | solution.py:246
  6.6 8.1 %collective-permute-start = (bf16[2,768,128]{2,1,0:T(8,128)(2,1)}, bf16[2,768,128]{2,1,0:T(8,128)(2,1)S(1)}, u32[]{:S(2)}, u32[]{:S(2)}) collective-permute-start(bf16[2,768,128]{2,1,0:T(8,128)(2,1)} %get-tuple-element.9.refs_0_.kv), channel_id=1, source_target_pairs={{0,1},{1,0},{2,3},{3,2},{4,5},{5,4},{6,7},{7,6},{8,9},{9,8},{10,11... | collective-permute-start | bytes 1179656 | tf_op jit(solution)/shard_map/ppermute | solution.py:241
  6.6 14.2 %collective-permute-start.3 = (bf16[2,768,128]{2,1,0:T(8,128)(2,1)}, bf16[2,768,128]{2,1,0:T(8,128)(2,1)S(1)}, u32[]{:S(2)}, u32[]{:S(2)}) collective-permute-start(bf16[2,768,128]{2,1,0:T(8,128)(2,1)} %get-tuple-element.9.refs_0_.kv), channel_id=1, source_target_pairs={{4,0},{5,1},{6,2},{7,3},{8,4},{9,5},{10,6},{11,7},{12,8},{13,9},{1... | collective-permute-start | bytes 1179656 | tf_op jit(solution)/shard_map/ppermute | solution.py:262
  8.7 15.4 %collective-permute-start.2 = (bf16[2,768,128]{2,1,0:T(8,128)(2,1)}, bf16[2,768,128]{2,1,0:T(8,128)(2,1)S(1)}, u32[]{:S(2)}, u32[]{:S(2)}) collective-permute-start(bf16[2,768,128]{2,1,0:T(8,128)(2,1)} %get-tuple-element.9.refs_0_.kv), channel_id=1, source_target_pairs={{0,4},{1,5},{2,6},{3,7},{4,8},{5,9},{6,10},{7,11},{8,12},{9,13},{1... | collective-permute-start | bytes 1179656 | tf_op jit(solution)/shard_map/ppermute | solution.py:262
  11.9 12.3 %collective-permute-start.13 = (bf16[2,768,128]{2,1,0:T(8,128)(2,1)}, bf16[2,768,128]{2,1,0:T(8,128)(2,1)S(1)}, u32[]{:S(2)}, u32[]{:S(2)}) collective-permute-start(bf16[2,768,128]{2,1,0:T(8,128)(2,1)} %get-tuple-element.8.qg.refs_0_), channel_id=1, source_target_pairs={{1,2},{2,1},{5,6},{6,5},{9,10},{10,9},{13,14},{14,13},{17,18},{18,... | collective-permute-start | bytes 1179656 | tf_op jit(solution)/shard_map/ppermute | solution.py:246
  14.6 45.0 %collective-permute-start.12 = (bf16[2,768,128]{2,1,0:T(8,128)(2,1)}, bf16[2,768,128]{2,1,0:T(8,128)(2,1)S(1)}, u32[]{:S(2)}, u32[]{:S(2)}) collective-permute-start(bf16[2,768,128]{2,1,0:T(8,128)(2,1)} %get-tuple-element.8.qg.refs_0_), channel_id=1, source_target_pairs={{0,1},{1,0},{2,3},{3,2},{4,5},{5,4},{6,7},{7,6},{8,9},{9,8},{10,11... | collective-permute-start | bytes 1179656 | tf_op jit(solution)/shard_map/ppermute | solution.py:241
  14.7 18.3 %collective-permute-start.7 = (bf16[2,768,128]{2,1,0:T(8,128)(2,1)S(1)}, bf16[2,768,128]{2,1,0:T(8,128)(2,1)S(1)}, u32[]{:S(2)}, u32[]{:S(2)}) collective-permute-start(bf16[2,768,128]{2,1,0:T(8,128)(2,1)S(1)} %collective-permute-done.1.refs_0_.refs_2_), channel_id=1, source_target_pairs={{5,1},{6,2},{9,5},{10,6},{13,9},{14,10},{21,17},{22,18},{25,21},{2... | collective-permute-start | bytes 1179656 | tf_op jit(solution)/shard_map/ppermute | solution.py:262
  16.8 1.0 %copy-start = (bf16[2,768,128]{2,1,0:T(8,128)(2,1)S(1)}, bf16[2,768,128]{2,1,0:T(8,128)(2,1)}, u32[]{:S(2)}) copy-start(bf16[2,768,128]{2,1,0:T(8,128)(2,1)} %get-tuple-element.8.qg.refs_0_) | copy-start | bytes 1179652
  17.8 1.0 %copy-start.2 = (bf16[2,768,128]{2,1,0:T(8,128)(2,1)S(1)}, bf16[2,768,128]{2,1,0:T(8,128)(2,1)}, u32[]{:S(2)}) copy-start(bf16[2,768,128]{2,1,0:T(8,128)(2,1)} %get-tuple-element.9.refs_0_.kv) | copy-start | bytes 1179652
  20.8 4.0 %copy-start.1 = (bf16[2,768,128]{2,1,0:T(8,128)(2,1)S(1)}, bf16[2,768,128]{2,1,0:T(8,128)(2,1)}, u32[]{:S(2)}) copy-start(bf16[2,768,128]{2,1,0:T(8,128)(2,1)} %get-tuple-element.8.qg.refs_0_) | copy-start | bytes 1179652
  20.8 12.1 %collective-permute-start.6 = (bf16[2,768,128]{2,1,0:T(8,128)(2,1)S(1)}, bf16[2,768,128]{2,1,0:T(8,128)(2,1)S(1)}, u32[]{:S(2)}, u32[]{:S(2)}) collective-permute-start(bf16[2,768,128]{2,1,0:T(8,128)(2,1)S(1)} %collective-permute-done.1.refs_0_.refs_2_), channel_id=1, source_target_pairs={{1,5},{2,6},{5,9},{6,10},{9,13},{10,14},{17,21},{18,22},{21,25},{2... | collective-permute-start | bytes 1179656 | tf_op jit(solution)/shard_map/ppermute | solution.py:262
  24.1 3.5 %collective-permute-start.5 = (bf16[2,768,128]{2,1,0:T(8,128)(2,1)S(1)}, bf16[2,768,128]{2,1,0:T(8,128)(2,1)S(1)}, u32[]{:S(2)}, u32[]{:S(2)}) collective-permute-start(bf16[2,768,128]{2,1,0:T(8,128)(2,1)S(1)} %collective-permute-done.3.refs_2_.refs_4_), channel_id=1, source_target_pairs={{0,1},{1,0},{2,3},{3,2},{4,5},{5,4},{6,7},{7,6},{8,9},{9,8},{10,11... | collective-permute-start | bytes 1179656 | tf_op jit(solution)/shard_map/ppermute | solution.py:241
  24.2 5.3 %collective-permute-start.4 = (bf16[2,768,128]{2,1,0:T(8,128)(2,1)S(1)}, bf16[2,768,128]{2,1,0:T(8,128)(2,1)S(1)}, u32[]{:S(2)}, u32[]{:S(2)}) collective-permute-start(bf16[2,768,128]{2,1,0:T(8,128)(2,1)S(1)} %collective-permute-done.2.refs_1_.refs_3_), channel_id=1, source_target_pairs={{0,1},{1,0},{2,3},{3,2},{4,5},{5,4},{6,7},{7,6},{8,9},{9,8},{10,11... | collective-permute-start | bytes 1179656 | tf_op jit(solution)/shard_map/ppermute | solution.py:241
  27.6 31.3 %collective-permute-start.15 = (bf16[4,768,128]{2,1,0:T(8,128)(2,1)S(1)}, bf16[4,768,128]{2,1,0:T(8,128)(2,1)S(1)}, u32[]{:S(2)}, u32[]{:S(2)}) collective-permute-start(bf16[4,768,128]{2,1,0:T(8,128)(2,1)S(1)} %pad_maximum_fusion), channel_id=1, source_target_pairs={{4,0},{5,1},{6,2},{7,3},{8,4},{9,5},{10,6},{11,7},{12,8},{13,9},{1... | collective-permute-start | bytes 2359304 | tf_op jit(solution)/shard_map/ppermute | solution.py:262
  29.5 29.5 %collective-permute-start.14 = (bf16[4,768,128]{2,1,0:T(8,128)(2,1)S(1)}, bf16[4,768,128]{2,1,0:T(8,128)(2,1)S(1)}, u32[]{:S(2)}, u32[]{:S(2)}) collective-permute-start(bf16[4,768,128]{2,1,0:T(8,128)(2,1)S(1)} %pad_maximum_fusion), channel_id=1, source_target_pairs={{0,4},{1,5},{2,6},{3,7},{4,8},{5,9},{6,10},{7,11},{8,12},{9,13},{1... | collective-permute-start | bytes 2359304 | tf_op jit(solution)/shard_map/ppermute | solution.py:262
  36.5 15.9 %collective-permute-start.9 = (f32[2,768]{1,0:T(2,128)S(1)}, f32[2,768]{1,0:T(2,128)S(1)}, u32[]{:S(2)}, u32[]{:S(2)}) collective-permute-start(f32[2,768]{1,0:T(2,128)S(1)} %row_stats.5.rows), channel_id=1, source_target_pairs={{1,2},{2,1},{5,6},{6,5},{9,10},{10,9},{13,14},{14,13},{17,18},{18,... | collective-permute-start | bytes 18440 | tf_op jit(solution)/shard_map/ppermute | solution.py:246
  40.7 11.7 %collective-permute-start.8 = (f32[2,768]{1,0:T(2,128)S(1)}, f32[2,768]{1,0:T(2,128)S(1)}, u32[]{:S(2)}, u32[]{:S(2)}) collective-permute-start(f32[2,768]{1,0:T(2,128)S(1)} %row_stats.5.rows), channel_id=1, source_target_pairs={{0,1},{1,0},{2,3},{3,2},{4,5},{5,4},{6,7},{7,6},{8,9},{9,8},{10,11... | collective-permute-start | bytes 18440 | tf_op jit(solution)/shard_map/ppermute | solution.py:241
  52.5 6.4 %collective-permute-start.11 = (f32[3,2,768]{2,1,0:T(2,128)S(1)}, f32[3,2,768]{2,1,0:T(2,128)S(1)}, u32[]{:S(2)}, u32[]{:S(2)}) collective-permute-start(f32[3,2,768]{2,1,0:T(2,128)S(1)} %pad_maximum_fusion.1), channel_id=1, source_target_pairs={{4,0},{5,1},{6,2},{7,3},{8,4},{9,5},{10,6},{11,7},{12,8},{13,9},{1... | collective-permute-start | bytes 55304 | tf_op jit(solution)/shard_map/ppermute | solution.py:262
  54.4 4.5 %collective-permute-start.10 = (f32[3,2,768]{2,1,0:T(2,128)S(1)}, f32[3,2,768]{2,1,0:T(2,128)S(1)}, u32[]{:S(2)}, u32[]{:S(2)}) collective-permute-start(f32[3,2,768]{2,1,0:T(2,128)S(1)} %pad_maximum_fusion.1), channel_id=1, source_target_pairs={{0,4},{1,5},{2,6},{3,7},{4,8},{5,9},{6,10},{7,11},{8,12},{9,13},{1... | collective-permute-start | bytes 55304 | tf_op jit(solution)/shard_map/ppermute | solution.py:262
  58.9 2.4 %collective-permute-start.17 = (bf16[4,768,128]{2,1,0:T(8,128)(2,1)S(1)}, bf16[4,768,128]{2,1,0:T(8,128)(2,1)S(1)}, u32[]{:S(2)}, u32[]{:S(2)}) collective-permute-start(bf16[4,768,128]{2,1,0:T(8,128)(2,1)S(1)} %collective-permute-done.15.refs_4_), channel_id=1, source_target_pairs={{0,1},{1,0},{2,3},{3,2},{4,5},{5,4},{6,7},{7,6},{8,9},{9,8},{10,11... | collective-permute-start | bytes 2359304 | tf_op jit(solution)/shard_map/ppermute | solution.py:241
  59.0 3.4 %collective-permute-start.16 = (bf16[4,768,128]{2,1,0:T(8,128)(2,1)S(1)}, bf16[4,768,128]{2,1,0:T(8,128)(2,1)S(1)}, u32[]{:S(2)}, u32[]{:S(2)}) collective-permute-start(bf16[4,768,128]{2,1,0:T(8,128)(2,1)S(1)} %collective-permute-done.14.refs_3_), channel_id=1, source_target_pairs={{0,1},{1,0},{2,3},{3,2},{4,5},{5,4},{6,7},{7,6},{8,9},{9,8},{10,11... | collective-permute-start | bytes 2359304 | tf_op jit(solution)/shard_map/ppermute | solution.py:241

commit v3 on v2

--- a/solution.py
+++ b/solution.py
@@ -40,11 +40,11 @@
 
 def cost(products, slabs, tokens, dim):
     pairs = slabs * tokens * tokens
-    return pl.CostEstimate(flops=8 * products * pairs * dim, bytes_accessed=slabs * 4 * tokens * dim, transcendentals=pairs)
+    return pl.CostEstimate(flops=products * pairs * dim, bytes_accessed=slabs * tokens * dim, transcendentals=0)
 
 
 def prepare_kernel(key_scales, value_scales, slots, queries, key_codes, value_codes, grad_out, kv, qg,
-                   scale_mem, slot_mem, codes, packed, sems):
+                   scale_mem, slot_mem, codes, sems):
     blocks = slots.shape[1]
     size = queries.shape[0] // blocks
     loads = [
@@ -53,8 +53,8 @@
         pltpu.make_async_copy(slots.at[0], slot_mem, sems.at[2]),
         pltpu.make_async_copy(key_codes, codes.at[0], sems.at[3]),
         pltpu.make_async_copy(value_codes, codes.at[1], sems.at[4]),
-        pltpu.make_async_copy(queries, packed.at[2], sems.at[5]),
-        pltpu.make_async_copy(grad_out, packed.at[3], sems.at[6]),
+        pltpu.make_async_copy(queries, qg.at[0], sems.at[5]),
+        pltpu.make_async_copy(grad_out, qg.at[1], sems.at[6]),
     ]
     for load in loads:
         load.start()
@@ -64,15 +64,9 @@
         rows = slice(block * size, (block + 1) * size)
         slot = slot_mem[block]
         for part in range(2):
-            packed[part, rows] = (codes[part, rows].astype(F32) * scale_mem[part, slot]).astype(BF16)
-    stores = [pltpu.make_async_copy(packed.at[0:2], kv, sems.at[7])]
-    stores[0].start()
+            kv[part, rows] = (codes[part, rows].astype(F32) * scale_mem[part, slot]).astype(BF16)
     for load in loads[5:]:
         load.wait()
-    stores.append(pltpu.make_async_copy(packed.at[2:4], qg, sems.at[8]))
-    stores[1].start()
-    for store in stores:
-        store.wait()
 
 
 def prepare(queries, key_codes, value_codes, key_scales, value_scales, slots, grad_out):
@@ -81,14 +75,13 @@
     return pl.pallas_call(
         prepare_kernel,
         in_specs=[anywhere] * 7,
-        out_specs=[anywhere] * 2,
+        out_specs=[pl.BlockSpec(memory_space=pltpu.VMEM)] * 2,
         out_shape=[jax.ShapeDtypeStruct((n,) + queries.shape, BF16) for n in (2, 2)],
         scratch_shapes=[
             pltpu.SMEM((2, blocks), F32),
             pltpu.SMEM((blocks,), jnp.int32),
             pltpu.VMEM((2,) + queries.shape, BF16),
-            pltpu.VMEM((4,) + queries.shape, BF16),
-            pltpu.SemaphoreType.DMA((9,)),
+            pltpu.SemaphoreType.DMA((7,)),
         ],
         compiler_params=pltpu.CompilerParams(vmem_limit_bytes=60 * 2**20),
         name="prepare",
@@ -173,10 +166,10 @@
     )[0]
 
 
-def query_kernel(places, valid, qg, rows, *refs):
-    out, total = refs[-2:]
+def query_kernel(first, places, finish, valid, qg, rows, start, *refs):
+    total = refs[-1]
     tokens = qg.shape[1]
-    total[...] = jnp.zeros_like(total)
+    total[...] = start[...]
 
     def body(number, part):
         for tile in range(tokens // TILE_TOKENS):
@@ -189,23 +182,25 @@
             dscore = (attn_prob * (grad_prob - rows[1:2, cols])).astype(BF16)
             total[:, cols] += dot(keys, dscore, TN)
 
-    for_each_slab(valid, 0, places, refs, body)
-    out[...] = (total[...] * SCALE).T.astype(BF16)
-
-
-def query_side(valid, qg, window, rows):
+    for_each_slab(valid, first, places, refs, body)
+    if finish:
+        refs[-2][...] = (total[...] * SCALE).T.astype(BF16)
+
+
+def query_side(valid, first, qg, window, rows, start, finish):
     tokens, dim = qg.shape[1:]
     arrays, places = arrays_of(window)
+    outs = jax.ShapeDtypeStruct((tokens, dim), BF16) if finish else jax.ShapeDtypeStruct((dim, tokens), F32)
     return vmem_call(
-        functools.partial(query_kernel, places), "query_side", 3, len(window),
-        [jax.ShapeDtypeStruct((tokens, dim), BF16)], [pltpu.VMEM((dim, tokens), F32)], valid, qg, rows, *arrays,
+        functools.partial(query_kernel, first, places, finish), "query_side", 3, len(window),
+        [outs], [pltpu.VMEM((dim, tokens), F32)] if finish else [], valid, qg, rows, start, *arrays,
     )[0]
 
 
-def key_kernel(places, valid, kv, rows, *refs):
-    key_out, value_out, totals = refs[-3:]
+def key_kernel(first, places, finish, valid, kv, rows, start, *refs):
+    totals = refs[-1]
     tokens = kv.shape[1]
-    totals[...] = jnp.zeros_like(totals)
+    totals[...] = start[...]
 
     def body(number, part):
         for tile in range(tokens // TILE_TOKENS):
@@ -214,25 +209,28 @@
             queries = part(0, slice(low, high))
             grads = part(1, slice(low, high))
             scores = dot(kv[0, cols], queries, NT)
-            attn_prob = jnp.exp2(scores * SCALE2 - rows[number, 0:1, low:high])
+            attn_prob = jnp.exp2(scores * SCALE2 - rows[first + number, 0:1, low:high])
             grad_prob = dot(kv[1, cols], grads, NT)
-            dscore = (attn_prob * (grad_prob - rows[number, 1:2, low:high])).astype(BF16)
+            dscore = (attn_prob * (grad_prob - rows[first + number, 1:2, low:high])).astype(BF16)
             key_part = (dot(dscore, queries, NN) * SCALE).astype(BF16)
             value_part = dot(attn_prob.astype(BF16), grads, NN).astype(BF16)
             totals[0, cols] += key_part.astype(F32)
             totals[1, cols] += value_part.astype(F32)
 
-    for_each_slab(valid, 0, places, refs, body)
-    key_out[...] = totals[0].astype(BF16)
-    value_out[...] = totals[1].astype(BF16)
-
-
-def key_side(valid, kv, window, rows):
+    for_each_slab(valid, first, places, refs, body)
+    if finish:
+        refs[-3][...] = totals[0].astype(BF16)
+        refs[-2][...] = totals[1].astype(BF16)
+
+
+def key_side(valid, first, kv, window, rows, start, finish):
     tokens, dim = kv.shape[1:]
     arrays, places = arrays_of(window)
+    totals = (2, tokens, dim)
+    outs = [jax.ShapeDtypeStruct((tokens, dim), BF16)] * 2 if finish else [jax.ShapeDtypeStruct(totals, F32)]
     return vmem_call(
-        functools.partial(key_kernel, places), "key_side", 4, len(window),
-        [jax.ShapeDtypeStruct((tokens, dim), BF16)] * 2, [pltpu.VMEM((2, tokens, dim), F32)], valid, kv, rows, *arrays,
+        functools.partial(key_kernel, first, places, finish), "key_side", 4, len(window),
+        outs, [pltpu.VMEM(totals, F32)] if finish else [], valid, kv, rows, start, *arrays,
     )
 
 
@@ -254,19 +252,17 @@
     return 0 <= cross_of(row) < ROW_TILES
 
 
-def shift_frame(value, steps, cross_only=False):
+def frame_step(frame, phase):
+    return 1 - 2 * ((frame + phase) % 2)
+
+
+def swap_frames(value, phase, cross_only=False):
     count = lax.axis_size("tm")
-    pairs = [(s, s + steps * ROW_TILES) for s in range(count) if 0 <= s + steps * ROW_TILES < count]
+    pairs = [(s, s + frame_step(s // ROW_TILES, phase) * ROW_TILES) for s in range(count)]
+    pairs = [pair for pair in pairs if 0 <= pair[1] < count]
     if cross_only:
         pairs = [pair for pair in pairs if has_cross(pair[0] % ROW_TILES)]
     return lax.ppermute(value, "tm", pairs)
-
-
-def row_neighbours(rows):
-    trio = jnp.stack([rows, swap_mate(rows), swap_cross(rows)])
-    before = shift_frame(trio, 1)
-    after = shift_frame(trio, -1)
-    return jnp.stack([trio[0], trio[1], trio[2], before[0], after[0], before[1], after[1], before[2], after[2]])
 
 
 def per_device(queries, key_codes, value_codes, key_scales, value_scales, scale_slot, grad_out):
@@ -274,46 +270,52 @@
     frames = lax.axis_size("tm") // ROW_TILES
     frame = index // ROW_TILES
     row = index % ROW_TILES
-    before = (frame > 0).astype(jnp.int32)
-    after = (frame < frames - 1).astype(jnp.int32)
     cross = functools.reduce(lax.bitwise_or, [row == r for r in range(ROW_TILES) if has_cross(r)]).astype(jnp.int32)
+    others = [frame + frame_step(frame, phase) for phase in range(2)]
+    frame_a, frame_b = [((other >= 0) & (other < frames)).astype(jnp.int32) for other in others]
     one = jnp.ones((), jnp.int32)
-    valid = jnp.stack([one, one, cross, before, after, before, after, cross * before, cross * after])
+    valid = jnp.stack([one, one, cross, frame_a, frame_b, cross * frame_a, cross * frame_b, frame_a, frame_b])
 
     kv, qg = prepare(queries, key_codes, value_codes, key_scales, value_scales, scale_slot, grad_out)
-    kv_before = shift_frame(kv, 1)
-    kv_after = shift_frame(kv, -1)
+    kv_a = swap_frames(kv, 0)
+    kv_b = swap_frames(kv, 1)
     kv_cross = swap_cross(kv)
     kv_mate = swap_mate(kv)
     qg_cross = swap_cross(qg)
-    kv_cross_before = shift_frame(kv_cross, 1, True)
-    kv_cross_after = shift_frame(kv_cross, -1, True)
-    kv_mate_before = swap_mate(kv_before)
-    kv_mate_after = swap_mate(kv_after)
-
-    qg_pair, _, _ = lax.optimization_barrier((jnp.concatenate([qg, qg_cross]), kv_before, kv_after))
-    qg_before = shift_frame(qg_pair, 1)
-    qg_after = shift_frame(qg_pair, -1)
+    kv_cross_a = swap_frames(kv_cross, 0, True)
+    kv_cross_b = swap_frames(kv_cross, 1, True)
+    kv_mate_a = swap_mate(kv_a)
+    kv_mate_b = swap_mate(kv_b)
+
+    qg_pair, _, _ = lax.optimization_barrier((jnp.concatenate([qg, qg_cross]), kv_a, kv_b))
+    qg_a = swap_frames(qg_pair, 0)
+    qg_b = swap_frames(qg_pair, 1)
     qg_mate = swap_mate(qg)
-    qg_mate_before = swap_mate(qg_before)
-    qg_mate_after = swap_mate(qg_after)
-    qg_window = [(qg, 0), (qg_mate, 0), (qg_cross, 0), (qg_before, 0), (qg_after, 0),
-                 (qg_mate_before, 0), (qg_mate_after, 0), (qg_before, 2), (qg_after, 2)]
-
-    tokens = queries.shape[0]
+    qg_mate_a = swap_mate(qg_a)
+    qg_mate_b = swap_mate(qg_b)
+
+    tokens, dim = queries.shape
+    kv_near = [(kv, 0), (kv_mate, 0)]
+    kv_next = [(kv_cross, 0), (kv_a, 0), (kv_b, 0)]
+    kv_last = [(kv_cross_a, 0), (kv_cross_b, 0), (kv_mate_a, 0), (kv_mate_b, 0)]
     zeros = jnp.zeros((8, tokens), F32)
     running = jnp.stack([zeros + BIG_NEGATIVE, zeros, zeros])
-    groups = [
-        [(kv, 0), (kv_mate, 0)],
-        [(kv_cross, 0), (kv_before, 0), (kv_after, 0)],
-        [(kv_mate_before, 0), (kv_mate_after, 0), (kv_cross_before, 0), (kv_cross_after, 0)],
-    ]
-    running = stats(valid, 0, qg, groups[0], running, False)
-    running = stats(valid, 2, qg, groups[1], running, False)
-    rows = stats(valid, 5, qg, groups[2], running, True)
-    rows_all = row_neighbours(rows)
-    query_grad = query_side(valid, qg, groups[0] + groups[1] + groups[2], rows)
-    key_grad, value_grad = key_side(valid, kv, qg_window, rows_all)
+    running = stats(valid, 0, qg, kv_near, running, False)
+    running = stats(valid, 2, qg, kv_next, running, False)
+    rows = stats(valid, 5, qg, kv_last, running, True)
+
+    trio = jnp.stack([rows, swap_mate(rows), swap_cross(rows)])
+    query_total = query_side(valid, 0, qg, kv_near + kv_next, rows, jnp.zeros((dim, tokens), F32), False)
+    trio, query_total = lax.optimization_barrier((trio, query_total))
+    trio_a = swap_frames(trio, 0)
+    trio_b = swap_frames(trio, 1)
+    query_grad = query_side(valid, 5, qg, kv_last, rows, query_total, True)
+
+    rows_all = jnp.stack([trio[0], trio[1], trio[2], trio_a[0], trio_b[0], trio_a[2], trio_b[2], trio_a[1], trio_b[1]])
+    qg_first = [(qg, 0), (qg_mate, 0), (qg_cross, 0), (qg_a, 0), (qg_b, 0), (qg_a, 2), (qg_b, 2)]
+    qg_last = [(qg_mate_a, 0), (qg_mate_b, 0)]
+    (totals,) = key_side(valid, 0, kv, qg_first, rows_all, jnp.zeros((2, tokens, dim), F32), False)
+    key_grad, value_grad = key_side(valid, 7, kv, qg_last, rows_all, totals, True)
     return query_grad, key_grad, value_grad
 
 

time: 76.6 us -> 66.6 us (0.87)
  starting transfers between devices: 33.1 us -> 25.5 us
  waiting for transfers between devices: 4.01 us -> 1.55 us
  local copies, waits for them, and re-layouts: 2.15 us -> 0.23 us
  Pallas kernels: 35.6 us -> 36.9 us
  other arithmetic: 0.08 us -> 1.15 us
    ppermute x8, starting transfers between devices: 21.3 us -> 14.7 us  [swap_frames(): return lax.ppermute(value, 'tm', pairs)]
    ppermute x7, waiting for transfers between devices: 2.87 us -> 0.02 us  [swap_mate(): lax.ppermute(value, 'tm', [(source, source ^ 1) for source in range(count)])]
    unnamed x16 -> x12, local copies, waits for them, and re-layouts: 2.05 us -> 0.06 us
    pallas_call x5 -> x7, Pallas kernels: 33.5 us -> 34.7 us  [vmem_call(): pl.pallas_call(kernel, in_specs=[pl.BlockSpec(memory_space=pltpu.SMEM)] +...]
    ppermute x3, starting transfers between devices: 10.5 us -> 9.43 us  [swap_cross(): lax.ppermute(value, 'tm', [(s, cross_of(s)) for s in range(count) if has_...]
    concatenate x1, other arithmetic: 0.07 us -> 1.14 us  [per_device(): jnp.concatenate([qg, qg_cross])]
    ppermute x3, waiting for transfers between devices: 0.01 us -> 1.06 us  [swap_cross(): lax.ppermute(value, 'tm', [(s, cross_of(s)) for s in range(count) if has_...]
  transfers between devices with their start and end apart: 18 -> 18, of which waited for: 3 -> 2; matrix products, arithmetic and copies ran while one was open for 0% -> 2% of each run, Pallas kernels for 26% -> 46%
where the time goes in v3:
time: 66.6 us; the launch traced here: 66.3 us
  Pallas kernels  36.9 us (55%)
  starting transfers between devices  25.5 us (38%)
  waiting for transfers between devices  1.55 us (2%)
  other arithmetic  1.15 us (2%)
  between operations  0.95 us (1%)
    pallas_call x7, Pallas kernels, vmem_call(): pl.pallas_call(kernel, in_specs=[pl.BlockSpec(memory_space=pltpu.SMEM)] +...  34.7 us
    ppermute x8, starting transfers between devices, swap_frames(): return lax.ppermute(value, 'tm', pairs)  14.7 us
    ppermute x3, starting transfers between devices, swap_cross(): lax.ppermute(value, 'tm', [(s, cross_of(s)) for s in range(count) if has_...  9.43 us
    pallas_call x1, Pallas kernels, prepare(): pl.pallas_call(prepare_kernel, in_specs=[anywhere] * 7, out_specs=[pl.Blo...  2.17 us
    ppermute x7, starting transfers between devices, swap_mate(): lax.ppermute(value, 'tm', [(source, source ^ 1) for source in range(count)])  1.35 us
  transfers between devices with their start and end apart: 18, of which 2 were waited for; matrix products, arithmetic and copies ran while one was open for 2% of the time, Pallas kernels for 46%

profile of v3, /device:TPU:11, one launch (start us, length us, event | category | flops | bytes accessed | tf_op | source)
XLA Modules:
  0.0 66.3 jit_solution(16490768350876891343)
XLA Ops:
  0.6 2.2 %prepare.1 = (bf16[2,768,128]{2,1,0:T(8,128)(2,1)}, bf16[2,768,128]{2,1,0:T(8,128)(2,1)}) custom-call(f32[6]{0:T(128)} %key_scales.1, f32[6]{0:T(128)} %value_scales.1, s32[1,6]{1,0:T(1,128)} %slots.1, bf16[768,128]{1,0:T(8,128)(2,1)} %queries.1, bf16[768,128]{1,0:T(8,128)(2,1)} %key_codes.1, bf16[768,128]{1,0:T(8,128)(2,1)} %value_codes.1, ...), custom_call_target="tpu_custom_call" | custom-call | tf_op jit(solution)/shard_map/prepare/pallas_call | solution.py:75
  2.8 3.7 %collective-permute-start.1 = (bf16[2,768,128]{2,1,0:T(8,128)(2,1)}, bf16[2,768,128]{2,1,0:T(8,128)(2,1)S(1)}, u32[]{:S(2)}, u32[]{:S(2)}) collective-permute-start(bf16[2,768,128]{2,1,0:T(8,128)(2,1)} %get-tuple-element.11.refs_0_.kv), channel_id=1, source_target_pairs={{1,2},{2,1},{5,6},{6,5},{9,10},{10,9},{13,14},{14,13},{17,18},{18,... | collective-permute-start | bytes 1179656 | tf_op jit(solution)/shard_map/ppermute | solution.py:244
  6.5 0.2 collective-permute-start.2
  6.8 4.3 %collective-permute-start.3 = (bf16[2,768,128]{2,1,0:T(8,128)(2,1)}, bf16[2,768,128]{2,1,0:T(8,128)(2,1)S(1)}, u32[]{:S(2)}, u32[]{:S(2)}) collective-permute-start(bf16[2,768,128]{2,1,0:T(8,128)(2,1)} %get-tuple-element.11.refs_0_.kv), channel_id=1, source_target_pairs={{4,8},{5,9},{6,10},{7,11},{8,4},{9,5},{10,6},{11,7},{20,24},{21,25... | collective-permute-start | bytes 1179656 | tf_op jit(solution)/shard_map/ppermute | solution.py:265
  11.1 2.5 %collective-permute-start.13 = (bf16[2,768,128]{2,1,0:T(8,128)(2,1)}, bf16[2,768,128]{2,1,0:T(8,128)(2,1)S(1)}, u32[]{:S(2)}, u32[]{:S(2)}) collective-permute-start(bf16[2,768,128]{2,1,0:T(8,128)(2,1)} %get-tuple-element.10.qg.refs_0_), channel_id=1, source_target_pairs={{1,2},{2,1},{5,6},{6,5},{9,10},{10,9},{13,14},{14,13},{17,18},{18,... | collective-permute-start | bytes 1179656 | tf_op jit(solution)/shard_map/ppermute | solution.py:244
  13.6 0.1 collective-permute-start
  13.7 0.0 collective-permute-done.1.refs_0_.refs_2_
  13.7 1.9 %collective-permute-start.4 = (bf16[2,768,128]{2,1,0:T(8,128)(2,1)S(1)}, bf16[2,768,128]{2,1,0:T(8,128)(2,1)S(1)}, u32[]{:S(2)}, u32[]{:S(2)}) collective-permute-start(bf16[2,768,128]{2,1,0:T(8,128)(2,1)S(1)} %collective-permute-done.1.refs_0_.refs_2_), channel_id=1, source_target_pairs={{1,5},{2,6},{5,1},{6,2},{9,13},{10,14},{13,9},{14,10},{17,21},{18,... | collective-permute-start | bytes 1179656 | tf_op jit(solution)/shard_map/ppermute | solution.py:265
  15.6 0.5 collective-permute-done.2.refs_1_.refs_3_
  16.1 3.2 %collective-permute-start.5 = (bf16[2,768,128]{2,1,0:T(8,128)(2,1)S(1)}, bf16[2,768,128]{2,1,0:T(8,128)(2,1)S(1)}, u32[]{:S(2)}, u32[]{:S(2)}) collective-permute-start(bf16[2,768,128]{2,1,0:T(8,128)(2,1)S(1)} %collective-permute-done.1.refs_0_.refs_2_), channel_id=1, source_target_pairs={{5,9},{6,10},{9,5},{10,6},{21,25},{22,26},{25,21},{26,22}} | collective-permute-start | bytes 1179656 | tf_op jit(solution)/shard_map/ppermute | solution.py:265
  19.3 0.1 collective-permute-start.6
  19.3 1.1 %collective-permute-done.13.refs_2_ = bf16[2,768,128]{2,1,0:T(8,128)(2,1)S(1)} collective-permute-done((bf16[2,768,128]{2,1,0:T(8,128)(2,1)}, bf16[2,768,128]{2,1,0:T(8,128)(2,1)S(1)}, u32[]{:S(2)}, u32[]{:S(2)}) %collective-permute-start.13) | collective-permute-done | bytes 393248 | tf_op jit(solution)/shard_map/ppermute | solution.py:244
  20.4 0.1 stack.48.valid
  20.5 0.0 copy-start.2
  20.5 1.1 %pad_maximum_fusion = bf16[4,768,128]{2,1,0:T(8,128)(2,1)S(1)} fusion(bf16[2,768,128]{2,1,0:T(8,128)(2,1)S(1)} %collective-permute-done.13.refs_2_, bf16[2,768,128]{2,1,0:T(8,128)(2,1)} %get-tuple-element.10.qg.refs_0_), kind=kLoop, calls=%fused_computation | loop fusion | flops 393216 | bytes 1572864 | tf_op jit(solution)/shard_map/concatenate | solution.py:290
  21.7 0.6 collective-permute-start.12
  22.3 2.0 %row_stats.3.start = f32[3,8,768]{2,1,0:T(8,128)S(1)} custom-call(s32[9]{0:T(128)S(1)} %stack.48.valid, bf16[2,768,128]{2,1,0:T(8,128)(2,1)S(1)} %copy-done, f32[3,8,768]{2,1,0:T(8,128)S(1)} %copy-done.2, bf16[2,768,128]{2,1,0:T(8,128)(2,1)S(1)} %copy-done.1, bf16[2,768,128]{2,1,0:T(8,128)(2,1)S(1)} %collective-permute-done.refs_1_), custom_call_target="tpu_custom_call" | custom-call | flops 301989888 | bytes 196608 | tf_op jit(solution)/shard_map/row_stats/pallas_call | solution.py:94
  24.3 2.8 %row_stats.4.start = f32[3,8,768]{2,1,0:T(8,128)S(1)} custom-call(s32[9]{0:T(128)S(1)} %stack.48.valid, bf16[2,768,128]{2,1,0:T(8,128)(2,1)S(1)} %copy-done, f32[3,8,768]{2,1,0:T(8,128)S(1)} %row_stats.3.start, bf16[2,768,128]{2,1,0:T(8,128)(2,1)S(1)} %collective-permute-done.1.refs_0_.refs_2_, ...), custom_call_target="tpu_custom_call" | custom-call | flops 452984832 | bytes 294912 | tf_op jit(solution)/shard_map/row_stats/pallas_call | solution.py:94
  27.1 0.1 collective-permute-start.14
  27.2 2.1 %collective-permute-start.15 = (bf16[4,768,128]{2,1,0:T(8,128)(2,1)S(1)}, bf16[4,768,128]{2,1,0:T(8,128)(2,1)S(1)}, u32[]{:S(2)}, u32[]{:S(2)}) collective-permute-start(bf16[4,768,128]{2,1,0:T(8,128)(2,1)S(1)} %pad_maximum_fusion), channel_id=1, source_target_pairs={{4,8},{5,9},{6,10},{7,11},{8,4},{9,5},{10,6},{11,7},{20,24},{21,25... | collective-permute-start | bytes 2359304 | tf_op jit(solution)/shard_map/ppermute | solution.py:265
  29.3 3.6 %row_stats.5.rows = f32[2,768]{1,0:T(2,128)S(1)} custom-call(s32[9]{0:T(128)S(1)} %stack.48.valid, bf16[2,768,128]{2,1,0:T(8,128)(2,1)S(1)} %copy-done, f32[3,8,768]{2,1,0:T(8,128)S(1)} %row_stats.4.start, bf16[2,768,128]{2,1,0:T(8,128)(2,1)S(1)} %collective-permute-done.4.refs_0_, bf16[2,768,128]{2,1,0:T(8,128)(2,1)S(1)} %collective-permute-done.5.refs_1_, ...), custom_call_target="tpu_custom_call" | custom-call | flops 603979776 | bytes 393216 | tf_op jit(solution)/shard_map/row_stats/pallas_call | solution.py:94
  32.8 3.2 %collective-permute-start.9 = (f32[2,768]{1,0:T(2,128)S(1)}, f32[2,768]{1,0:T(2,128)S(1)}, u32[]{:S(2)}, u32[]{:S(2)}) collective-permute-start(f32[2,768]{1,0:T(2,128)S(1)} %row_stats.5.rows), channel_id=1, source_target_pairs={{1,2},{2,1},{5,6},{6,5},{9,10},{10,9},{13,14},{14,13},{17,18},{18,... | collective-permute-start | bytes 18440 | tf_op jit(solution)/shard_map/ppermute | solution.py:244
  36.1 0.1 collective-permute-start.8
  36.2 6.3 %query_side.2.start = f32[128,768]{1,0:T(8,128)S(1)} custom-call(s32[9]{0:T(128)S(1)} %stack.48.valid, bf16[2,768,128]{2,1,0:T(8,128)(2,1)S(1)} %copy-done, f32[2,768]{1,0:T(2,128)S(1)} %row_stats.5.rows, f32[128,768]{1,0:T(8,128)S(1)} %broadcast_in_dim.6.start, bf16[2,768,128]{2,1,0:T(8,128)(2,1)S(1)} %copy-done.1, ...), custom_call_target="tpu_custom_call" | custom-call | flops 1132462080 | bytes 491520 | tf_op jit(solution)/shard_map/query_side/pallas_call | solution.py:94
  42.6 0.1 collective-permute-start.10
  42.7 2.9 %collective-permute-start.11 = (f32[3,2,768]{2,1,0:T(2,128)S(1)}, f32[3,2,768]{2,1,0:T(2,128)S(1)}, u32[]{:S(2)}, u32[]{:S(2)}) collective-permute-start(f32[3,2,768]{2,1,0:T(2,128)S(1)} %pad_maximum_fusion.1), channel_id=1, source_target_pairs={{4,8},{5,9},{6,10},{7,11},{8,4},{9,5},{10,6},{11,7},{20,24},{21,25... | collective-permute-start | bytes 55304 | tf_op jit(solution)/shard_map/ppermute | solution.py:265
  45.5 5.9 %query_side.3 = bf16[768,128]{1,0:T(8,128)(2,1)} custom-call(s32[9]{0:T(128)S(1)} %stack.48.valid, bf16[2,768,128]{2,1,0:T(8,128)(2,1)S(1)} %copy-done, f32[2,768]{1,0:T(2,128)S(1)} %row_stats.5.rows, f32[128,768]{1,0:T(8,128)S(1)} %query_side.2.start, bf16[2,768,128]{2,1,0:T(8,128)(2,1)S(1)} %collective-permute-done.4.refs_0_, ...), custom_call_target="tpu_custom_call" | custom-call | flops 905969664 | bytes 393216 | tf_op jit(solution)/shard_map/query_side/pallas_call | solution.py:94
  51.5 0.1 collective-permute-start.16
  51.6 0.5 collective-permute-start.17
  52.1 0.1 broadcast_in_dim.7.start
  52.1 10.1 %key_side.2.start = f32[2,768,128]{2,1,0:T(8,128)S(1)} custom-call(s32[9]{0:T(128)S(1)} %stack.48.valid, bf16[2,768,128]{2,1,0:T(8,128)(2,1)S(1)} %copy-done.1, f32[9,2,768]{2,1,0:T(2,128)S(1)} %constant_dynamic-update-slice_fusion.rows, f32[2,768,128]{2,1,0:T(8,128)S(1)} %broadcast_in_dim.7.start, bf16[2,768,128]{2,1,0:T(8,128)(2,1)S(1)} %copy-done, ...), custom_call_target="tpu_custom_call" | custom-call | flops 2113929216 | bytes 688128 | tf_op jit(solution)/shard_map/key_side/pallas_call | solution.py:94
  62.3 4.0 %key_side.3 = (bf16[768,128]{1,0:T(8,128)(2,1)}, bf16[768,128]{1,0:T(8,128)(2,1)}) custom-call(s32[9]{0:T(128)S(1)} %stack.48.valid, bf16[2,768,128]{2,1,0:T(8,128)(2,1)S(1)} %copy-done.1, f32[9,2,768]{2,1,0:T(2,128)S(1)} %constant_dynamic-update-slice_fusion.rows, f32[2,768,128]{2,1,0:T(8,128)S(1)} %key_side.2.start, ...), custom_call_target="tpu_custom_call" | custom-call | flops 603979776 | bytes 196608 | tf_op jit(solution)/shard_map/key_side/pallas_call | solution.py:94
  (31 shorter events, 0.1 us)
Async XLA Ops:
  2.8 10.8 %collective-permute-start.1 = (bf16[2,768,128]{2,1,0:T(8,128)(2,1)}, bf16[2,768,128]{2,1,0:T(8,128)(2,1)S(1)}, u32[]{:S(2)}, u32[]{:S(2)}) collective-permute-start(bf16[2,768,128]{2,1,0:T(8,128)(2,1)} %get-tuple-element.11.refs_0_.kv), channel_id=1, source_target_pairs={{1,2},{2,1},{5,6},{6,5},{9,10},{10,9},{13,14},{14,13},{17,18},{18,... | collective-permute-start | bytes 1179656 | tf_op jit(solution)/shard_map/ppermute | solution.py:244
  6.5 9.5 %collective-permute-start.2 = (bf16[2,768,128]{2,1,0:T(8,128)(2,1)}, bf16[2,768,128]{2,1,0:T(8,128)(2,1)S(1)}, u32[]{:S(2)}, u32[]{:S(2)}) collective-permute-start(bf16[2,768,128]{2,1,0:T(8,128)(2,1)} %get-tuple-element.11.refs_0_.kv), channel_id=1, source_target_pairs={{0,4},{1,5},{2,6},{3,7},{4,0},{5,1},{6,2},{7,3},{8,12},{9,13},{10,... | collective-permute-start | bytes 1179656 | tf_op jit(solution)/shard_map/ppermute | solution.py:265
  6.8 12.5 %collective-permute-start.3 = (bf16[2,768,128]{2,1,0:T(8,128)(2,1)}, bf16[2,768,128]{2,1,0:T(8,128)(2,1)S(1)}, u32[]{:S(2)}, u32[]{:S(2)}) collective-permute-start(bf16[2,768,128]{2,1,0:T(8,128)(2,1)} %get-tuple-element.11.refs_0_.kv), channel_id=1, source_target_pairs={{4,8},{5,9},{6,10},{7,11},{8,4},{9,5},{10,6},{11,7},{20,24},{21,25... | collective-permute-start | bytes 1179656 | tf_op jit(solution)/shard_map/ppermute | solution.py:265
  11.1 9.3 %collective-permute-start.13 = (bf16[2,768,128]{2,1,0:T(8,128)(2,1)}, bf16[2,768,128]{2,1,0:T(8,128)(2,1)S(1)}, u32[]{:S(2)}, u32[]{:S(2)}) collective-permute-start(bf16[2,768,128]{2,1,0:T(8,128)(2,1)} %get-tuple-element.10.qg.refs_0_), channel_id=1, source_target_pairs={{1,2},{2,1},{5,6},{6,5},{9,10},{10,9},{13,14},{14,13},{17,18},{18,... | collective-permute-start | bytes 1179656 | tf_op jit(solution)/shard_map/ppermute | solution.py:244
  13.6 8.1 %collective-permute-start = (bf16[2,768,128]{2,1,0:T(8,128)(2,1)}, bf16[2,768,128]{2,1,0:T(8,128)(2,1)S(1)}, u32[]{:S(2)}, u32[]{:S(2)}) collective-permute-start(bf16[2,768,128]{2,1,0:T(8,128)(2,1)} %get-tuple-element.11.refs_0_.kv), channel_id=1, source_target_pairs={{0,1},{1,0},{2,3},{3,2},{4,5},{5,4},{6,7},{7,6},{8,9},{9,8},{10,11... | collective-permute-start | bytes 1179656 | tf_op jit(solution)/shard_map/ppermute | solution.py:239
  13.7 13.4 %collective-permute-start.4 = (bf16[2,768,128]{2,1,0:T(8,128)(2,1)S(1)}, bf16[2,768,128]{2,1,0:T(8,128)(2,1)S(1)}, u32[]{:S(2)}, u32[]{:S(2)}) collective-permute-start(bf16[2,768,128]{2,1,0:T(8,128)(2,1)S(1)} %collective-permute-done.1.refs_0_.refs_2_), channel_id=1, source_target_pairs={{1,5},{2,6},{5,1},{6,2},{9,13},{10,14},{13,9},{14,10},{17,21},{18,... | collective-permute-start | bytes 1179656 | tf_op jit(solution)/shard_map/ppermute | solution.py:265
  16.1 11.1 %collective-permute-start.5 = (bf16[2,768,128]{2,1,0:T(8,128)(2,1)S(1)}, bf16[2,768,128]{2,1,0:T(8,128)(2,1)S(1)}, u32[]{:S(2)}, u32[]{:S(2)}) collective-permute-start(bf16[2,768,128]{2,1,0:T(8,128)(2,1)S(1)} %collective-permute-done.1.refs_0_.refs_2_), channel_id=1, source_target_pairs={{5,9},{6,10},{9,5},{10,6},{21,25},{22,26},{25,21},{26,22}} | collective-permute-start | bytes 1179656 | tf_op jit(solution)/shard_map/ppermute | solution.py:265
  19.3 10.0 %collective-permute-start.6 = (bf16[2,768,128]{2,1,0:T(8,128)(2,1)S(1)}, bf16[2,768,128]{2,1,0:T(8,128)(2,1)S(1)}, u32[]{:S(2)}, u32[]{:S(2)}) collective-permute-start(bf16[2,768,128]{2,1,0:T(8,128)(2,1)S(1)} %collective-permute-done.2.refs_1_.refs_3_), channel_id=1, source_target_pairs={{0,1},{1,0},{2,3},{3,2},{4,5},{5,4},{6,7},{7,6},{8,9},{9,8},{10,11... | collective-permute-start | bytes 1179656 | tf_op jit(solution)/shard_map/ppermute | solution.py:239
  20.4 8.8 %collective-permute-start.7 = (bf16[2,768,128]{2,1,0:T(8,128)(2,1)S(1)}, bf16[2,768,128]{2,1,0:T(8,128)(2,1)S(1)}, u32[]{:S(2)}, u32[]{:S(2)}) collective-permute-start(bf16[2,768,128]{2,1,0:T(8,128)(2,1)S(1)} %collective-permute-done.3.refs_2_.refs_4_), channel_id=1, source_target_pairs={{0,1},{1,0},{2,3},{3,2},{4,5},{5,4},{6,7},{7,6},{8,9},{9,8},{10,11... | collective-permute-start | bytes 1179656 | tf_op jit(solution)/shard_map/ppermute | solution.py:239
  20.5 1.2 %copy-start = (bf16[2,768,128]{2,1,0:T(8,128)(2,1)S(1)}, bf16[2,768,128]{2,1,0:T(8,128)(2,1)}, u32[]{:S(2)}) copy-start(bf16[2,768,128]{2,1,0:T(8,128)(2,1)} %get-tuple-element.10.qg.refs_0_) | copy-start | bytes 1179652
  20.5 1.8 %copy-start.1 = (bf16[2,768,128]{2,1,0:T(8,128)(2,1)S(1)}, bf16[2,768,128]{2,1,0:T(8,128)(2,1)}, u32[]{:S(2)}) copy-start(bf16[2,768,128]{2,1,0:T(8,128)(2,1)} %get-tuple-element.11.refs_0_.kv) | copy-start | bytes 1179652
  20.5 1.8 %copy-start.2 = (f32[3,8,768]{2,1,0:T(8,128)S(1)}, f32[3,8,768]{2,1,0:T(8,128)}, u32[]{:S(2)}) copy-start(f32[3,8,768]{2,1,0:T(8,128)} %constant.50.clone.1.start) | copy-start | bytes 221188
  21.7 30.4 %collective-permute-start.12 = (bf16[2,768,128]{2,1,0:T(8,128)(2,1)S(1)}, bf16[2,768,128]{2,1,0:T(8,128)(2,1)S(1)}, u32[]{:S(2)}, u32[]{:S(2)}) collective-permute-start(bf16[2,768,128]{2,1,0:T(8,128)(2,1)S(1)} %copy-done), channel_id=1, source_target_pairs={{0,1},{1,0},{2,3},{3,2},{4,5},{5,4},{6,7},{7,6},{8,9},{9,8},{10,11... | collective-permute-start | bytes 1179656 | tf_op jit(solution)/shard_map/ppermute | solution.py:239
  27.1 24.4 %collective-permute-start.14 = (bf16[4,768,128]{2,1,0:T(8,128)(2,1)S(1)}, bf16[4,768,128]{2,1,0:T(8,128)(2,1)S(1)}, u32[]{:S(2)}, u32[]{:S(2)}) collective-permute-start(bf16[4,768,128]{2,1,0:T(8,128)(2,1)S(1)} %pad_maximum_fusion), channel_id=1, source_target_pairs={{0,4},{1,5},{2,6},{3,7},{4,0},{5,1},{6,2},{7,3},{8,12},{9,13},{10,... | collective-permute-start | bytes 2359304 | tf_op jit(solution)/shard_map/ppermute | solution.py:265
  27.2 24.4 %collective-permute-start.15 = (bf16[4,768,128]{2,1,0:T(8,128)(2,1)S(1)}, bf16[4,768,128]{2,1,0:T(8,128)(2,1)S(1)}, u32[]{:S(2)}, u32[]{:S(2)}) collective-permute-start(bf16[4,768,128]{2,1,0:T(8,128)(2,1)S(1)} %pad_maximum_fusion), channel_id=1, source_target_pairs={{4,8},{5,9},{6,10},{7,11},{8,4},{9,5},{10,6},{11,7},{20,24},{21,25... | collective-permute-start | bytes 2359304 | tf_op jit(solution)/shard_map/ppermute | solution.py:265
  32.8 9.7 %collective-permute-start.9 = (f32[2,768]{1,0:T(2,128)S(1)}, f32[2,768]{1,0:T(2,128)S(1)}, u32[]{:S(2)}, u32[]{:S(2)}) collective-permute-start(f32[2,768]{1,0:T(2,128)S(1)} %row_stats.5.rows), channel_id=1, source_target_pairs={{1,2},{2,1},{5,6},{6,5},{9,10},{10,9},{13,14},{14,13},{17,18},{18,... | collective-permute-start | bytes 18440 | tf_op jit(solution)/shard_map/ppermute | solution.py:244
  36.1 6.5 %collective-permute-start.8 = (f32[2,768]{1,0:T(2,128)S(1)}, f32[2,768]{1,0:T(2,128)S(1)}, u32[]{:S(2)}, u32[]{:S(2)}) collective-permute-start(f32[2,768]{1,0:T(2,128)S(1)} %row_stats.5.rows), channel_id=1, source_target_pairs={{0,1},{1,0},{2,3},{3,2},{4,5},{5,4},{6,7},{7,6},{8,9},{9,8},{10,11... | collective-permute-start | bytes 18440 | tf_op jit(solution)/shard_map/ppermute | solution.py:239
  42.6 8.8 %collective-permute-start.10 = (f32[3,2,768]{2,1,0:T(2,128)S(1)}, f32[3,2,768]{2,1,0:T(2,128)S(1)}, u32[]{:S(2)}, u32[]{:S(2)}) collective-permute-start(f32[3,2,768]{2,1,0:T(2,128)S(1)} %pad_maximum_fusion.1), channel_id=1, source_target_pairs={{0,4},{1,5},{2,6},{3,7},{4,0},{5,1},{6,2},{7,3},{8,12},{9,13},{10,... | collective-permute-start | bytes 55304 | tf_op jit(solution)/shard_map/ppermute | solution.py:265
  42.7 8.8 %collective-permute-start.11 = (f32[3,2,768]{2,1,0:T(2,128)S(1)}, f32[3,2,768]{2,1,0:T(2,128)S(1)}, u32[]{:S(2)}, u32[]{:S(2)}) collective-permute-start(f32[3,2,768]{2,1,0:T(2,128)S(1)} %pad_maximum_fusion.1), channel_id=1, source_target_pairs={{4,8},{5,9},{6,10},{7,11},{8,4},{9,5},{10,6},{11,7},{20,24},{21,25... | collective-permute-start | bytes 55304 | tf_op jit(solution)/shard_map/ppermute | solution.py:265
  51.5 10.8 %collective-permute-start.16 = (bf16[4,768,128]{2,1,0:T(8,128)(2,1)S(1)}, bf16[4,768,128]{2,1,0:T(8,128)(2,1)S(1)}, u32[]{:S(2)}, u32[]{:S(2)}) collective-permute-start(bf16[4,768,128]{2,1,0:T(8,128)(2,1)S(1)} %collective-permute-done.14.refs_3_), channel_id=1, source_target_pairs={{0,1},{1,0},{2,3},{3,2},{4,5},{5,4},{6,7},{7,6},{8,9},{9,8},{10,11... | collective-permute-start | bytes 2359304 | tf_op jit(solution)/shard_map/ppermute | solution.py:239
  51.6 10.7 %collective-permute-start.17 = (bf16[4,768,128]{2,1,0:T(8,128)(2,1)S(1)}, bf16[4,768,128]{2,1,0:T(8,128)(2,1)S(1)}, u32[]{:S(2)}, u32[]{:S(2)}) collective-permute-start(bf16[4,768,128]{2,1,0:T(8,128)(2,1)S(1)} %collective-permute-done.15.refs_4_), channel_id=1, source_target_pairs={{0,1},{1,0},{2,3},{3,2},{4,5},{5,4},{6,7},{7,6},{8,9},{9,8},{10,11... | collective-permute-start | bytes 2359304 | tf_op jit(solution)/shard_map/ppermute | solution.py:239

commit v4 on v3

v4 whole, which is shorter than its diff:
```python
import functools
import math

import jax
import jax.numpy as jnp
from jax import lax
from jax.experimental import pallas as pl
from jax.experimental.pallas import tpu as pltpu
from jax.sharding import PartitionSpec as P

HEAD_DIM = 128
TILE_TOKENS = 256
ROW_TILES = 4
CHIP_ROWS = 2

SCALE = HEAD_DIM ** (-0.5)
SCALE2 = SCALE * math.log2(math.e)
BIG_NEGATIVE = -1e30
STATS_KEYS = 128
VMEM_LIMIT = 8 * 2**20

F32 = jnp.float32
BF16 = jnp.bfloat16
NT = (((1,), (1,)), ((), ()))
TN = (((0,), (0,)), ((), ()))
NN = (((1,), (0,)), ((), ()))


def dot(left, right, dims):
    return lax.dot_general(left, right, dims, preferred_element_type=F32)


def near(tile, tokens):
    return max(0, tile - 1) * TILE_TOKENS, min(tokens, (tile + 2) * TILE_TOKENS)


def params():
    return pltpu.CompilerParams(vmem_limit_bytes=VMEM_LIMIT)


def cost(products, slabs, tokens, dim):
    pairs = slabs * tokens * tokens
    return pl.CostEstimate(flops=products * pairs * dim, bytes_accessed=slabs * tokens * dim, transcendentals=0)


def prepare(queries, key_codes, value_codes, key_scales, value_scales, scale_slot, grad_out):
    tokens, dim = queries.shape
    blocks = scale_slot.shape[1]
    picker = scale_slot[0][:, None] == jnp.arange(blocks, dtype=jnp.int32)[None, :]

    def scaled(codes, scales):
        picked = jnp.sum(jnp.where(picker, scales[None, :], 0.0), axis=1)
        blocked = codes.astype(F32).reshape(blocks, tokens // blocks, dim)
        return (blocked * picked[:, None, None]).astype(BF16).reshape(tokens, dim)

    kv = jnp.stack([scaled(key_codes, key_scales), scaled(value_codes, value_scales)])
    return kv, jnp.stack([queries, grad_out])


def vmem_call(kernel, name, products, slabs, outs, scratch, *operands):
    tokens, dim = operands[-1].shape[1:]
    vmem = pl.BlockSpec(memory_space=pltpu.VMEM)
    return pl.pallas_call(
        kernel,
        in_specs=[pl.BlockSpec(memory_space=pltpu.SMEM)] + [vmem] * (len(operands) - 1),
        out_specs=[vmem] * len(outs),
        out_shape=outs,
        scratch_shapes=scratch,
        cost_estimate=cost(products, slabs, tokens, dim),
        compiler_params=params(),
        name=name,
    )(*operands)


def arrays_of(window):
    arrays = []
    for array, _ in window:
        if not any(array is other for other in arrays):
            arrays.append(array)
    places = [([array is other for other in arrays].index(True), offset) for array, offset in window]
    return arrays, places


def for_each_slab(valid, first, places, refs, body):
    for number, (place, offset) in enumerate(places):

        @pl.when(valid[first + number] > 0)
        def _(ref=refs[place], offset=offset, number=number):
            body(number, lambda part, rows: ref[offset + part, rows])


def tile_pairs(tokens):
    tiles = tokens // TILE_TOKENS
    return [(tile, key) for tile in range(tiles) for key in range(max(0, tile - 1), min(tiles, tile + 2))]


def stats_kernel(first, places, finish, valid, qg, *refs):
    tokens = qg.shape[1]
    running, kept = refs[-1], refs[-2]
    if first == 0:
        running[0] = jnp.full(running.shape[1:], BIG_NEGATIVE, F32)
        running[1:] = jnp.zeros((2,) + running.shape[1:], F32)
    else:
        running[...] = refs[0][...]
        refs = refs[1:]
    shape = (STATS_KEYS // 8, 8, TILE_TOKENS)

    def body(number, part):
        for tile in range(tokens // TILE_TOKENS):
            cols = slice(tile * TILE_TOKENS, (tile + 1) * TILE_TOKENS)
            top, total, weighted = running[0, :, cols], running[1, :, cols], running[2, :, cols]
            for place, pair in enumerate(tile_pairs(tokens)):
                if pair[0] != tile:
                    continue
                for key in range(0, TILE_TOKENS, STATS_KEYS):
                    inner = slice(key, key + STATS_KEYS)
                    keys = slice(pair[1] * TILE_TOKENS + key, pair[1] * TILE_TOKENS + key + STATS_KEYS)
                    scores = dot(part(0, keys), qg[0, cols], NT) * SCALE2
                    grad_prob = dot(part(1, keys), qg[1, cols], NT)
                    kept[number, place, 0, inner] = scores
                    kept[number, place, 1, inner] = grad_prob
                    scores = scores.reshape(shape)
                    new_top = jnp.maximum(top, jnp.max(scores, axis=0))
                    unscaled = jnp.exp2(scores - new_top[None])
                    rescale = jnp.exp2(top - new_top)
                    top = new_top
                    total = total * rescale + jnp.sum(unscaled, axis=0)
                    weighted = weighted * rescale + jnp.sum(unscaled * grad_prob.reshape(shape), axis=0)
            running[0, :, cols], running[1, :, cols], running[2, :, cols] = top, total, weighted

    for_each_slab(valid, first, places, refs, body)
    if finish:
        final = refs[-3]
        top = running[0]
        row_top = jnp.max(top, axis=0, keepdims=True)
        rescale = jnp.exp2(top - row_top)
        total = jnp.sum(running[1] * rescale, axis=0, keepdims=True)
        weighted = jnp.sum(running[2] * rescale, axis=0, keepdims=True)
        final[0:1] = row_top + jnp.log2(total)
        final[1:2] = weighted / total


def stats(valid, first, qg, window, start, finish):
    tokens = qg.shape[1]
    arrays, places = arrays_of(window)
    running = (3, 8, tokens)
    kept = jax.ShapeDtypeStruct((len(window), len(tile_pairs(tokens)), 2, TILE_TOKENS, TILE_TOKENS), F32)
    result = jax.ShapeDtypeStruct((2, tokens) if finish else running, F32)
    outs = vmem_call(
        functools.partial(stats_kernel, first, places, finish), "row_stats", 2, len(window),
        [result, kept] if finish else [kept, result], [pltpu.VMEM(running, F32)] if finish else [],
        valid, qg, *([] if first == 0 else [start]), *arrays,
    )
    return outs if finish else outs[::-1]


def query_kernel(places, groups, valid, rows, *refs):
    out, total = refs[-2:]
    tokens = rows.shape[1]
    total[...] = jnp.zeros_like(total)
    kept = [(ref, number) for ref in refs[:groups] for number in range(ref.shape[0])]

    def body(number, part):
        scores, index = kept[number]
        for tile in range(tokens // TILE_TOKENS):
            cols = slice(tile * TILE_TOKENS, (tile + 1) * TILE_TOKENS)
            low, high = near(tile, tokens)
            dscores = []
            for place, pair in enumerate(tile_pairs(tokens)):
                if pair[0] == tile:
                    attn_prob = jnp.exp2(scores[index, place, 0] - rows[0:1, cols])
                    dscores.append((attn_prob * (scores[index, place, 1] - rows[1:2, cols])).astype(BF16))
            total[:, cols] += dot(part(0, slice(low, high)), jnp.concatenate(dscores), TN)

    for_each_slab(valid, 0, places, refs[groups:], body)
    out[...] = (total[...] * SCALE).T.astype(BF16)


def query_side(valid, window, kept, rows):
    tokens, dim = window[0][0].shape[1:]
    arrays, places = arrays_of(window)
    return vmem_call(
        functools.partial(query_kernel, places, len(kept)), "query_side", 1, len(window),
        [jax.ShapeDtypeStruct((tokens, dim), BF16)], [pltpu.VMEM((dim, tokens), F32)], valid, rows, *kept, *arrays,
    )[0]


def key_kernel(first, places, finish, valid, kv, rows, *refs):
    totals = refs[-1]
    tokens = kv.shape[1]
    if first == 0:
        totals[...] = jnp.zeros_like(totals)
    else:
        totals[...] = refs[0][...]
        refs = refs[1:]

    def body(number, part):
        for tile in range(tokens // TILE_TOKENS):
            cols = slice(tile * TILE_TOKENS, (tile + 1) * TILE_TOKENS)
            low, high = near(tile, tokens)
            queries = part(0, slice(low, high))
            grads = part(1, slice(low, high))
            scores = dot(kv[0, cols], queries, NT)
            attn_prob = jnp.exp2(scores * SCALE2 - rows[number, 0:1, low:high])
            grad_prob = dot(kv[1, cols], grads, NT)
            dscore = (attn_prob * (grad_prob - rows[number, 1:2, low:high])).astype(BF16)
            key_part = (dot(dscore, queries, NN) * SCALE).astype(BF16)
            value_part = dot(attn_prob.astype(BF16), grads, NN).astype(BF16)
            totals[0, cols] += key_part.astype(F32)
            totals[1, cols] += value_part.astype(F32)

    for_each_slab(valid, first, places, refs, body)
    if finish:
        refs[-3][...] = totals[0].astype(BF16)
        refs[-2][...] = totals[1].astype(BF16)


def key_side(valid, first, kv, window, rows, start, finish):
    tokens, dim = kv.shape[1:]
    arrays, places = arrays_of(window)
    totals = (2, tokens, dim)
    outs = [jax.ShapeDtypeStruct((tokens, dim), BF16)] * 2 if finish else [jax.ShapeDtypeStruct(totals, F32)]
    return vmem_call(
        functools.partial(key_kernel, first, places, finish), "key_side", 4, len(window),
        outs, [pltpu.VMEM(totals, F32)] if finish else [], valid, kv, rows,
        *([] if first == 0 else [start]), *arrays,
    )


def swap_mate(value):
    count = lax.axis_size("tm")
    return lax.ppermute(value, "tm", [(source, source ^ 1) for source in range(count)])


def swap_cross(value):
    count = lax.axis_size("tm")
    return lax.ppermute(value, "tm", [(s, cross_of(s)) for s in range(count) if has_cross(s % ROW_TILES)])


def cross_of(index):
    return index + 1 if index % CHIP_ROWS == CHIP_ROWS - 1 else index - 1


def has_cross(row):
    return 0 <= cross_of(row) < ROW_TILES


def frame_step(frame, phase):
    return 1 - 2 * ((frame + phase) % 2)


def swap_frames(value, phase, cross_only=False):
    count = lax.axis_size("tm")
    pairs = [(s, s + frame_step(s // ROW_TILES, phase) * ROW_TILES) for s in range(count)]
    pairs = [pair for pair in pairs if 0 <= pair[1] < count]
    if cross_only:
        pairs = [pair for pair in pairs if has_cross(pair[0] % ROW_TILES)]
    return lax.ppermute(value, "tm", pairs)


def per_device(queries, key_codes, value_codes, key_scales, value_scales, scale_slot, grad_out):
    index = lax.axis_index("tm")
    frames = lax.axis_size("tm") // ROW_TILES
    frame = index // ROW_TILES
    row = index % ROW_TILES
    cross = functools.reduce(lax.bitwise_or, [row == r for r in range(ROW_TILES) if has_cross(r)]).astype(jnp.int32)
    others = [frame + frame_step(frame, phase) for phase in range(2)]
    frame_a, frame_b = [((other >= 0) & (other < frames)).astype(jnp.int32) for other in others]
    one = jnp.ones((), jnp.int32)
    valid = jnp.stack([one, one, cross, frame_a, frame_b, cross * frame_a, cross * frame_b, frame_a, frame_b])

    kv, qg = prepare(queries, key_codes, value_codes, key_scales, value_scales, scale_slot, grad_out)
    kv_a = swap_frames(kv, 0)
    kv_b = swap_frames(kv, 1)
    kv_cross = swap_cross(kv)
    kv_mate = swap_mate(kv)
    qg_sent, kv_cross = lax.optimization_barrier((qg, kv_cross))
    qg_cross = swap_cross(qg_sent)
    kv_cross_a = swap_frames(kv_cross, 0, True)
    kv_cross_b = swap_frames(kv_cross, 1, True)
    kv_mate_a = swap_mate(kv_a)
    kv_mate_b = swap_mate(kv_b)

    kv_near = [(kv, 0), (kv_mate, 0)]
    kv_next = [(kv_cross, 0), (kv_a, 0), (kv_b, 0)]
    kv_last = [(kv_cross_a, 0), (kv_cross_b, 0), (kv_mate_a, 0), (kv_mate_b, 0)]
    running, kept_near = stats(valid, 0, qg, kv_near, None, False)

    running, kept_next = stats(valid, 2, qg, kv_next, running, False)
    qg_cross, running = lax.optimization_barrier((qg_cross, running))
    qg_pair = jnp.concatenate([qg, qg_cross])
    qg_a = swap_frames(qg_pair, 0)
    qg_b = swap_frames(qg_pair, 1)
    qg_mate = swap_mate(qg)
    qg_mate_a = swap_mate(qg_a)
    qg_mate_b = swap_mate(qg_b)

    rows, kept_last = stats(valid, 5, qg, kv_last, running, True)

    trio = jnp.stack([rows, swap_mate(rows), swap_cross(rows)])
    query_grad = query_side(valid, kv_near + kv_next + kv_last, [kept_near, kept_next, kept_last], rows)
    trio, query_grad = lax.optimization_barrier((trio, query_grad))
    trio_a = swap_frames(trio, 0)
    trio_b = swap_frames(trio, 1)

    qg_near = [(qg, 0), (qg_mate, 0), (qg_cross, 0)]
    qg_next = [(qg_a, 0), (qg_b, 0), (qg_a, 2), (qg_b, 2)]
    qg_last = [(qg_mate_a, 0), (qg_mate_b, 0)]
    rows_next = jnp.stack([trio_a[0], trio_b[0], trio_a[2], trio_b[2]])
    rows_last = jnp.stack([trio_a[1], trio_b[1]])
    (totals,) = key_side(valid, 0, kv, qg_near, trio, None, False)
    (totals,) = key_side(valid, 3, kv, qg_next, rows_next, totals, False)
    key_grad, value_grad = key_side(valid, 7, kv, qg_last, rows_last, totals, True)
    return query_grad, key_grad, value_grad


def solution(mesh):
    whole_axis = ("grp", "tm")
    flat = P(whole_axis)
    split = P(whole_axis, None)
    return jax.shard_map(
        per_device,
        mesh=mesh,
        in_specs=(split, split, split, flat, flat, split, split),
        out_specs=(split, split, split),
        check_vma=False,
    )
```

time: 66.6 us -> 64.9 us (0.974)
  Pallas kernels: 36.9 us -> 28.5 us
  other arithmetic: 1.15 us -> 5.33 us
  starting transfers between devices: 25.5 us -> 27.8 us
    pallas_call x7, Pallas kernels: 34.7 us -> 28.5 us  [vmem_call(): pl.pallas_call(kernel, in_specs=[pl.BlockSpec(memory_space=pltpu.SMEM)] +...]
    convert_element_type x0 -> x2, other arithmetic: none -> 2.2 us  [scaled(): return (blocked * picked[:, None, None]).astype(BF16).reshape(tokens, dim)]
    pallas_call x1 -> x0, Pallas kernels: 2.17 us -> none  [prepare(): pl.pallas_call(prepare_kernel, in_specs=[anywhere] * 7, out_specs=[pl.Blo...]
    ppermute x8, starting transfers between devices: 14.7 us -> 16.7 us  [swap_frames(): return lax.ppermute(value, 'tm', pairs)]
    ppermute x7, waiting for transfers between devices: 0.02 us -> 1.69 us  [swap_mate(): lax.ppermute(value, 'tm', [(source, source ^ 1) for source in range(count)])]
    another operation x0 -> x4, other arithmetic: none -> 1.12 us  [the longest x1 1.06 us: prepare(): return (kv, jnp.stack([queries, grad_out]))]
    ppermute x3, waiting for transfers between devices: 1.06 us -> 0.04 us  [swap_cross(): lax.ppermute(value, 'tm', [(s, cross_of(s)) for s in range(count) if has_...]
    reduce_sum x0 -> x1, other arithmetic: none -> 0.9 us  [scaled(): picked = jnp.sum(jnp.where(picker, scales[None, :], 0.0), axis=1)]
  transfers between devices with their start and end apart: 18 -> 18, of which waited for: 2 -> 2; matrix products, arithmetic and copies ran while one was open for 2% -> 4% of each run, Pallas kernels for 46% -> 38%
where the time goes in v4:
time: 64.9 us; the launch traced here: 64.6 us
  Pallas kernels  28.5 us (44%)
  starting transfers between devices  27.8 us (43%)
  other arithmetic  5.33 us (8%)
  waiting for transfers between devices  1.76 us (3%)
  between operations  0.98 us (2%)
    pallas_call x7, Pallas kernels, vmem_call(): pl.pallas_call(kernel, in_specs=[pl.BlockSpec(memory_space=pltpu.SMEM)] +...  28.5 us
    ppermute x8, starting transfers between devices, swap_frames(): return lax.ppermute(value, 'tm', pairs)  16.7 us
    ppermute x3, starting transfers between devices, swap_cross(): lax.ppermute(value, 'tm', [(s, cross_of(s)) for s in range(count) if has_...  9.83 us
    convert_element_type x2, other arithmetic, scaled(): return (blocked * picked[:, None, None]).astype(BF16).reshape(tokens, dim)  2.2 us
    ppermute x7, waiting for transfers between devices, swap_mate(): lax.ppermute(value, 'tm', [(source, source ^ 1) for source in range(count)])  1.69 us
    ppermute x7, starting transfers between devices, swap_mate(): lax.ppermute(value, 'tm', [(source, source ^ 1) for source in range(count)])  1.35 us
  transfers between devices with their start and end apart: 18, of which 2 were waited for; matrix products, arithmetic and copies ran while one was open for 4% of the time, Pallas kernels for 38%

profile of v4, /device:TPU:11, one launch (start us, length us, event | category | flops | bytes accessed | tf_op | source)
XLA Modules:
  0.0 64.6 jit_solution(4562808802160870389)
XLA Ops:
  0.6 0.9 %select_reduce_fusion.1 = (f32[6]{0:T(128)S(1)}, f32[6]{0:T(128)S(1)}) fusion(f32[6]{0:T(128)} %param.10, s32[6]{0:T(128)} %bitcast.26, f32[6]{0:T(128)} %param.11), kind=kLoop, calls=%fused_computation.11 | loop fusion | flops 168 | bytes 120 | tf_op jit(solution)/shard_map/reduce_sum | solution.py:52
  1.5 0.1 broadcast_bitcast_fusion
  1.6 1.1 %fusion = bf16[1,768,128]{2,1,0:T(8,128)(2,1)S(1)} fusion(bf16[768,128]{1,0:T(8,128)(2,1)} %param.8, f32[768]{0:T(1024)S(1)} %get-tuple-element.40), kind=kLoop, calls=%fused_computation.5 | loop fusion | flops 294912 | bytes 396288 | tf_op jit(solution)/shard_map/convert_element_type | solution.py:54
  2.7 1.1 %fusion.1 = bf16[1,768,128]{2,1,0:T(8,128)(2,1)S(1)} fusion(bf16[768,128]{1,0:T(8,128)(2,1)} %param.9, f32[768]{0:T(1024)S(1)} %get-tuple-element.39), kind=kLoop, calls=%fused_computation.6 | loop fusion | flops 294912 | bytes 396288 | tf_op jit(solution)/shard_map/convert_element_type | solution.py:54
  3.9 3.7 %collective-permute-start = (bf16[2,768,128]{2,1,0:T(8,128)(2,1)S(1)}, bf16[2,768,128]{2,1,0:T(8,128)(2,1)S(1)}, u32[]{:S(2)}, u32[]{:S(2)}) collective-permute-start(bf16[2,768,128]{2,1,0:T(8,128)(2,1)S(1)} %pad_maximum_fusion.2.refs_0_.refs_3_.kv), channel_id=1, source_target_pairs={{1,2},{2,1},{5,6},{6,5},{9,10},{10,9},{13,14},{14,13},{17,18},{18,... | collective-permute-start | bytes 1179656 | tf_op jit(solution)/shard_map/ppermute | solution.py:237
  7.7 0.2 collective-permute-start.3
  7.9 4.3 %collective-permute-start.4 = (bf16[2,768,128]{2,1,0:T(8,128)(2,1)S(1)}, bf16[2,768,128]{2,1,0:T(8,128)(2,1)S(1)}, u32[]{:S(2)}, u32[]{:S(2)}) collective-permute-start(bf16[2,768,128]{2,1,0:T(8,128)(2,1)S(1)} %pad_maximum_fusion.2.refs_0_.refs_3_.kv), channel_id=1, source_target_pairs={{4,8},{5,9},{6,10},{7,11},{8,4},{9,5},{10,6},{11,7},{20,24},{21,25... | collective-permute-start | bytes 1179656 | tf_op jit(solution)/shard_map/ppermute | solution.py:258
  12.2 1.1 %pad_maximum_fusion.1.qg.refs_0_ = bf16[2,768,128]{2,1,0:T(8,128)(2,1)S(1)} fusion(bf16[1,768,128]{2,1,0:T(8,128)(2,1)} %bitcast.20, bf16[1,768,128]{2,1,0:T(8,128)(2,1)} %bitcast.22), kind=kLoop, calls=%fused_computation.1 | loop fusion | flops 196608 | bytes 786432 | tf_op jit(solution)/shard_map/stack | solution.py:57
  13.3 3.3 %collective-permute-start.1 = (bf16[2,768,128]{2,1,0:T(8,128)(2,1)S(1)}, bf16[2,768,128]{2,1,0:T(8,128)(2,1)S(1)}, u32[]{:S(2)}, u32[]{:S(2)}) collective-permute-start(bf16[2,768,128]{2,1,0:T(8,128)(2,1)S(1)} %pad_maximum_fusion.1.qg.refs_0_), channel_id=1, source_target_pairs={{1,2},{2,1},{5,6},{6,5},{9,10},{10,9},{13,14},{14,13},{17,18},{18,... | collective-permute-start | bytes 1179656 | tf_op jit(solution)/shard_map/ppermute | solution.py:237
  16.7 2.1 %collective-permute-start.5 = (bf16[2,768,128]{2,1,0:T(8,128)(2,1)S(1)}, bf16[2,768,128]{2,1,0:T(8,128)(2,1)S(1)}, u32[]{:S(2)}, u32[]{:S(2)}) collective-permute-start(bf16[2,768,128]{2,1,0:T(8,128)(2,1)S(1)} %collective-permute-done.refs_1_.refs_5_), channel_id=1, source_target_pairs={{1,5},{2,6},{5,1},{6,2},{9,13},{10,14},{13,9},{14,10},{17,21},{18,... | collective-permute-start | bytes 1179656 | tf_op jit(solution)/shard_map/ppermute | solution.py:258
  18.8 0.1 stack.63.valid
  18.9 4.3 %collective-permute-start.6 = (bf16[2,768,128]{2,1,0:T(8,128)(2,1)S(1)}, bf16[2,768,128]{2,1,0:T(8,128)(2,1)S(1)}, u32[]{:S(2)}, u32[]{:S(2)}) collective-permute-start(bf16[2,768,128]{2,1,0:T(8,128)(2,1)S(1)} %collective-permute-done.refs_1_.refs_5_), channel_id=1, source_target_pairs={{5,9},{6,10},{9,5},{10,6},{21,25},{22,26},{25,21},{26,22}} | collective-permute-start | bytes 1179656 | tf_op jit(solution)/shard_map/ppermute | solution.py:258
  23.3 2.0 %row_stats.3 = (f32[2,7,2,256,256]{4,3,2,1,0:T(8,128)S(1)}, f32[3,8,768]{2,1,0:T(8,128)S(1)}) custom-call(s32[9]{0:T(128)S(1)} %stack.63.valid, bf16[2,768,128]{2,1,0:T(8,128)(2,1)S(1)} %pad_maximum_fusion.1.qg.refs_0_, bf16[2,768,128]{2,1,0:T(8,128)(2,1)S(1)} %pad_maximum_fusion.2.refs_0_.refs_3_.kv, ...), custom_call_target="tpu_custom_call" | custom-call | flops 301989888 | bytes 196608 | tf_op jit(solution)/shard_map/row_stats/pallas_call | solution.py:63
  25.3 2.8 %row_stats.4 = (f32[3,7,2,256,256]{4,3,2,1,0:T(8,128)S(1)}, f32[3,8,768]{2,1,0:T(8,128)S(1)}) custom-call(s32[9]{0:T(128)S(1)} %stack.63.valid, bf16[2,768,128]{2,1,0:T(8,128)(2,1)S(1)} %pad_maximum_fusion.1.qg.refs_0_, f32[3,8,768]{2,1,0:T(8,128)S(1)} %get-tuple-element.18.refs_0_, bf16[2,768,128]{2,1,0:T(8,128)(2,1)S(1)} %collective-permute-done.refs_1_.refs_5_, ...), custom_call_target="tpu_custom_call" | custom-call | flops 452984832 | bytes 294912 | tf_op jit(solution)/shard_map/row_stats/pallas_call | solution.py:63
  28.1 1.1 %pad_maximum_fusion = bf16[4,768,128]{2,1,0:T(8,128)(2,1)S(1)} fusion(bf16[2,768,128]{2,1,0:T(8,128)(2,1)S(1)} %collective-permute-done.1.refs_2_, bf16[1,768,128]{2,1,0:T(8,128)(2,1)} %bitcast.21, bf16[1,768,128]{2,1,0:T(8,128)(2,1)} %bitcast.23), kind=kLoop, calls=%fused_computation | loop fusion | flops 786432 | bytes 1572864 | tf_op jit(solution)/shard_map/concatenate | solution.py:291
  29.2 0.1 collective-permute-start.14
  29.3 1.9 %collective-permute-start.15 = (bf16[4,768,128]{2,1,0:T(8,128)(2,1)S(1)}, bf16[4,768,128]{2,1,0:T(8,128)(2,1)S(1)}, u32[]{:S(2)}, u32[]{:S(2)}) collective-permute-start(bf16[4,768,128]{2,1,0:T(8,128)(2,1)S(1)} %pad_maximum_fusion), channel_id=1, source_target_pairs={{4,8},{5,9},{6,10},{7,11},{8,4},{9,5},{10,6},{11,7},{20,24},{21,25... | collective-permute-start | bytes 2359304 | tf_op jit(solution)/shard_map/ppermute | solution.py:258
  31.2 0.1 collective-permute-start.7
  31.3 0.5 collective-permute-start.8
  31.8 0.1 collective-permute-start.13
  31.9 1.1 %collective-permute-done.7.refs_3_.refs_10_ = bf16[2,768,128]{2,1,0:T(8,128)(2,1)S(1)} collective-permute-done((bf16[2,768,128]{2,1,0:T(8,128)(2,1)S(1)}, bf16[2,768,128]{2,1,0:T(8,128)(2,1)S(1)}, u32[]{:S(2)}, u32[]{:S(2)}) %collective-permute-start.7) | collective-permute-done | bytes 393248 | tf_op jit(solution)/shard_map/ppermute | solution.py:232
  33.0 0.6 collective-permute-done.8.refs_4_.refs_11_
  33.6 3.6 %row_stats.5 = (f32[2,768]{1,0:T(2,128)S(1)}, f32[4,7,2,256,256]{4,3,2,1,0:T(8,128)S(1)}) custom-call(s32[9]{0:T(128)S(1)} %stack.63.valid, bf16[2,768,128]{2,1,0:T(8,128)(2,1)S(1)} %pad_maximum_fusion.1.qg.refs_0_, f32[3,8,768]{2,1,0:T(8,128)S(1)} %get-tuple-element.21.refs_0_, bf16[2,768,128]{2,1,0:T(8,128)(2,1)S(1)} %collective-permute-done.5.refs_1_.refs_8_, ...), custom_call_target="tpu_custom_call" | custom-call | flops 603979776 | bytes 393216 | tf_op jit(solution)/shard_map/row_stats/pallas_call | solution.py:63
  37.2 0.1 collective-permute-start.9
  37.3 2.8 %collective-permute-start.10 = (f32[2,768]{1,0:T(2,128)S(1)}, f32[2,768]{1,0:T(2,128)S(1)}, u32[]{:S(2)}, u32[]{:S(2)}) collective-permute-start(f32[2,768]{1,0:T(2,128)S(1)} %get-tuple-element.22.rows), channel_id=1, source_target_pairs={{1,2},{2,1},{5,6},{6,5},{9,10},{10,9},{13,14},{14,13},{17,18},{18,... | collective-permute-start | bytes 18440 | tf_op jit(solution)/shard_map/ppermute | solution.py:237
  40.1 5.6 %query_side.1 = bf16[768,128]{1,0:T(8,128)(2,1)} custom-call(s32[9]{0:T(128)S(1)} %stack.63.valid, f32[2,768]{1,0:T(2,128)S(1)} %get-tuple-element.22.rows, f32[2,7,2,256,256]{4,3,2,1,0:T(8,128)S(1)} %get-tuple-element.23.refs_0_, f32[3,7,2,256,256]{4,3,2,1,0:T(8,128)S(1)} %get-tuple-element.24.refs_1_, ...), custom_call_target="tpu_custom_call" | custom-call | flops 679477248 | bytes 884736 | tf_op jit(solution)/shard_map/query_side/pallas_call | solution.py:63
  45.7 3.6 %collective-permute-start.12 = (f32[3,2,768]{2,1,0:T(2,128)S(1)}, f32[3,2,768]{2,1,0:T(2,128)S(1)}, u32[]{:S(2)}, u32[]{:S(2)}) collective-permute-start(f32[3,2,768]{2,1,0:T(2,128)S(1)} %pad_maximum_fusion.4.rows), channel_id=1, source_target_pairs={{4,8},{5,9},{6,10},{7,11},{8,4},{9,5},{10,6},{11,7},{20,24},{21,25... | collective-permute-start | bytes 55304 | tf_op jit(solution)/shard_map/ppermute | solution.py:258
  49.4 4.5 %key_side.3.refs_0_ = f32[2,768,128]{2,1,0:T(8,128)S(1)} custom-call(s32[9]{0:T(128)S(1)} %stack.63.valid, bf16[2,768,128]{2,1,0:T(8,128)(2,1)S(1)} %pad_maximum_fusion.2.refs_0_.refs_3_.kv, f32[3,2,768]{2,1,0:T(2,128)S(1)} %pad_maximum_fusion.4.rows, bf16[2,768,128]{2,1,0:T(8,128)(2,1)S(1)} %pad_maximum_fusion.1.qg.refs_0_, ...), custom_call_target="tpu_custom_call" | custom-call | flops 905969664 | bytes 294912 | tf_op jit(solution)/shard_map/key_side/pallas_call | solution.py:63
  53.9 0.1 collective-permute-start.16
  54.0 0.5 collective-permute-start.17
  54.6 5.9 %key_side.4.refs_0_ = f32[2,768,128]{2,1,0:T(8,128)S(1)} custom-call(s32[9]{0:T(128)S(1)} %stack.63.valid, bf16[2,768,128]{2,1,0:T(8,128)(2,1)S(1)} %pad_maximum_fusion.2.refs_0_.refs_3_.kv, f32[4,2,768]{2,1,0:T(2,128)S(1)} %pad_maximum_fusion.3.rows, f32[2,768,128]{2,1,0:T(8,128)S(1)} %key_side.3.refs_0_, ...), custom_call_target="tpu_custom_call" | custom-call | flops 1207959552 | bytes 393216 | tf_op jit(solution)/shard_map/key_side/pallas_call | solution.py:63
  60.5 4.0 %key_side.5 = (bf16[768,128]{1,0:T(8,128)(2,1)}, bf16[768,128]{1,0:T(8,128)(2,1)}) custom-call(s32[9]{0:T(128)S(1)} %stack.63.valid, bf16[2,768,128]{2,1,0:T(8,128)(2,1)S(1)} %pad_maximum_fusion.2.refs_0_.refs_3_.kv, f32[2,2,768]{2,1,0:T(2,128)S(1)} %pad_maximum_fusion.5.rows, f32[2,768,128]{2,1,0:T(8,128)S(1)} %key_side.4.refs_0_, ...), custom_call_target="tpu_custom_call" | custom-call | flops 603979776 | bytes 196608 | tf_op jit(solution)/shard_map/key_side/pallas_call | solution.py:63
  (25 shorter events, 0.3 us)
Async XLA Ops:
  3.9 9.5 %collective-permute-start = (bf16[2,768,128]{2,1,0:T(8,128)(2,1)S(1)}, bf16[2,768,128]{2,1,0:T(8,128)(2,1)S(1)}, u32[]{:S(2)}, u32[]{:S(2)}) collective-permute-start(bf16[2,768,128]{2,1,0:T(8,128)(2,1)S(1)} %pad_maximum_fusion.2.refs_0_.refs_3_.kv), channel_id=1, source_target_pairs={{1,2},{2,1},{5,6},{6,5},{9,10},{10,9},{13,14},{14,13},{17,18},{18,... | collective-permute-start | bytes 1179656 | tf_op jit(solution)/shard_map/ppermute | solution.py:237
  7.6 11.3 %collective-permute-start.2 = (bf16[2,768,128]{2,1,0:T(8,128)(2,1)S(1)}, bf16[2,768,128]{2,1,0:T(8,128)(2,1)S(1)}, u32[]{:S(2)}, u32[]{:S(2)}) collective-permute-start(bf16[2,768,128]{2,1,0:T(8,128)(2,1)S(1)} %pad_maximum_fusion.2.refs_0_.refs_3_.kv), channel_id=1, source_target_pairs={{0,1},{1,0},{2,3},{3,2},{4,5},{5,4},{6,7},{7,6},{8,9},{9,8},{10,11... | collective-permute-start | bytes 1179656 | tf_op jit(solution)/shard_map/ppermute | solution.py:232
  7.7 17.7 %collective-permute-start.3 = (bf16[2,768,128]{2,1,0:T(8,128)(2,1)S(1)}, bf16[2,768,128]{2,1,0:T(8,128)(2,1)S(1)}, u32[]{:S(2)}, u32[]{:S(2)}) collective-permute-start(bf16[2,768,128]{2,1,0:T(8,128)(2,1)S(1)} %pad_maximum_fusion.2.refs_0_.refs_3_.kv), channel_id=1, source_target_pairs={{0,4},{1,5},{2,6},{3,7},{4,0},{5,1},{6,2},{7,3},{8,12},{9,13},{10,... | collective-permute-start | bytes 1179656 | tf_op jit(solution)/shard_map/ppermute | solution.py:258
  7.9 17.4 %collective-permute-start.4 = (bf16[2,768,128]{2,1,0:T(8,128)(2,1)S(1)}, bf16[2,768,128]{2,1,0:T(8,128)(2,1)S(1)}, u32[]{:S(2)}, u32[]{:S(2)}) collective-permute-start(bf16[2,768,128]{2,1,0:T(8,128)(2,1)S(1)} %pad_maximum_fusion.2.refs_0_.refs_3_.kv), channel_id=1, source_target_pairs={{4,8},{5,9},{6,10},{7,11},{8,4},{9,5},{10,6},{11,7},{20,24},{21,25... | collective-permute-start | bytes 1179656 | tf_op jit(solution)/shard_map/ppermute | solution.py:258
  13.3 14.8 %collective-permute-start.1 = (bf16[2,768,128]{2,1,0:T(8,128)(2,1)S(1)}, bf16[2,768,128]{2,1,0:T(8,128)(2,1)S(1)}, u32[]{:S(2)}, u32[]{:S(2)}) collective-permute-start(bf16[2,768,128]{2,1,0:T(8,128)(2,1)S(1)} %pad_maximum_fusion.1.qg.refs_0_), channel_id=1, source_target_pairs={{1,2},{2,1},{5,6},{6,5},{9,10},{10,9},{13,14},{14,13},{17,18},{18,... | collective-permute-start | bytes 1179656 | tf_op jit(solution)/shard_map/ppermute | solution.py:237
  16.7 14.7 %collective-permute-start.5 = (bf16[2,768,128]{2,1,0:T(8,128)(2,1)S(1)}, bf16[2,768,128]{2,1,0:T(8,128)(2,1)S(1)}, u32[]{:S(2)}, u32[]{:S(2)}) collective-permute-start(bf16[2,768,128]{2,1,0:T(8,128)(2,1)S(1)} %collective-permute-done.refs_1_.refs_5_), channel_id=1, source_target_pairs={{1,5},{2,6},{5,1},{6,2},{9,13},{10,14},{13,9},{14,10},{17,21},{18,... | collective-permute-start | bytes 1179656 | tf_op jit(solution)/shard_map/ppermute | solution.py:258
  18.9 12.9 %collective-permute-start.6 = (bf16[2,768,128]{2,1,0:T(8,128)(2,1)S(1)}, bf16[2,768,128]{2,1,0:T(8,128)(2,1)S(1)}, u32[]{:S(2)}, u32[]{:S(2)}) collective-permute-start(bf16[2,768,128]{2,1,0:T(8,128)(2,1)S(1)} %collective-permute-done.refs_1_.refs_5_), channel_id=1, source_target_pairs={{5,9},{6,10},{9,5},{10,6},{21,25},{22,26},{25,21},{26,22}} | collective-permute-start | bytes 1179656 | tf_op jit(solution)/shard_map/ppermute | solution.py:258
  29.2 24.7 %collective-permute-start.14 = (bf16[4,768,128]{2,1,0:T(8,128)(2,1)S(1)}, bf16[4,768,128]{2,1,0:T(8,128)(2,1)S(1)}, u32[]{:S(2)}, u32[]{:S(2)}) collective-permute-start(bf16[4,768,128]{2,1,0:T(8,128)(2,1)S(1)} %pad_maximum_fusion), channel_id=1, source_target_pairs={{0,4},{1,5},{2,6},{3,7},{4,0},{5,1},{6,2},{7,3},{8,12},{9,13},{10,... | collective-permute-start | bytes 2359304 | tf_op jit(solution)/shard_map/ppermute | solution.py:258
  29.3 24.7 %collective-permute-start.15 = (bf16[4,768,128]{2,1,0:T(8,128)(2,1)S(1)}, bf16[4,768,128]{2,1,0:T(8,128)(2,1)S(1)}, u32[]{:S(2)}, u32[]{:S(2)}) collective-permute-start(bf16[4,768,128]{2,1,0:T(8,128)(2,1)S(1)} %pad_maximum_fusion), channel_id=1, source_target_pairs={{4,8},{5,9},{6,10},{7,11},{8,4},{9,5},{10,6},{11,7},{20,24},{21,25... | collective-permute-start | bytes 2359304 | tf_op jit(solution)/shard_map/ppermute | solution.py:258
  31.2 1.8 %collective-permute-start.7 = (bf16[2,768,128]{2,1,0:T(8,128)(2,1)S(1)}, bf16[2,768,128]{2,1,0:T(8,128)(2,1)S(1)}, u32[]{:S(2)}, u32[]{:S(2)}) collective-permute-start(bf16[2,768,128]{2,1,0:T(8,128)(2,1)S(1)} %collective-permute-done.3.refs_2_.refs_6_), channel_id=1, source_target_pairs={{0,1},{1,0},{2,3},{3,2},{4,5},{5,4},{6,7},{7,6},{8,9},{9,8},{10,11... | collective-permute-start | bytes 1179656 | tf_op jit(solution)/shard_map/ppermute | solution.py:232
  31.3 2.3 %collective-permute-start.8 = (bf16[2,768,128]{2,1,0:T(8,128)(2,1)S(1)}, bf16[2,768,128]{2,1,0:T(8,128)(2,1)S(1)}, u32[]{:S(2)}, u32[]{:S(2)}) collective-permute-start(bf16[2,768,128]{2,1,0:T(8,128)(2,1)S(1)} %collective-permute-done.4.refs_3_.refs_7_), channel_id=1, source_target_pairs={{0,1},{1,0},{2,3},{3,2},{4,5},{5,4},{6,7},{7,6},{8,9},{9,8},{10,11... | collective-permute-start | bytes 1179656 | tf_op jit(solution)/shard_map/ppermute | solution.py:232
  31.8 17.6 %collective-permute-start.13 = (bf16[2,768,128]{2,1,0:T(8,128)(2,1)S(1)}, bf16[2,768,128]{2,1,0:T(8,128)(2,1)S(1)}, u32[]{:S(2)}, u32[]{:S(2)}) collective-permute-start(bf16[2,768,128]{2,1,0:T(8,128)(2,1)S(1)} %pad_maximum_fusion.1.qg.refs_0_), channel_id=1, source_target_pairs={{0,1},{1,0},{2,3},{3,2},{4,5},{5,4},{6,7},{7,6},{8,9},{9,8},{10,11... | collective-permute-start | bytes 1179656 | tf_op jit(solution)/shard_map/ppermute | solution.py:232
  37.2 8.4 %collective-permute-start.9 = (f32[2,768]{1,0:T(2,128)S(1)}, f32[2,768]{1,0:T(2,128)S(1)}, u32[]{:S(2)}, u32[]{:S(2)}) collective-permute-start(f32[2,768]{1,0:T(2,128)S(1)} %get-tuple-element.22.rows), channel_id=1, source_target_pairs={{0,1},{1,0},{2,3},{3,2},{4,5},{5,4},{6,7},{7,6},{8,9},{9,8},{10,11... | collective-permute-start | bytes 18440 | tf_op jit(solution)/shard_map/ppermute | solution.py:232
  37.3 8.4 %collective-permute-start.10 = (f32[2,768]{1,0:T(2,128)S(1)}, f32[2,768]{1,0:T(2,128)S(1)}, u32[]{:S(2)}, u32[]{:S(2)}) collective-permute-start(f32[2,768]{1,0:T(2,128)S(1)} %get-tuple-element.22.rows), channel_id=1, source_target_pairs={{1,2},{2,1},{5,6},{6,5},{9,10},{10,9},{13,14},{14,13},{17,18},{18,... | collective-permute-start | bytes 18440 | tf_op jit(solution)/shard_map/ppermute | solution.py:237
  45.7 8.9 %collective-permute-start.11 = (f32[3,2,768]{2,1,0:T(2,128)S(1)}, f32[3,2,768]{2,1,0:T(2,128)S(1)}, u32[]{:S(2)}, u32[]{:S(2)}) collective-permute-start(f32[3,2,768]{2,1,0:T(2,128)S(1)} %pad_maximum_fusion.4.rows), channel_id=1, source_target_pairs={{0,4},{1,5},{2,6},{3,7},{4,0},{5,1},{6,2},{7,3},{8,12},{9,13},{10,... | collective-permute-start | bytes 55304 | tf_op jit(solution)/shard_map/ppermute | solution.py:258
  45.7 8.8 %collective-permute-start.12 = (f32[3,2,768]{2,1,0:T(2,128)S(1)}, f32[3,2,768]{2,1,0:T(2,128)S(1)}, u32[]{:S(2)}, u32[]{:S(2)}) collective-permute-start(f32[3,2,768]{2,1,0:T(2,128)S(1)} %pad_maximum_fusion.4.rows), channel_id=1, source_target_pairs={{4,8},{5,9},{6,10},{7,11},{8,4},{9,5},{10,6},{11,7},{20,24},{21,25... | collective-permute-start | bytes 55304 | tf_op jit(solution)/shard_map/ppermute | solution.py:258
  53.9 6.6 %collective-permute-start.16 = (bf16[4,768,128]{2,1,0:T(8,128)(2,1)S(1)}, bf16[4,768,128]{2,1,0:T(8,128)(2,1)S(1)}, u32[]{:S(2)}, u32[]{:S(2)}) collective-permute-start(bf16[4,768,128]{2,1,0:T(8,128)(2,1)S(1)} %collective-permute-done.14.refs_1_), channel_id=1, source_target_pairs={{0,1},{1,0},{2,3},{3,2},{4,5},{5,4},{6,7},{7,6},{8,9},{9,8},{10,11... | collective-permute-start | bytes 2359304 | tf_op jit(solution)/shard_map/ppermute | solution.py:232
  54.0 6.5 %collective-permute-start.17 = (bf16[4,768,128]{2,1,0:T(8,128)(2,1)S(1)}, bf16[4,768,128]{2,1,0:T(8,128)(2,1)S(1)}, u32[]{:S(2)}, u32[]{:S(2)}) collective-permute-start(bf16[4,768,128]{2,1,0:T(8,128)(2,1)S(1)} %collective-permute-done.15.refs_2_), channel_id=1, source_target_pairs={{0,1},{1,0},{2,3},{3,2},{4,5},{5,4},{6,7},{7,6},{8,9},{9,8},{10,11... | collective-permute-start | bytes 2359304 | tf_op jit(solution)/shard_map/ppermute | solution.py:232

commit v5 on v4

--- a/solution.py
+++ b/solution.py
@@ -195,19 +195,37 @@
         refs = refs[1:]
 
     def body(number, part):
-        for tile in range(tokens // TILE_TOKENS):
-            cols = slice(tile * TILE_TOKENS, (tile + 1) * TILE_TOKENS)
-            low, high = near(tile, tokens)
-            queries = part(0, slice(low, high))
-            grads = part(1, slice(low, high))
-            scores = dot(kv[0, cols], queries, NT)
-            attn_prob = jnp.exp2(scores * SCALE2 - rows[number, 0:1, low:high])
-            grad_prob = dot(kv[1, cols], grads, NT)
-            dscore = (attn_prob * (grad_prob - rows[number, 1:2, low:high])).astype(BF16)
-            key_part = (dot(dscore, queries, NN) * SCALE).astype(BF16)
-            value_part = dot(attn_prob.astype(BF16), grads, NN).astype(BF16)
+        tiles = tokens // TILE_TOKENS
+
+        def ends(tile):
+            return slice(tile * TILE_TOKENS, (tile + 1) * TILE_TOKENS), slice(*near(tile, tokens))
+
+        def front(tile):
+            cols, window = ends(tile)
+            return dot(kv[0, cols], part(0, window), NT), dot(kv[1, cols], part(1, window), NT)
+
+        def middle(tile, scores, grad_prob):
+            window = ends(tile)[1]
+            attn_prob = jnp.exp2(scores * SCALE2 - rows[number, 0:1, window])
+            dscore = (attn_prob * (grad_prob - rows[number, 1:2, window])).astype(BF16)
+            return dscore, attn_prob.astype(BF16)
+
+        def back(tile, dscore, prob_low):
+            cols, window = ends(tile)
+            key_part = (dot(dscore, part(0, window), NN) * SCALE).astype(BF16)
+            value_part = dot(prob_low, part(1, window), NN).astype(BF16)
             totals[0, cols] += key_part.astype(F32)
             totals[1, cols] += value_part.astype(F32)
+
+        ahead, behind = front(0), None
+        for tile in range(tiles):
+            now = middle(tile, *ahead)
+            if tile + 1 < tiles:
+                ahead = front(tile + 1)
+            if behind is not None:
+                back(tile - 1, *behind)
+            behind = now
+        back(tiles - 1, *behind)
 
     for_each_slab(valid, first, places, refs, body)
     if finish:

time: 64.9 us -> 63.6 us (0.980)
  Pallas kernels: 28.5 us -> 27.1 us
    pallas_call x7, Pallas kernels: 28.5 us -> 27.1 us  [vmem_call(): pl.pallas_call(kernel, in_specs=[pl.BlockSpec(memory_space=pltpu.SMEM)] +...]
  transfers between devices with their start and end apart: 18 -> 18, of which waited for: 2 -> 2; matrix products, arithmetic and copies ran while one was open for 4% -> 4% of each run, Pallas kernels for 38% -> 37%
where the time goes in v5:
time: 63.6 us; the launch traced here: 63.2 us
  starting transfers between devices  27.8 us (44%)
  Pallas kernels  27.1 us (43%)
  other arithmetic  5.33 us (8%)
  waiting for transfers between devices  1.76 us (3%)
  between operations  0.99 us (2%)
    pallas_call x7, Pallas kernels, vmem_call(): pl.pallas_call(kernel, in_specs=[pl.BlockSpec(memory_space=pltpu.SMEM)] +...  27.1 us
    ppermute x8, starting transfers between devices, swap_frames(): return lax.ppermute(value, 'tm', pairs)  16.7 us
    ppermute x3, starting transfers between devices, swap_cross(): lax.ppermute(value, 'tm', [(s, cross_of(s)) for s in range(count) if has_...  9.83 us
    convert_element_type x2, other arithmetic, scaled(): return (blocked * picked[:, None, None]).astype(BF16).reshape(tokens, dim)  2.2 us
    ppermute x7, waiting for transfers between devices, swap_mate(): lax.ppermute(value, 'tm', [(source, source ^ 1) for source in range(count)])  1.69 us
    ppermute x7, starting transfers between devices, swap_mate(): lax.ppermute(value, 'tm', [(source, source ^ 1) for source in range(count)])  1.35 us
  transfers between devices with their start and end apart: 18, of which 2 were waited for; matrix products, arithmetic and copies ran while one was open for 4% of the time, Pallas kernels for 37%

profile of v5, /device:TPU:11, one launch (start us, length us, event | category | flops | bytes accessed | tf_op | source)
XLA Modules:
  0.0 63.2 jit_solution(12008314977217636009)
XLA Ops:
  0.6 0.9 %select_reduce_fusion.1 = (f32[6]{0:T(128)S(1)}, f32[6]{0:T(128)S(1)}) fusion(f32[6]{0:T(128)} %param.10, s32[6]{0:T(128)} %bitcast.26, f32[6]{0:T(128)} %param.11), kind=kLoop, calls=%fused_computation.11 | loop fusion | flops 168 | bytes 120 | tf_op jit(solution)/shard_map/reduce_sum | solution.py:52
  1.5 0.1 broadcast_bitcast_fusion
  1.6 1.1 %fusion = bf16[1,768,128]{2,1,0:T(8,128)(2,1)S(1)} fusion(bf16[768,128]{1,0:T(8,128)(2,1)} %param.8, f32[768]{0:T(1024)S(1)} %get-tuple-element.40), kind=kLoop, calls=%fused_computation.5 | loop fusion | flops 294912 | bytes 396288 | tf_op jit(solution)/shard_map/convert_element_type | solution.py:54
  2.7 1.1 %fusion.1 = bf16[1,768,128]{2,1,0:T(8,128)(2,1)S(1)} fusion(bf16[768,128]{1,0:T(8,128)(2,1)} %param.9, f32[768]{0:T(1024)S(1)} %get-tuple-element.39), kind=kLoop, calls=%fused_computation.6 | loop fusion | flops 294912 | bytes 396288 | tf_op jit(solution)/shard_map/convert_element_type | solution.py:54
  3.9 3.7 %collective-permute-start = (bf16[2,768,128]{2,1,0:T(8,128)(2,1)S(1)}, bf16[2,768,128]{2,1,0:T(8,128)(2,1)S(1)}, u32[]{:S(2)}, u32[]{:S(2)}) collective-permute-start(bf16[2,768,128]{2,1,0:T(8,128)(2,1)S(1)} %pad_maximum_fusion.2.refs_0_.refs_3_.kv), channel_id=1, source_target_pairs={{1,2},{2,1},{5,6},{6,5},{9,10},{10,9},{13,14},{14,13},{17,18},{18,... | collective-permute-start | bytes 1179656 | tf_op jit(solution)/shard_map/ppermute | solution.py:255
  7.6 0.1 collective-permute-start.2
  7.7 0.2 collective-permute-start.3
  7.9 4.3 %collective-permute-start.4 = (bf16[2,768,128]{2,1,0:T(8,128)(2,1)S(1)}, bf16[2,768,128]{2,1,0:T(8,128)(2,1)S(1)}, u32[]{:S(2)}, u32[]{:S(2)}) collective-permute-start(bf16[2,768,128]{2,1,0:T(8,128)(2,1)S(1)} %pad_maximum_fusion.2.refs_0_.refs_3_.kv), channel_id=1, source_target_pairs={{4,8},{5,9},{6,10},{7,11},{8,4},{9,5},{10,6},{11,7},{20,24},{21,25... | collective-permute-start | bytes 1179656 | tf_op jit(solution)/shard_map/ppermute | solution.py:276
  12.2 1.1 %pad_maximum_fusion.1.qg.refs_0_ = bf16[2,768,128]{2,1,0:T(8,128)(2,1)S(1)} fusion(bf16[1,768,128]{2,1,0:T(8,128)(2,1)} %bitcast.20, bf16[1,768,128]{2,1,0:T(8,128)(2,1)} %bitcast.22), kind=kLoop, calls=%fused_computation.1 | loop fusion | flops 196608 | bytes 786432 | tf_op jit(solution)/shard_map/stack | solution.py:57
  13.3 3.3 %collective-permute-start.1 = (bf16[2,768,128]{2,1,0:T(8,128)(2,1)S(1)}, bf16[2,768,128]{2,1,0:T(8,128)(2,1)S(1)}, u32[]{:S(2)}, u32[]{:S(2)}) collective-permute-start(bf16[2,768,128]{2,1,0:T(8,128)(2,1)S(1)} %pad_maximum_fusion.1.qg.refs_0_), channel_id=1, source_target_pairs={{1,2},{2,1},{5,6},{6,5},{9,10},{10,9},{13,14},{14,13},{17,18},{18,... | collective-permute-start | bytes 1179656 | tf_op jit(solution)/shard_map/ppermute | solution.py:255
  16.7 2.1 %collective-permute-start.5 = (bf16[2,768,128]{2,1,0:T(8,128)(2,1)S(1)}, bf16[2,768,128]{2,1,0:T(8,128)(2,1)S(1)}, u32[]{:S(2)}, u32[]{:S(2)}) collective-permute-start(bf16[2,768,128]{2,1,0:T(8,128)(2,1)S(1)} %collective-permute-done.refs_1_.refs_5_), channel_id=1, source_target_pairs={{1,5},{2,6},{5,1},{6,2},{9,13},{10,14},{13,9},{14,10},{17,21},{18,... | collective-permute-start | bytes 1179656 | tf_op jit(solution)/shard_map/ppermute | solution.py:276
  18.8 0.1 stack.63.valid
  18.9 4.3 %collective-permute-start.6 = (bf16[2,768,128]{2,1,0:T(8,128)(2,1)S(1)}, bf16[2,768,128]{2,1,0:T(8,128)(2,1)S(1)}, u32[]{:S(2)}, u32[]{:S(2)}) collective-permute-start(bf16[2,768,128]{2,1,0:T(8,128)(2,1)S(1)} %collective-permute-done.refs_1_.refs_5_), channel_id=1, source_target_pairs={{5,9},{6,10},{9,5},{10,6},{21,25},{22,26},{25,21},{26,22}} | collective-permute-start | bytes 1179656 | tf_op jit(solution)/shard_map/ppermute | solution.py:276
  23.3 2.0 %row_stats.3 = (f32[2,7,2,256,256]{4,3,2,1,0:T(8,128)S(1)}, f32[3,8,768]{2,1,0:T(8,128)S(1)}) custom-call(s32[9]{0:T(128)S(1)} %stack.63.valid, bf16[2,768,128]{2,1,0:T(8,128)(2,1)S(1)} %pad_maximum_fusion.1.qg.refs_0_, bf16[2,768,128]{2,1,0:T(8,128)(2,1)S(1)} %pad_maximum_fusion.2.refs_0_.refs_3_.kv, ...), custom_call_target="tpu_custom_call" | custom-call | flops 301989888 | bytes 196608 | tf_op jit(solution)/shard_map/row_stats/pallas_call | solution.py:63
  25.3 2.8 %row_stats.4 = (f32[3,7,2,256,256]{4,3,2,1,0:T(8,128)S(1)}, f32[3,8,768]{2,1,0:T(8,128)S(1)}) custom-call(s32[9]{0:T(128)S(1)} %stack.63.valid, bf16[2,768,128]{2,1,0:T(8,128)(2,1)S(1)} %pad_maximum_fusion.1.qg.refs_0_, f32[3,8,768]{2,1,0:T(8,128)S(1)} %get-tuple-element.18.refs_0_, bf16[2,768,128]{2,1,0:T(8,128)(2,1)S(1)} %collective-permute-done.refs_1_.refs_5_, ...), custom_call_target="tpu_custom_call" | custom-call | flops 452984832 | bytes 294912 | tf_op jit(solution)/shard_map/row_stats/pallas_call | solution.py:63
  28.1 1.1 %pad_maximum_fusion = bf16[4,768,128]{2,1,0:T(8,128)(2,1)S(1)} fusion(bf16[2,768,128]{2,1,0:T(8,128)(2,1)S(1)} %collective-permute-done.1.refs_2_, bf16[1,768,128]{2,1,0:T(8,128)(2,1)} %bitcast.21, bf16[1,768,128]{2,1,0:T(8,128)(2,1)} %bitcast.23), kind=kLoop, calls=%fused_computation | loop fusion | flops 786432 | bytes 1572864 | tf_op jit(solution)/shard_map/concatenate | solution.py:309
  29.2 0.1 collective-permute-start.14
  29.3 1.9 %collective-permute-start.15 = (bf16[4,768,128]{2,1,0:T(8,128)(2,1)S(1)}, bf16[4,768,128]{2,1,0:T(8,128)(2,1)S(1)}, u32[]{:S(2)}, u32[]{:S(2)}) collective-permute-start(bf16[4,768,128]{2,1,0:T(8,128)(2,1)S(1)} %pad_maximum_fusion), channel_id=1, source_target_pairs={{4,8},{5,9},{6,10},{7,11},{8,4},{9,5},{10,6},{11,7},{20,24},{21,25... | collective-permute-start | bytes 2359304 | tf_op jit(solution)/shard_map/ppermute | solution.py:276
  31.2 0.1 collective-permute-start.7
  31.3 0.5 collective-permute-start.8
  31.8 0.1 collective-permute-start.13
  31.9 1.1 %collective-permute-done.7.refs_3_.refs_10_ = bf16[2,768,128]{2,1,0:T(8,128)(2,1)S(1)} collective-permute-done((bf16[2,768,128]{2,1,0:T(8,128)(2,1)S(1)}, bf16[2,768,128]{2,1,0:T(8,128)(2,1)S(1)}, u32[]{:S(2)}, u32[]{:S(2)}) %collective-permute-start.7) | collective-permute-done | bytes 393248 | tf_op jit(solution)/shard_map/ppermute | solution.py:250
  33.0 0.6 collective-permute-done.8.refs_4_.refs_11_
  33.6 3.6 %row_stats.5 = (f32[2,768]{1,0:T(2,128)S(1)}, f32[4,7,2,256,256]{4,3,2,1,0:T(8,128)S(1)}) custom-call(s32[9]{0:T(128)S(1)} %stack.63.valid, bf16[2,768,128]{2,1,0:T(8,128)(2,1)S(1)} %pad_maximum_fusion.1.qg.refs_0_, f32[3,8,768]{2,1,0:T(8,128)S(1)} %get-tuple-element.21.refs_0_, bf16[2,768,128]{2,1,0:T(8,128)(2,1)S(1)} %collective-permute-done.5.refs_1_.refs_8_, ...), custom_call_target="tpu_custom_call" | custom-call | flops 603979776 | bytes 393216 | tf_op jit(solution)/shard_map/row_stats/pallas_call | solution.py:63
  37.2 0.1 collective-permute-start.9
  37.3 2.8 %collective-permute-start.10 = (f32[2,768]{1,0:T(2,128)S(1)}, f32[2,768]{1,0:T(2,128)S(1)}, u32[]{:S(2)}, u32[]{:S(2)}) collective-permute-start(f32[2,768]{1,0:T(2,128)S(1)} %get-tuple-element.22.rows), channel_id=1, source_target_pairs={{1,2},{2,1},{5,6},{6,5},{9,10},{10,9},{13,14},{14,13},{17,18},{18,... | collective-permute-start | bytes 18440 | tf_op jit(solution)/shard_map/ppermute | solution.py:255
  40.1 5.6 %query_side.1 = bf16[768,128]{1,0:T(8,128)(2,1)} custom-call(s32[9]{0:T(128)S(1)} %stack.63.valid, f32[2,768]{1,0:T(2,128)S(1)} %get-tuple-element.22.rows, f32[2,7,2,256,256]{4,3,2,1,0:T(8,128)S(1)} %get-tuple-element.23.refs_0_, f32[3,7,2,256,256]{4,3,2,1,0:T(8,128)S(1)} %get-tuple-element.24.refs_1_, ...), custom_call_target="tpu_custom_call" | custom-call | flops 679477248 | bytes 884736 | tf_op jit(solution)/shard_map/query_side/pallas_call | solution.py:63
  45.7 3.6 %collective-permute-start.12 = (f32[3,2,768]{2,1,0:T(2,128)S(1)}, f32[3,2,768]{2,1,0:T(2,128)S(1)}, u32[]{:S(2)}, u32[]{:S(2)}) collective-permute-start(f32[3,2,768]{2,1,0:T(2,128)S(1)} %pad_maximum_fusion.4.rows), channel_id=1, source_target_pairs={{4,8},{5,9},{6,10},{7,11},{8,4},{9,5},{10,6},{11,7},{20,24},{21,25... | collective-permute-start | bytes 55304 | tf_op jit(solution)/shard_map/ppermute | solution.py:276
  49.4 4.0 %key_side.3.refs_0_ = f32[2,768,128]{2,1,0:T(8,128)S(1)} custom-call(s32[9]{0:T(128)S(1)} %stack.63.valid, bf16[2,768,128]{2,1,0:T(8,128)(2,1)S(1)} %pad_maximum_fusion.2.refs_0_.refs_3_.kv, f32[3,2,768]{2,1,0:T(2,128)S(1)} %pad_maximum_fusion.4.rows, bf16[2,768,128]{2,1,0:T(8,128)(2,1)S(1)} %pad_maximum_fusion.1.qg.refs_0_, ...), custom_call_target="tpu_custom_call" | custom-call | flops 905969664 | bytes 294912 | tf_op jit(solution)/shard_map/key_side/pallas_call | solution.py:63
  53.5 0.5 collective-permute-start.17
  54.1 5.4 %key_side.4.refs_0_ = f32[2,768,128]{2,1,0:T(8,128)S(1)} custom-call(s32[9]{0:T(128)S(1)} %stack.63.valid, bf16[2,768,128]{2,1,0:T(8,128)(2,1)S(1)} %pad_maximum_fusion.2.refs_0_.refs_3_.kv, f32[4,2,768]{2,1,0:T(2,128)S(1)} %pad_maximum_fusion.3.rows, f32[2,768,128]{2,1,0:T(8,128)S(1)} %key_side.3.refs_0_, ...), custom_call_target="tpu_custom_call" | custom-call | flops 1207959552 | bytes 393216 | tf_op jit(solution)/shard_map/key_side/pallas_call | solution.py:63
  59.5 3.7 %key_side.5 = (bf16[768,128]{1,0:T(8,128)(2,1)}, bf16[768,128]{1,0:T(8,128)(2,1)}) custom-call(s32[9]{0:T(128)S(1)} %stack.63.valid, bf16[2,768,128]{2,1,0:T(8,128)(2,1)S(1)} %pad_maximum_fusion.2.refs_0_.refs_3_.kv, f32[2,2,768]{2,1,0:T(2,128)S(1)} %pad_maximum_fusion.5.rows, f32[2,768,128]{2,1,0:T(8,128)S(1)} %key_side.4.refs_0_, ...), custom_call_target="tpu_custom_call" | custom-call | flops 603979776 | bytes 196608 | tf_op jit(solution)/shard_map/key_side/pallas_call | solution.py:63
  (25 shorter events, 0.3 us)
Async XLA Ops:
  3.9 9.5 %collective-permute-start = (bf16[2,768,128]{2,1,0:T(8,128)(2,1)S(1)}, bf16[2,768,128]{2,1,0:T(8,128)(2,1)S(1)}, u32[]{:S(2)}, u32[]{:S(2)}) collective-permute-start(bf16[2,768,128]{2,1,0:T(8,128)(2,1)S(1)} %pad_maximum_fusion.2.refs_0_.refs_3_.kv), channel_id=1, source_target_pairs={{1,2},{2,1},{5,6},{6,5},{9,10},{10,9},{13,14},{14,13},{17,18},{18,... | collective-permute-start | bytes 1179656 | tf_op jit(solution)/shard_map/ppermute | solution.py:255
  7.6 11.3 %collective-permute-start.2 = (bf16[2,768,128]{2,1,0:T(8,128)(2,1)S(1)}, bf16[2,768,128]{2,1,0:T(8,128)(2,1)S(1)}, u32[]{:S(2)}, u32[]{:S(2)}) collective-permute-start(bf16[2,768,128]{2,1,0:T(8,128)(2,1)S(1)} %pad_maximum_fusion.2.refs_0_.refs_3_.kv), channel_id=1, source_target_pairs={{0,1},{1,0},{2,3},{3,2},{4,5},{5,4},{6,7},{7,6},{8,9},{9,8},{10,11... | collective-permute-start | bytes 1179656 | tf_op jit(solution)/shard_map/ppermute | solution.py:250
  7.7 17.7 %collective-permute-start.3 = (bf16[2,768,128]{2,1,0:T(8,128)(2,1)S(1)}, bf16[2,768,128]{2,1,0:T(8,128)(2,1)S(1)}, u32[]{:S(2)}, u32[]{:S(2)}) collective-permute-start(bf16[2,768,128]{2,1,0:T(8,128)(2,1)S(1)} %pad_maximum_fusion.2.refs_0_.refs_3_.kv), channel_id=1, source_target_pairs={{0,4},{1,5},{2,6},{3,7},{4,0},{5,1},{6,2},{7,3},{8,12},{9,13},{10,... | collective-permute-start | bytes 1179656 | tf_op jit(solution)/shard_map/ppermute | solution.py:276
  7.9 17.4 %collective-permute-start.4 = (bf16[2,768,128]{2,1,0:T(8,128)(2,1)S(1)}, bf16[2,768,128]{2,1,0:T(8,128)(2,1)S(1)}, u32[]{:S(2)}, u32[]{:S(2)}) collective-permute-start(bf16[2,768,128]{2,1,0:T(8,128)(2,1)S(1)} %pad_maximum_fusion.2.refs_0_.refs_3_.kv), channel_id=1, source_target_pairs={{4,8},{5,9},{6,10},{7,11},{8,4},{9,5},{10,6},{11,7},{20,24},{21,25... | collective-permute-start | bytes 1179656 | tf_op jit(solution)/shard_map/ppermute | solution.py:276
  13.3 14.8 %collective-permute-start.1 = (bf16[2,768,128]{2,1,0:T(8,128)(2,1)S(1)}, bf16[2,768,128]{2,1,0:T(8,128)(2,1)S(1)}, u32[]{:S(2)}, u32[]{:S(2)}) collective-permute-start(bf16[2,768,128]{2,1,0:T(8,128)(2,1)S(1)} %pad_maximum_fusion.1.qg.refs_0_), channel_id=1, source_target_pairs={{1,2},{2,1},{5,6},{6,5},{9,10},{10,9},{13,14},{14,13},{17,18},{18,... | collective-permute-start | bytes 1179656 | tf_op jit(solution)/shard_map/ppermute | solution.py:255
  16.7 14.7 %collective-permute-start.5 = (bf16[2,768,128]{2,1,0:T(8,128)(2,1)S(1)}, bf16[2,768,128]{2,1,0:T(8,128)(2,1)S(1)}, u32[]{:S(2)}, u32[]{:S(2)}) collective-permute-start(bf16[2,768,128]{2,1,0:T(8,128)(2,1)S(1)} %collective-permute-done.refs_1_.refs_5_), channel_id=1, source_target_pairs={{1,5},{2,6},{5,1},{6,2},{9,13},{10,14},{13,9},{14,10},{17,21},{18,... | collective-permute-start | bytes 1179656 | tf_op jit(solution)/shard_map/ppermute | solution.py:276
  18.9 12.9 %collective-permute-start.6 = (bf16[2,768,128]{2,1,0:T(8,128)(2,1)S(1)}, bf16[2,768,128]{2,1,0:T(8,128)(2,1)S(1)}, u32[]{:S(2)}, u32[]{:S(2)}) collective-permute-start(bf16[2,768,128]{2,1,0:T(8,128)(2,1)S(1)} %collective-permute-done.refs_1_.refs_5_), channel_id=1, source_target_pairs={{5,9},{6,10},{9,5},{10,6},{21,25},{22,26},{25,21},{26,22}} | collective-permute-start | bytes 1179656 | tf_op jit(solution)/shard_map/ppermute | solution.py:276
  29.2 24.2 %collective-permute-start.14 = (bf16[4,768,128]{2,1,0:T(8,128)(2,1)S(1)}, bf16[4,768,128]{2,1,0:T(8,128)(2,1)S(1)}, u32[]{:S(2)}, u32[]{:S(2)}) collective-permute-start(bf16[4,768,128]{2,1,0:T(8,128)(2,1)S(1)} %pad_maximum_fusion), channel_id=1, source_target_pairs={{0,4},{1,5},{2,6},{3,7},{4,0},{5,1},{6,2},{7,3},{8,12},{9,13},{10,... | collective-permute-start | bytes 2359304 | tf_op jit(solution)/shard_map/ppermute | solution.py:276
  29.3 24.2 %collective-permute-start.15 = (bf16[4,768,128]{2,1,0:T(8,128)(2,1)S(1)}, bf16[4,768,128]{2,1,0:T(8,128)(2,1)S(1)}, u32[]{:S(2)}, u32[]{:S(2)}) collective-permute-start(bf16[4,768,128]{2,1,0:T(8,128)(2,1)S(1)} %pad_maximum_fusion), channel_id=1, source_target_pairs={{4,8},{5,9},{6,10},{7,11},{8,4},{9,5},{10,6},{11,7},{20,24},{21,25... | collective-permute-start | bytes 2359304 | tf_op jit(solution)/shard_map/ppermute | solution.py:276
  31.2 1.8 %collective-permute-start.7 = (bf16[2,768,128]{2,1,0:T(8,128)(2,1)S(1)}, bf16[2,768,128]{2,1,0:T(8,128)(2,1)S(1)}, u32[]{:S(2)}, u32[]{:S(2)}) collective-permute-start(bf16[2,768,128]{2,1,0:T(8,128)(2,1)S(1)} %collective-permute-done.3.refs_2_.refs_6_), channel_id=1, source_target_pairs={{0,1},{1,0},{2,3},{3,2},{4,5},{5,4},{6,7},{7,6},{8,9},{9,8},{10,11... | collective-permute-start | bytes 1179656 | tf_op jit(solution)/shard_map/ppermute | solution.py:250
  31.3 2.3 %collective-permute-start.8 = (bf16[2,768,128]{2,1,0:T(8,128)(2,1)S(1)}, bf16[2,768,128]{2,1,0:T(8,128)(2,1)S(1)}, u32[]{:S(2)}, u32[]{:S(2)}) collective-permute-start(bf16[2,768,128]{2,1,0:T(8,128)(2,1)S(1)} %collective-permute-done.4.refs_3_.refs_7_), channel_id=1, source_target_pairs={{0,1},{1,0},{2,3},{3,2},{4,5},{5,4},{6,7},{7,6},{8,9},{9,8},{10,11... | collective-permute-start | bytes 1179656 | tf_op jit(solution)/shard_map/ppermute | solution.py:250
  31.8 17.6 %collective-permute-start.13 = (bf16[2,768,128]{2,1,0:T(8,128)(2,1)S(1)}, bf16[2,768,128]{2,1,0:T(8,128)(2,1)S(1)}, u32[]{:S(2)}, u32[]{:S(2)}) collective-permute-start(bf16[2,768,128]{2,1,0:T(8,128)(2,1)S(1)} %pad_maximum_fusion.1.qg.refs_0_), channel_id=1, source_target_pairs={{0,1},{1,0},{2,3},{3,2},{4,5},{5,4},{6,7},{7,6},{8,9},{9,8},{10,11... | collective-permute-start | bytes 1179656 | tf_op jit(solution)/shard_map/ppermute | solution.py:250
  37.2 8.4 %collective-permute-start.9 = (f32[2,768]{1,0:T(2,128)S(1)}, f32[2,768]{1,0:T(2,128)S(1)}, u32[]{:S(2)}, u32[]{:S(2)}) collective-permute-start(f32[2,768]{1,0:T(2,128)S(1)} %get-tuple-element.22.rows), channel_id=1, source_target_pairs={{0,1},{1,0},{2,3},{3,2},{4,5},{5,4},{6,7},{7,6},{8,9},{9,8},{10,11... | collective-permute-start | bytes 18440 | tf_op jit(solution)/shard_map/ppermute | solution.py:250
  37.3 8.4 %collective-permute-start.10 = (f32[2,768]{1,0:T(2,128)S(1)}, f32[2,768]{1,0:T(2,128)S(1)}, u32[]{:S(2)}, u32[]{:S(2)}) collective-permute-start(f32[2,768]{1,0:T(2,128)S(1)} %get-tuple-element.22.rows), channel_id=1, source_target_pairs={{1,2},{2,1},{5,6},{6,5},{9,10},{10,9},{13,14},{14,13},{17,18},{18,... | collective-permute-start | bytes 18440 | tf_op jit(solution)/shard_map/ppermute | solution.py:255
  45.7 8.4 %collective-permute-start.11 = (f32[3,2,768]{2,1,0:T(2,128)S(1)}, f32[3,2,768]{2,1,0:T(2,128)S(1)}, u32[]{:S(2)}, u32[]{:S(2)}) collective-permute-start(f32[3,2,768]{2,1,0:T(2,128)S(1)} %pad_maximum_fusion.4.rows), channel_id=1, source_target_pairs={{0,4},{1,5},{2,6},{3,7},{4,0},{5,1},{6,2},{7,3},{8,12},{9,13},{10,... | collective-permute-start | bytes 55304 | tf_op jit(solution)/shard_map/ppermute | solution.py:276
  45.7 8.3 %collective-permute-start.12 = (f32[3,2,768]{2,1,0:T(2,128)S(1)}, f32[3,2,768]{2,1,0:T(2,128)S(1)}, u32[]{:S(2)}, u32[]{:S(2)}) collective-permute-start(f32[3,2,768]{2,1,0:T(2,128)S(1)} %pad_maximum_fusion.4.rows), channel_id=1, source_target_pairs={{4,8},{5,9},{6,10},{7,11},{8,4},{9,5},{10,6},{11,7},{20,24},{21,25... | collective-permute-start | bytes 55304 | tf_op jit(solution)/shard_map/ppermute | solution.py:276
  53.4 6.0 %collective-permute-start.16 = (bf16[4,768,128]{2,1,0:T(8,128)(2,1)S(1)}, bf16[4,768,128]{2,1,0:T(8,128)(2,1)S(1)}, u32[]{:S(2)}, u32[]{:S(2)}) collective-permute-start(bf16[4,768,128]{2,1,0:T(8,128)(2,1)S(1)} %collective-permute-done.14.refs_1_), channel_id=1, source_target_pairs={{0,1},{1,0},{2,3},{3,2},{4,5},{5,4},{6,7},{7,6},{8,9},{9,8},{10,11... | collective-permute-start | bytes 2359304 | tf_op jit(solution)/shard_map/ppermute | solution.py:250
  53.5 5.9 %collective-permute-start.17 = (bf16[4,768,128]{2,1,0:T(8,128)(2,1)S(1)}, bf16[4,768,128]{2,1,0:T(8,128)(2,1)S(1)}, u32[]{:S(2)}, u32[]{:S(2)}) collective-permute-start(bf16[4,768,128]{2,1,0:T(8,128)(2,1)S(1)} %collective-permute-done.15.refs_2_), channel_id=1, source_target_pairs={{0,1},{1,0},{2,3},{3,2},{4,5},{5,4},{6,7},{7,6},{8,9},{9,8},{10,11... | collective-permute-start | bytes 2359304 | tf_op jit(solution)/shard_map/ppermute | solution.py:250

commit v6 on v5

--- a/solution.py
+++ b/solution.py
@@ -301,7 +301,8 @@
 
     kv_near = [(kv, 0), (kv_mate, 0)]
     kv_next = [(kv_cross, 0), (kv_a, 0), (kv_b, 0)]
-    kv_last = [(kv_cross_a, 0), (kv_cross_b, 0), (kv_mate_a, 0), (kv_mate_b, 0)]
+    kv_third = [(kv_cross_a, 0), (kv_cross_b, 0)]
+    kv_last = [(kv_mate_a, 0), (kv_mate_b, 0)]
     running, kept_near = stats(valid, 0, qg, kv_near, None, False)
 
     running, kept_next = stats(valid, 2, qg, kv_next, running, False)
@@ -313,10 +314,13 @@
     qg_mate_a = swap_mate(qg_a)
     qg_mate_b = swap_mate(qg_b)
 
-    rows, kept_last = stats(valid, 5, qg, kv_last, running, True)
+    running, kept_third = stats(valid, 5, qg, kv_third, running, False)
+    rows, kept_last = stats(valid, 7, qg, kv_last, running, True)
 
     trio = jnp.stack([rows, swap_mate(rows), swap_cross(rows)])
-    query_grad = query_side(valid, kv_near + kv_next + kv_last, [kept_near, kept_next, kept_last], rows)
+    query_grad = query_side(
+        valid, kv_near + kv_next + kv_third + kv_last, [kept_near, kept_next, kept_third, kept_last], rows
+    )
     trio, query_grad = lax.optimization_barrier((trio, query_grad))
     trio_a = swap_frames(trio, 0)
     trio_b = swap_frames(trio, 1)

time: 63.6 us -> 62.4 us (0.981)
  waiting for transfers between devices: 1.76 us -> 0.08 us
    ppermute x7, waiting for transfers between devices: 1.69 us -> 0.02 us  [swap_mate(): lax.ppermute(value, 'tm', [(source, source ^ 1) for source in range(count)])]
    pallas_call x7 -> x8, Pallas kernels: 27.1 us -> 27.6 us  [vmem_call(): pl.pallas_call(kernel, in_specs=[pl.BlockSpec(memory_space=pltpu.SMEM)] +...]
  transfers between devices with their start and end apart: 18 -> 18, of which waited for: 2 -> 0; matrix products, arithmetic and copies ran while one was open for 4% -> 4% of each run, Pallas kernels for 37% -> 39%
where the time goes in v6:
time: 62.4 us; the launch traced here: 62 us
  starting transfers between devices  27.8 us (45%)
  Pallas kernels  27.6 us (44%)
  other arithmetic  5.33 us (9%)
  between operations  1.01 us (2%)
    pallas_call x8, Pallas kernels, vmem_call(): pl.pallas_call(kernel, in_specs=[pl.BlockSpec(memory_space=pltpu.SMEM)] +...  27.6 us
    ppermute x8, starting transfers between devices, swap_frames(): return lax.ppermute(value, 'tm', pairs)  16.7 us
    ppermute x3, starting transfers between devices, swap_cross(): lax.ppermute(value, 'tm', [(s, cross_of(s)) for s in range(count) if has_...  9.82 us
    convert_element_type x2, other arithmetic, scaled(): return (blocked * picked[:, None, None]).astype(BF16).reshape(tokens, dim)  2.2 us
    ppermute x7, starting transfers between devices, swap_mate(): lax.ppermute(value, 'tm', [(source, source ^ 1) for source in range(count)])  1.35 us
  transfers between devices with their start and end apart: 18, of which 0 were waited for; matrix products, arithmetic and copies ran while one was open for 4% of the time, Pallas kernels for 39%

profile of v6, /device:TPU:11, one launch (start us, length us, event | category | flops | bytes accessed | tf_op | source)
XLA Modules:
  0.0 62.0 jit_solution(16470416521479211725)
XLA Ops:
  0.6 0.9 %select_reduce_fusion.1 = (f32[6]{0:T(128)S(1)}, f32[6]{0:T(128)S(1)}) fusion(f32[6]{0:T(128)} %param.10, s32[6]{0:T(128)} %bitcast.26, f32[6]{0:T(128)} %param.11), kind=kLoop, calls=%fused_computation.11 | loop fusion | flops 168 | bytes 120 | tf_op jit(solution)/shard_map/reduce_sum | solution.py:52
  1.5 0.1 broadcast_bitcast_fusion
  1.6 1.1 %fusion = bf16[1,768,128]{2,1,0:T(8,128)(2,1)S(1)} fusion(bf16[768,128]{1,0:T(8,128)(2,1)} %param.8, f32[768]{0:T(1024)S(1)} %get-tuple-element.44), kind=kLoop, calls=%fused_computation.5 | loop fusion | flops 294912 | bytes 396288 | tf_op jit(solution)/shard_map/convert_element_type | solution.py:54
  2.7 1.1 %fusion.1 = bf16[1,768,128]{2,1,0:T(8,128)(2,1)S(1)} fusion(bf16[768,128]{1,0:T(8,128)(2,1)} %param.9, f32[768]{0:T(1024)S(1)} %get-tuple-element.43), kind=kLoop, calls=%fused_computation.6 | loop fusion | flops 294912 | bytes 396288 | tf_op jit(solution)/shard_map/convert_element_type | solution.py:54
  3.9 3.7 %collective-permute-start = (bf16[2,768,128]{2,1,0:T(8,128)(2,1)S(1)}, bf16[2,768,128]{2,1,0:T(8,128)(2,1)S(1)}, u32[]{:S(2)}, u32[]{:S(2)}) collective-permute-start(bf16[2,768,128]{2,1,0:T(8,128)(2,1)S(1)} %pad_maximum_fusion.2.refs_0_.refs_4_.kv), channel_id=1, source_target_pairs={{1,2},{2,1},{5,6},{6,5},{9,10},{10,9},{13,14},{14,13},{17,18},{18,... | collective-permute-start | bytes 1179656 | tf_op jit(solution)/shard_map/ppermute | solution.py:255
  7.6 0.1 collective-permute-start.2
  7.7 0.2 collective-permute-start.3
  7.9 4.3 %collective-permute-start.4 = (bf16[2,768,128]{2,1,0:T(8,128)(2,1)S(1)}, bf16[2,768,128]{2,1,0:T(8,128)(2,1)S(1)}, u32[]{:S(2)}, u32[]{:S(2)}) collective-permute-start(bf16[2,768,128]{2,1,0:T(8,128)(2,1)S(1)} %pad_maximum_fusion.2.refs_0_.refs_4_.kv), channel_id=1, source_target_pairs={{4,8},{5,9},{6,10},{7,11},{8,4},{9,5},{10,6},{11,7},{20,24},{21,25... | collective-permute-start | bytes 1179656 | tf_op jit(solution)/shard_map/ppermute | solution.py:276
  12.2 1.1 %pad_maximum_fusion.1.qg.refs_0_ = bf16[2,768,128]{2,1,0:T(8,128)(2,1)S(1)} fusion(bf16[1,768,128]{2,1,0:T(8,128)(2,1)} %bitcast.20, bf16[1,768,128]{2,1,0:T(8,128)(2,1)} %bitcast.22), kind=kLoop, calls=%fused_computation.1 | loop fusion | flops 196608 | bytes 786432 | tf_op jit(solution)/shard_map/stack | solution.py:57
  13.3 3.3 %collective-permute-start.1 = (bf16[2,768,128]{2,1,0:T(8,128)(2,1)S(1)}, bf16[2,768,128]{2,1,0:T(8,128)(2,1)S(1)}, u32[]{:S(2)}, u32[]{:S(2)}) collective-permute-start(bf16[2,768,128]{2,1,0:T(8,128)(2,1)S(1)} %pad_maximum_fusion.1.qg.refs_0_), channel_id=1, source_target_pairs={{1,2},{2,1},{5,6},{6,5},{9,10},{10,9},{13,14},{14,13},{17,18},{18,... | collective-permute-start | bytes 1179656 | tf_op jit(solution)/shard_map/ppermute | solution.py:255
  16.7 2.1 %collective-permute-start.5 = (bf16[2,768,128]{2,1,0:T(8,128)(2,1)S(1)}, bf16[2,768,128]{2,1,0:T(8,128)(2,1)S(1)}, u32[]{:S(2)}, u32[]{:S(2)}) collective-permute-start(bf16[2,768,128]{2,1,0:T(8,128)(2,1)S(1)} %collective-permute-done.refs_1_.refs_6_), channel_id=1, source_target_pairs={{1,5},{2,6},{5,1},{6,2},{9,13},{10,14},{13,9},{14,10},{17,21},{18,... | collective-permute-start | bytes 1179656 | tf_op jit(solution)/shard_map/ppermute | solution.py:276
  18.8 0.1 stack.63.valid
  18.9 4.3 %collective-permute-start.6 = (bf16[2,768,128]{2,1,0:T(8,128)(2,1)S(1)}, bf16[2,768,128]{2,1,0:T(8,128)(2,1)S(1)}, u32[]{:S(2)}, u32[]{:S(2)}) collective-permute-start(bf16[2,768,128]{2,1,0:T(8,128)(2,1)S(1)} %collective-permute-done.refs_1_.refs_6_), channel_id=1, source_target_pairs={{5,9},{6,10},{9,5},{10,6},{21,25},{22,26},{25,21},{26,22}} | collective-permute-start | bytes 1179656 | tf_op jit(solution)/shard_map/ppermute | solution.py:276
  23.3 2.0 %row_stats.4 = (f32[2,7,2,256,256]{4,3,2,1,0:T(8,128)S(1)}, f32[3,8,768]{2,1,0:T(8,128)S(1)}) custom-call(s32[9]{0:T(128)S(1)} %stack.63.valid, bf16[2,768,128]{2,1,0:T(8,128)(2,1)S(1)} %pad_maximum_fusion.1.qg.refs_0_, bf16[2,768,128]{2,1,0:T(8,128)(2,1)S(1)} %pad_maximum_fusion.2.refs_0_.refs_4_.kv, ...), custom_call_target="tpu_custom_call" | custom-call | flops 301989888 | bytes 196608 | tf_op jit(solution)/shard_map/row_stats/pallas_call | solution.py:63
  25.3 2.8 %row_stats.5 = (f32[3,7,2,256,256]{4,3,2,1,0:T(8,128)S(1)}, f32[3,8,768]{2,1,0:T(8,128)S(1)}) custom-call(s32[9]{0:T(128)S(1)} %stack.63.valid, bf16[2,768,128]{2,1,0:T(8,128)(2,1)S(1)} %pad_maximum_fusion.1.qg.refs_0_, f32[3,8,768]{2,1,0:T(8,128)S(1)} %get-tuple-element.20.refs_0_, bf16[2,768,128]{2,1,0:T(8,128)(2,1)S(1)} %collective-permute-done.refs_1_.refs_6_, ...), custom_call_target="tpu_custom_call" | custom-call | flops 452984832 | bytes 294912 | tf_op jit(solution)/shard_map/row_stats/pallas_call | solution.py:63
  28.1 1.1 %pad_maximum_fusion = bf16[4,768,128]{2,1,0:T(8,128)(2,1)S(1)} fusion(bf16[2,768,128]{2,1,0:T(8,128)(2,1)S(1)} %collective-permute-done.1.refs_2_, bf16[1,768,128]{2,1,0:T(8,128)(2,1)} %bitcast.21, bf16[1,768,128]{2,1,0:T(8,128)(2,1)} %bitcast.23), kind=kLoop, calls=%fused_computation | loop fusion | flops 786432 | bytes 1572864 | tf_op jit(solution)/shard_map/concatenate | solution.py:310
  29.2 0.1 collective-permute-start.14
  29.3 1.9 %collective-permute-start.15 = (bf16[4,768,128]{2,1,0:T(8,128)(2,1)S(1)}, bf16[4,768,128]{2,1,0:T(8,128)(2,1)S(1)}, u32[]{:S(2)}, u32[]{:S(2)}) collective-permute-start(bf16[4,768,128]{2,1,0:T(8,128)(2,1)S(1)} %pad_maximum_fusion), channel_id=1, source_target_pairs={{4,8},{5,9},{6,10},{7,11},{8,4},{9,5},{10,6},{11,7},{20,24},{21,25... | collective-permute-start | bytes 2359304 | tf_op jit(solution)/shard_map/ppermute | solution.py:276
  31.3 0.5 collective-permute-start.8
  31.8 0.1 collective-permute-start.13
  31.9 2.0 %row_stats.6 = (f32[2,7,2,256,256]{4,3,2,1,0:T(8,128)S(1)}, f32[3,8,768]{2,1,0:T(8,128)S(1)}) custom-call(s32[9]{0:T(128)S(1)} %stack.63.valid, bf16[2,768,128]{2,1,0:T(8,128)(2,1)S(1)} %pad_maximum_fusion.1.qg.refs_0_, f32[3,8,768]{2,1,0:T(8,128)S(1)} %get-tuple-element.23.refs_0_, bf16[2,768,128]{2,1,0:T(8,128)(2,1)S(1)} %collective-permute-done.5.refs_1_.refs_9_, ...), custom_call_target="tpu_custom_call" | custom-call | flops 301989888 | bytes 196608 | tf_op jit(solution)/shard_map/row_stats/pallas_call | solution.py:63
  34.0 2.1 %row_stats.7 = (f32[2,768]{1,0:T(2,128)S(1)}, f32[2,7,2,256,256]{4,3,2,1,0:T(8,128)S(1)}) custom-call(s32[9]{0:T(128)S(1)} %stack.63.valid, bf16[2,768,128]{2,1,0:T(8,128)(2,1)S(1)} %pad_maximum_fusion.1.qg.refs_0_, f32[3,8,768]{2,1,0:T(8,128)S(1)} %get-tuple-element.24.refs_0_, bf16[2,768,128]{2,1,0:T(8,128)(2,1)S(1)} %collective-permute-done.7.refs_1_.refs_11_, ...), custom_call_target="tpu_custom_call" | custom-call | flops 301989888 | bytes 196608 | tf_op jit(solution)/shard_map/row_stats/pallas_call | solution.py:63
  36.1 0.1 collective-permute-start.9
  36.2 2.8 %collective-permute-start.10 = (f32[2,768]{1,0:T(2,128)S(1)}, f32[2,768]{1,0:T(2,128)S(1)}, u32[]{:S(2)}, u32[]{:S(2)}) collective-permute-start(f32[2,768]{1,0:T(2,128)S(1)} %get-tuple-element.25.rows), channel_id=1, source_target_pairs={{1,2},{2,1},{5,6},{6,5},{9,10},{10,9},{13,14},{14,13},{17,18},{18,... | collective-permute-start | bytes 18440 | tf_op jit(solution)/shard_map/ppermute | solution.py:255
  38.9 5.5 %query_side.1 = bf16[768,128]{1,0:T(8,128)(2,1)} custom-call(s32[9]{0:T(128)S(1)} %stack.63.valid, f32[2,768]{1,0:T(2,128)S(1)} %get-tuple-element.25.rows, f32[2,7,2,256,256]{4,3,2,1,0:T(8,128)S(1)} %get-tuple-element.26.refs_0_, f32[3,7,2,256,256]{4,3,2,1,0:T(8,128)S(1)} %get-tuple-element.27.refs_1_, ...), custom_call_target="tpu_custom_call" | custom-call | flops 679477248 | bytes 884736 | tf_op jit(solution)/shard_map/query_side/pallas_call | solution.py:63
  44.5 0.1 collective-permute-start.11
  44.6 3.6 %collective-permute-start.12 = (f32[3,2,768]{2,1,0:T(2,128)S(1)}, f32[3,2,768]{2,1,0:T(2,128)S(1)}, u32[]{:S(2)}, u32[]{:S(2)}) collective-permute-start(f32[3,2,768]{2,1,0:T(2,128)S(1)} %pad_maximum_fusion.4.rows), channel_id=1, source_target_pairs={{4,8},{5,9},{6,10},{7,11},{8,4},{9,5},{10,6},{11,7},{20,24},{21,25... | collective-permute-start | bytes 55304 | tf_op jit(solution)/shard_map/ppermute | solution.py:276
  48.2 4.0 %key_side.3.refs_0_ = f32[2,768,128]{2,1,0:T(8,128)S(1)} custom-call(s32[9]{0:T(128)S(1)} %stack.63.valid, bf16[2,768,128]{2,1,0:T(8,128)(2,1)S(1)} %pad_maximum_fusion.2.refs_0_.refs_4_.kv, f32[3,2,768]{2,1,0:T(2,128)S(1)} %pad_maximum_fusion.4.rows, bf16[2,768,128]{2,1,0:T(8,128)(2,1)S(1)} %pad_maximum_fusion.1.qg.refs_0_, ...), custom_call_target="tpu_custom_call" | custom-call | flops 905969664 | bytes 294912 | tf_op jit(solution)/shard_map/key_side/pallas_call | solution.py:63
  52.3 0.1 collective-permute-start.16
  52.4 0.5 collective-permute-start.17
  52.9 5.3 %key_side.4.refs_0_ = f32[2,768,128]{2,1,0:T(8,128)S(1)} custom-call(s32[9]{0:T(128)S(1)} %stack.63.valid, bf16[2,768,128]{2,1,0:T(8,128)(2,1)S(1)} %pad_maximum_fusion.2.refs_0_.refs_4_.kv, f32[4,2,768]{2,1,0:T(2,128)S(1)} %pad_maximum_fusion.3.rows, f32[2,768,128]{2,1,0:T(8,128)S(1)} %key_side.3.refs_0_, ...), custom_call_target="tpu_custom_call" | custom-call | flops 1207959552 | bytes 393216 | tf_op jit(solution)/shard_map/key_side/pallas_call | solution.py:63
  58.3 3.7 %key_side.5 = (bf16[768,128]{1,0:T(8,128)(2,1)}, bf16[768,128]{1,0:T(8,128)(2,1)}) custom-call(s32[9]{0:T(128)S(1)} %stack.63.valid, bf16[2,768,128]{2,1,0:T(8,128)(2,1)S(1)} %pad_maximum_fusion.2.refs_0_.refs_4_.kv, f32[2,2,768]{2,1,0:T(2,128)S(1)} %pad_maximum_fusion.5.rows, f32[2,768,128]{2,1,0:T(8,128)S(1)} %key_side.4.refs_0_, ...), custom_call_target="tpu_custom_call" | custom-call | flops 603979776 | bytes 196608 | tf_op jit(solution)/shard_map/key_side/pallas_call | solution.py:63
  (26 shorter events, 0.2 us)
Async XLA Ops:
  3.9 9.5 %collective-permute-start = (bf16[2,768,128]{2,1,0:T(8,128)(2,1)S(1)}, bf16[2,768,128]{2,1,0:T(8,128)(2,1)S(1)}, u32[]{:S(2)}, u32[]{:S(2)}) collective-permute-start(bf16[2,768,128]{2,1,0:T(8,128)(2,1)S(1)} %pad_maximum_fusion.2.refs_0_.refs_4_.kv), channel_id=1, source_target_pairs={{1,2},{2,1},{5,6},{6,5},{9,10},{10,9},{13,14},{14,13},{17,18},{18,... | collective-permute-start | bytes 1179656 | tf_op jit(solution)/shard_map/ppermute | solution.py:255
  7.6 11.3 %collective-permute-start.2 = (bf16[2,768,128]{2,1,0:T(8,128)(2,1)S(1)}, bf16[2,768,128]{2,1,0:T(8,128)(2,1)S(1)}, u32[]{:S(2)}, u32[]{:S(2)}) collective-permute-start(bf16[2,768,128]{2,1,0:T(8,128)(2,1)S(1)} %pad_maximum_fusion.2.refs_0_.refs_4_.kv), channel_id=1, source_target_pairs={{0,1},{1,0},{2,3},{3,2},{4,5},{5,4},{6,7},{7,6},{8,9},{9,8},{10,11... | collective-permute-start | bytes 1179656 | tf_op jit(solution)/shard_map/ppermute | solution.py:250
  7.7 17.7 %collective-permute-start.3 = (bf16[2,768,128]{2,1,0:T(8,128)(2,1)S(1)}, bf16[2,768,128]{2,1,0:T(8,128)(2,1)S(1)}, u32[]{:S(2)}, u32[]{:S(2)}) collective-permute-start(bf16[2,768,128]{2,1,0:T(8,128)(2,1)S(1)} %pad_maximum_fusion.2.refs_0_.refs_4_.kv), channel_id=1, source_target_pairs={{0,4},{1,5},{2,6},{3,7},{4,0},{5,1},{6,2},{7,3},{8,12},{9,13},{10,... | collective-permute-start | bytes 1179656 | tf_op jit(solution)/shard_map/ppermute | solution.py:276
  7.9 17.4 %collective-permute-start.4 = (bf16[2,768,128]{2,1,0:T(8,128)(2,1)S(1)}, bf16[2,768,128]{2,1,0:T(8,128)(2,1)S(1)}, u32[]{:S(2)}, u32[]{:S(2)}) collective-permute-start(bf16[2,768,128]{2,1,0:T(8,128)(2,1)S(1)} %pad_maximum_fusion.2.refs_0_.refs_4_.kv), channel_id=1, source_target_pairs={{4,8},{5,9},{6,10},{7,11},{8,4},{9,5},{10,6},{11,7},{20,24},{21,25... | collective-permute-start | bytes 1179656 | tf_op jit(solution)/shard_map/ppermute | solution.py:276
  13.3 14.8 %collective-permute-start.1 = (bf16[2,768,128]{2,1,0:T(8,128)(2,1)S(1)}, bf16[2,768,128]{2,1,0:T(8,128)(2,1)S(1)}, u32[]{:S(2)}, u32[]{:S(2)}) collective-permute-start(bf16[2,768,128]{2,1,0:T(8,128)(2,1)S(1)} %pad_maximum_fusion.1.qg.refs_0_), channel_id=1, source_target_pairs={{1,2},{2,1},{5,6},{6,5},{9,10},{10,9},{13,14},{14,13},{17,18},{18,... | collective-permute-start | bytes 1179656 | tf_op jit(solution)/shard_map/ppermute | solution.py:255
  16.7 14.7 %collective-permute-start.5 = (bf16[2,768,128]{2,1,0:T(8,128)(2,1)S(1)}, bf16[2,768,128]{2,1,0:T(8,128)(2,1)S(1)}, u32[]{:S(2)}, u32[]{:S(2)}) collective-permute-start(bf16[2,768,128]{2,1,0:T(8,128)(2,1)S(1)} %collective-permute-done.refs_1_.refs_6_), channel_id=1, source_target_pairs={{1,5},{2,6},{5,1},{6,2},{9,13},{10,14},{13,9},{14,10},{17,21},{18,... | collective-permute-start | bytes 1179656 | tf_op jit(solution)/shard_map/ppermute | solution.py:276
  18.9 12.9 %collective-permute-start.6 = (bf16[2,768,128]{2,1,0:T(8,128)(2,1)S(1)}, bf16[2,768,128]{2,1,0:T(8,128)(2,1)S(1)}, u32[]{:S(2)}, u32[]{:S(2)}) collective-permute-start(bf16[2,768,128]{2,1,0:T(8,128)(2,1)S(1)} %collective-permute-done.refs_1_.refs_6_), channel_id=1, source_target_pairs={{5,9},{6,10},{9,5},{10,6},{21,25},{22,26},{25,21},{26,22}} | collective-permute-start | bytes 1179656 | tf_op jit(solution)/shard_map/ppermute | solution.py:276
  29.2 23.1 %collective-permute-start.14 = (bf16[4,768,128]{2,1,0:T(8,128)(2,1)S(1)}, bf16[4,768,128]{2,1,0:T(8,128)(2,1)S(1)}, u32[]{:S(2)}, u32[]{:S(2)}) collective-permute-start(bf16[4,768,128]{2,1,0:T(8,128)(2,1)S(1)} %pad_maximum_fusion), channel_id=1, source_target_pairs={{0,4},{1,5},{2,6},{3,7},{4,0},{5,1},{6,2},{7,3},{8,12},{9,13},{10,... | collective-permute-start | bytes 2359304 | tf_op jit(solution)/shard_map/ppermute | solution.py:276
  29.3 23.1 %collective-permute-start.15 = (bf16[4,768,128]{2,1,0:T(8,128)(2,1)S(1)}, bf16[4,768,128]{2,1,0:T(8,128)(2,1)S(1)}, u32[]{:S(2)}, u32[]{:S(2)}) collective-permute-start(bf16[4,768,128]{2,1,0:T(8,128)(2,1)S(1)} %pad_maximum_fusion), channel_id=1, source_target_pairs={{4,8},{5,9},{6,10},{7,11},{8,4},{9,5},{10,6},{11,7},{20,24},{21,25... | collective-permute-start | bytes 2359304 | tf_op jit(solution)/shard_map/ppermute | solution.py:276
  31.2 2.7 %collective-permute-start.7 = (bf16[2,768,128]{2,1,0:T(8,128)(2,1)S(1)}, bf16[2,768,128]{2,1,0:T(8,128)(2,1)S(1)}, u32[]{:S(2)}, u32[]{:S(2)}) collective-permute-start(bf16[2,768,128]{2,1,0:T(8,128)(2,1)S(1)} %collective-permute-done.3.refs_2_.refs_7_), channel_id=1, source_target_pairs={{0,1},{1,0},{2,3},{3,2},{4,5},{5,4},{6,7},{7,6},{8,9},{9,8},{10,11... | collective-permute-start | bytes 1179656 | tf_op jit(solution)/shard_map/ppermute | solution.py:250
  31.3 2.6 %collective-permute-start.8 = (bf16[2,768,128]{2,1,0:T(8,128)(2,1)S(1)}, bf16[2,768,128]{2,1,0:T(8,128)(2,1)S(1)}, u32[]{:S(2)}, u32[]{:S(2)}) collective-permute-start(bf16[2,768,128]{2,1,0:T(8,128)(2,1)S(1)} %collective-permute-done.4.refs_3_.refs_8_), channel_id=1, source_target_pairs={{0,1},{1,0},{2,3},{3,2},{4,5},{5,4},{6,7},{7,6},{8,9},{9,8},{10,11... | collective-permute-start | bytes 1179656 | tf_op jit(solution)/shard_map/ppermute | solution.py:250
  31.8 16.4 %collective-permute-start.13 = (bf16[2,768,128]{2,1,0:T(8,128)(2,1)S(1)}, bf16[2,768,128]{2,1,0:T(8,128)(2,1)S(1)}, u32[]{:S(2)}, u32[]{:S(2)}) collective-permute-start(bf16[2,768,128]{2,1,0:T(8,128)(2,1)S(1)} %pad_maximum_fusion.1.qg.refs_0_), channel_id=1, source_target_pairs={{0,1},{1,0},{2,3},{3,2},{4,5},{5,4},{6,7},{7,6},{8,9},{9,8},{10,11... | collective-permute-start | bytes 1179656 | tf_op jit(solution)/shard_map/ppermute | solution.py:250
  36.1 8.4 %collective-permute-start.9 = (f32[2,768]{1,0:T(2,128)S(1)}, f32[2,768]{1,0:T(2,128)S(1)}, u32[]{:S(2)}, u32[]{:S(2)}) collective-permute-start(f32[2,768]{1,0:T(2,128)S(1)} %get-tuple-element.25.rows), channel_id=1, source_target_pairs={{0,1},{1,0},{2,3},{3,2},{4,5},{5,4},{6,7},{7,6},{8,9},{9,8},{10,11... | collective-permute-start | bytes 18440 | tf_op jit(solution)/shard_map/ppermute | solution.py:250
  36.2 8.3 %collective-permute-start.10 = (f32[2,768]{1,0:T(2,128)S(1)}, f32[2,768]{1,0:T(2,128)S(1)}, u32[]{:S(2)}, u32[]{:S(2)}) collective-permute-start(f32[2,768]{1,0:T(2,128)S(1)} %get-tuple-element.25.rows), channel_id=1, source_target_pairs={{1,2},{2,1},{5,6},{6,5},{9,10},{10,9},{13,14},{14,13},{17,18},{18,... | collective-permute-start | bytes 18440 | tf_op jit(solution)/shard_map/ppermute | solution.py:255
  44.5 8.4 %collective-permute-start.11 = (f32[3,2,768]{2,1,0:T(2,128)S(1)}, f32[3,2,768]{2,1,0:T(2,128)S(1)}, u32[]{:S(2)}, u32[]{:S(2)}) collective-permute-start(f32[3,2,768]{2,1,0:T(2,128)S(1)} %pad_maximum_fusion.4.rows), channel_id=1, source_target_pairs={{0,4},{1,5},{2,6},{3,7},{4,0},{5,1},{6,2},{7,3},{8,12},{9,13},{10,... | collective-permute-start | bytes 55304 | tf_op jit(solution)/shard_map/ppermute | solution.py:276
  44.6 8.3 %collective-permute-start.12 = (f32[3,2,768]{2,1,0:T(2,128)S(1)}, f32[3,2,768]{2,1,0:T(2,128)S(1)}, u32[]{:S(2)}, u32[]{:S(2)}) collective-permute-start(f32[3,2,768]{2,1,0:T(2,128)S(1)} %pad_maximum_fusion.4.rows), channel_id=1, source_target_pairs={{4,8},{5,9},{6,10},{7,11},{8,4},{9,5},{10,6},{11,7},{20,24},{21,25... | collective-permute-start | bytes 55304 | tf_op jit(solution)/shard_map/ppermute | solution.py:276
  52.3 6.0 %collective-permute-start.16 = (bf16[4,768,128]{2,1,0:T(8,128)(2,1)S(1)}, bf16[4,768,128]{2,1,0:T(8,128)(2,1)S(1)}, u32[]{:S(2)}, u32[]{:S(2)}) collective-permute-start(bf16[4,768,128]{2,1,0:T(8,128)(2,1)S(1)} %collective-permute-done.14.refs_1_), channel_id=1, source_target_pairs={{0,1},{1,0},{2,3},{3,2},{4,5},{5,4},{6,7},{7,6},{8,9},{9,8},{10,11... | collective-permute-start | bytes 2359304 | tf_op jit(solution)/shard_map/ppermute | solution.py:250
  52.4 5.9 %collective-permute-start.17 = (bf16[4,768,128]{2,1,0:T(8,128)(2,1)S(1)}, bf16[4,768,128]{2,1,0:T(8,128)(2,1)S(1)}, u32[]{:S(2)}, u32[]{:S(2)}) collective-permute-start(bf16[4,768,128]{2,1,0:T(8,128)(2,1)S(1)} %collective-permute-done.15.refs_2_), channel_id=1, source_target_pairs={{0,1},{1,0},{2,3},{3,2},{4,5},{5,4},{6,7},{7,6},{8,9},{9,8},{10,11... | collective-permute-start | bytes 2359304 | tf_op jit(solution)/shard_map/ppermute | solution.py:250
